TPU v7x, 32 devices: a whole 2x2x4 slice. The times are simulated.
32 devices in a mesh: src: 4 (over z), rcv: 8 (over y, x, core).
Axes of the slice: x: 2, y: 2, z: 4, core: 2. Of those that a mesh axis runs over, the one named last changes fastest.
Arguments:
- records: bfloat16 [512, 512, 512], P('src', 'rcv'), may hold values from -6 to 6
- surface_operator: float32 [256, 2], replicated, may hold values from -0.7 to 0.7
Outputs:
- multiples: bfloat16 [512, 512, 512], P('src', 'rcv')
All inputs are finite; a program needn't handle non-finite values.
Results may differ from a plain program's by a relative error of at most 0.011.
Values may be sent and summed in bfloat16 or wider, within the bound.
No kernel may reach another device: no remote copies, remote signals or barrier semaphores. Data moves between devices by JAX's collectives and lax.ppermute only.
A program may use at most 128 MiB of HBM per device.

v0:
```python
import math

import jax
import jax.numpy as jnp
from jax import lax
from jax.sharding import PartitionSpec as P


def dft_tables(freqs, samples):
    freq_index = lax.broadcasted_iota(jnp.int32, (freqs, samples), 0)
    time_index = lax.broadcasted_iota(jnp.int32, (freqs, samples), 1)
    phase = (freq_index * time_index % samples).astype(jnp.float32)
    angle = phase * (2.0 * math.pi / samples)
    norming = 1.0 / math.sqrt(samples)
    cosine = jnp.cos(angle) * norming
    sine = jnp.sin(angle) * norming
    weights = jnp.where(freq_index == 0, 1.0, 2.0).astype(jnp.float32)
    forward = jnp.stack([cosine, -sine], axis=1).reshape(2 * freqs, samples)
    inverse = jnp.stack([weights * cosine, -weights * sine], axis=1).reshape(2 * freqs, samples)
    return (forward.astype(jnp.bfloat16), inverse.astype(jnp.bfloat16))


def batch_product(left, right):

    def mult(first_op, second_op):
        return jnp.einsum("nij,njk->nik", first_op, second_op, preferred_element_type=jnp.float32)

    real_part = mult(left[:, 0], right[:, 0]) - mult(left[:, 1], right[:, 1])
    imag_part = mult(left[:, 0], right[:, 1]) + mult(left[:, 1], right[:, 0])
    return (real_part, imag_part)


def predict_block(blocks, coeff):
    order = blocks.shape[2]
    recip = (
        0.5 * (blocks.astype(jnp.float32) + jnp.swapaxes(blocks, 2, 3).astype(jnp.float32))
    ).astype(jnp.bfloat16)
    factor = coeff / math.sqrt(order)
    real_k = factor[:, 0][:, None, None]
    imag_k = factor[:, 1][:, None, None]

    def scaled(product):
        return jnp.stack(
            [real_k * product[0] - imag_k * product[1], real_k * product[1] + imag_k * product[0]],
            axis=1,
        )

    first = scaled(batch_product(recip, recip)).astype(jnp.bfloat16)
    second = scaled(batch_product(recip, first)).astype(jnp.bfloat16)
    third = scaled(batch_product(recip, second))
    return (first.astype(jnp.float32) + second.astype(jnp.float32) + third).astype(jnp.bfloat16)


def local(records, surface_operator):
    src_tiles, rcv_tiles, samples = records.shape
    freqs = surface_operator.shape[0]
    n_src = lax.axis_size("src")
    n_rcv = lax.axis_size("rcv")
    per_group = freqs // (n_src * n_rcv)
    columns = src_tiles * rcv_tiles
    whole_src = n_src * src_tiles
    whole_rcv = n_rcv * rcv_tiles
    forward, inverse = dft_tables(freqs, samples)
    flat_traces = records.reshape(columns, samples)
    spectrum = jnp.einsum(
        "kt,nt->kn", forward, flat_traces, preferred_element_type=jnp.float32
    ).astype(jnp.bfloat16)
    group_index = lax.axis_index("src") * n_rcv + lax.axis_index("rcv")
    coeff = lax.dynamic_slice_in_dim(surface_operator, group_index * per_group, per_group, 0)
    moved = lax.all_to_all(
        spectrum.reshape(freqs, 2, 1, columns),
        ("src", "rcv"),
        split_axis=0,
        concat_axis=2,
        tiled=True,
    )
    blocks = moved.reshape(per_group, 2, n_src, n_rcv, src_tiles, rcv_tiles)
    blocks = blocks.transpose(0, 1, 2, 4, 3, 5).reshape(per_group, 2, whole_src, whole_rcv)
    predicted = predict_block(blocks, coeff)
    outgoing = predicted.reshape(per_group, 2, n_src, src_tiles, n_rcv, rcv_tiles).transpose(
        0, 1, 2, 4, 3, 5
    )
    returned = lax.all_to_all(
        outgoing.reshape(1, per_group, 2, n_src * n_rcv, columns),
        ("src", "rcv"),
        split_axis=3,
        concat_axis=0,
        tiled=True,
    )
    returned = returned.reshape(2 * freqs, columns)
    result = jnp.einsum("kn,kt->nt", returned, inverse, preferred_element_type=jnp.float32)
    return result.astype(jnp.bfloat16).reshape(src_tiles, rcv_tiles, samples)


def solution(mesh):
    placed = (P("src", "rcv", None), P())
    return jax.shard_map(
        local, mesh=mesh, in_specs=placed, out_specs=P("src", "rcv", None), check_vma=False
    )
```

profile of v0, /device:TPU:10, one launch (start us, length us, event | category | flops | bytes accessed | tf_op | source)
XLA Modules:
  0.0 837.8 jit_solution(7434071799866372803)
XLA Ops:
  3.0 10.2 %convolution_convert_fusion.1 = bf16[512,8192]{1,0:T(8,128)(2,1)} fusion(bf16[512,512]{1,0:T(8,128)(2,1)S(1)} %convert_element_type.95, bf16[8192,512]{1,0:T(8,128)(2,1)} %bitcast.88), kind=kOutput, calls=%fused_computation.7 | convolution fusion | flops 4299161600 | bytes 17301504 | tf_op jit(solution)/shard_map/kt,nt->kn/dot_general | solution.py:65
  13.2 14.1 %reshape.184 = bf16[256,2,1,8192]{3,1,0,2:T(2,128)(2,1)} reshape(bf16[512,8192]{1,0:T(8,128)(2,1)} %convolution_convert_fusion.1) | data formatting | bytes 16777216 | tf_op jit(solution)/shard_map/reshape | solution.py:71
  34.2 180.3 %all-to-all-done = bf16[256,2,1,8192]{3,1,2,0:T(2,128)(2,1)} async-done(((bf16[256,2,1,8192]{3,1,2,0:T(2,128)(2,1)}), bf16[256,2,1,8192]{3,1,2,0:T(2,128)(2,1)}, u32[]{:S(2)}, u32[]{:S(2)}) %all-to-all-start) | async-done | bytes 8388640 | tf_op jit(solution)/shard_map/all_to_all | solution.py:70
  214.5 17.0 %convert_bitcast_fusion = f32[8,2,32,1,8192]{4,0,2,1,3:T(8,128)} fusion(bf16[256,2,1,8192]{3,1,2,0:T(2,128)(2,1)} %all-to-all-done), kind=kLoop, calls=%fused_computation.2 | loop fusion | flops 4194304 | bytes 25165824 | tf_op jit(solution)/shard_map/convert_element_type | solution.py:36
  231.4 17.7 %copy.55 = f32[8,2,32,1,8192]{4,2,1,0,3:T(8,128)} copy(f32[8,2,32,1,8192]{4,0,2,1,3:T(8,128)} %convert_bitcast_fusion) | data formatting | bytes 33554432 | tf_op jit(solution)/shard_map/convert_element_type | solution.py:36
  249.1 27.2 %reshape.190 = f32[8,2,4,8,128,64]{5,4,3,2,1,0:T(8,128)} reshape(f32[8,2,32,1,8192]{4,2,1,0,3:T(8,128)} %copy.55) | data formatting | bytes 33554432 | tf_op jit(solution)/shard_map/convert_element_type | solution.py:36
  276.2 27.8 %copy.56 = f32[8,2,4,128,8,64]{3,2,5,4,0,1:T(4,128)} copy(f32[8,2,4,128,8,64]{5,3,4,2,1,0:T(8,128)} %bitcast.86) | data formatting | bytes 33554432 | tf_op jit(solution)/shard_map/convert_element_type | solution.py:36
  304.1 19.9 %reshape.188 = f32[8,2,512,512]{2,3,0,1:T(8,128)} reshape(f32[8,2,4,128,8,64]{3,2,5,4,0,1:T(4,128)} %copy.56) | data formatting | bytes 33554432 | tf_op jit(solution)/shard_map/convert_element_type | solution.py:36
  324.0 17.3 %copy.57 = f32[8,2,512,512]{3,2,0,1:T(8,128)} copy(f32[8,2,512,512]{2,3,0,1:T(8,128)} %reshape.188) | data formatting | bytes 33554432 | tf_op jit(solution)/shard_map/convert_element_type | solution.py:36
  341.3 12.0 %fusion.2 = bf16[8,2,512,512]{3,2,0,1:T(8,128)(2,1)S(1)} fusion(f32[8,2,512,512]{3,2,0,1:T(8,128)} %copy.57, f32[8,2,512,512]{2,3,0,1:T(8,128)} %reshape.188), kind=kLoop, calls=%fused_computation.5 | loop fusion | flops 12582912 | bytes 41943040 | tf_op jit(solution)/shard_map/convert_element_type | solution.py:37
  370.3 16.1 %subtract_convert_fusion.1 = (bf16[8,512,512]{2,1,0:T(8,128)(2,1)}, bf16[8,512,512]{2,1,0:T(8,128)(2,1)}) fusion(f32[8]{0:T(128)S(1)} %get-tuple-element.12, f32[8]{0:T(128)S(1)} %get-tuple-element.11, f32[8,512,512]{2,1,0:T(8,128)} %fusion.8, f32[8,512,512]{2,1,0:T(8,128)} %fusion.10, f32[8,512,512]{2,1,0:T(8,128)} %fusion.15, ...), kind=kOutput, calls=%fused_computation.13 | convolution fusion | flops 2168455168 | bytes 41943104 | tf_op jit(solution)/shard_map/nij,njk->nik/dot_general | solution.py:26
  386.4 9.2 %fusion.7 = f32[8,512,512]{2,1,0:T(8,128)} fusion(bf16[8,512,512]{2,1,0:T(8,128)(2,1)} %get-tuple-element.9, bf16[8,2,512,512]{3,2,0,1:T(8,128)(2,1)} %copy-done), kind=kOutput, calls=%fused_computation.20 | convolution fusion | flops 2147483648 | bytes 16777216 | tf_op jit(solution)/shard_map/nij,njk->nik/dot_general | solution.py:26
  406.9 14.3 %subtract_convert_fusion = (bf16[8,512,512]{2,1,0:T(8,128)(2,1)S(1)}, bf16[8,512,512]{2,1,0:T(8,128)(2,1)}) fusion(f32[8]{0:T(128)S(1)} %get-tuple-element.12, f32[8]{0:T(128)S(1)} %get-tuple-element.11, f32[8,512,512]{2,1,0:T(8,128)} %fusion.13, f32[8,512,512]{2,1,0:T(8,128)} %fusion.7, f32[8,512,512]{2,1,0:T(8,128)} %fusion.14, ...), kind=kOutput, calls=%fused_computation.11 | convolution fusion | flops 2168455168 | bytes 41943104 | tf_op jit(solution)/shard_map/nij,njk->nik/dot_general | solution.py:26
  421.2 9.3 %fusion.5 = f32[8,512,512]{2,1,0:T(8,128)} fusion(bf16[8,512,512]{2,1,0:T(8,128)(2,1)S(1)} %get-tuple-element.7, bf16[8,2,512,512]{3,2,0,1:T(8,128)(2,1)} %copy-done), kind=kOutput, calls=%fused_computation.18 | convolution fusion | flops 2147483648 | bytes 16777216 | tf_op jit(solution)/shard_map/nij,njk->nik/dot_general | solution.py:26
  430.5 7.9 fusion.11
  444.9 9.0 %fusion.12 = f32[8,512,512]{2,1,0:T(8,128)} fusion(bf16[8,512,512]{2,1,0:T(8,128)(2,1)} %get-tuple-element.8, bf16[8,2,512,512]{3,2,0,1:T(8,128)(2,1)} %copy-done), kind=kOutput, calls=%fused_computation.25 | convolution fusion | flops 2147483648 | bytes 16777216 | tf_op jit(solution)/shard_map/nij,njk->nik/dot_general | solution.py:26
  473.6 19.6 %multiply_subtract_fusion = (f32[8,512,512]{2,1,0:T(8,128)}, f32[8,512,512]{2,1,0:T(8,128)}) fusion(f32[8]{0:T(128)S(1)} %get-tuple-element.12, f32[8]{0:T(128)S(1)} %get-tuple-element.11, f32[8,512,512]{2,1,0:T(8,128)} %fusion.11, f32[8,512,512]{2,1,0:T(8,128)} %fusion.5, f32[8,512,512]{2,1,0:T(8,128)} %fusion.12, ...), kind=kOutput, calls=%fused_computation.9 | convolution fusion | flops 2164260864 | bytes 50331712 | tf_op jit(solution)/shard_map/nij,njk->nik/dot_general | solution.py:26
  493.2 9.2 %copy.62 = f32[8,512,512]{1,2,0:T(8,128)} copy(f32[8,512,512]{2,1,0:T(8,128)} %get-tuple-element.5) | data formatting | bytes 16777216 | tf_op jit(solution)/shard_map/sub | solution.py:44
  502.4 9.9 %stack.52 = f32[8,1,4,128,8,64]{3,2,5,4,0,1:T(4,128)} reshape(f32[8,512,512]{1,2,0:T(8,128)} %copy.62) | data formatting | bytes 16777216 | tf_op jit(solution)/shard_map/stack | solution.py:43
  512.3 9.1 %copy.63 = f32[8,512,512]{1,2,0:T(8,128)} copy(f32[8,512,512]{2,1,0:T(8,128)} %get-tuple-element.6) | data formatting | bytes 16777216 | tf_op jit(solution)/shard_map/add | solution.py:44
  521.4 9.9 %stack.53 = f32[8,1,4,128,8,64]{3,2,5,4,0,1:T(4,128)} reshape(f32[8,512,512]{1,2,0:T(8,128)} %copy.63) | data formatting | bytes 16777216 | tf_op jit(solution)/shard_map/stack | solution.py:43
  531.3 6.9 stack.49
  538.3 7.0 stack.50
  545.2 6.9 stack.46
  552.1 6.9 stack.47
  559.0 17.8 %fusion.3 = bf16[8,2,4,8,128,64]{4,2,5,3,0,1:T(4,128)(2,1)} fusion(f32[8,1,4,128,8,64]{3,2,5,4,0,1:T(4,128)} %stack.53, f32[8,1,4,128,8,64]{3,2,5,4,0,1:T(4,128)} %stack.52, bf16[8,1,4,128,8,64]{3,2,5,4,0,1:T(4,128)(2,1)} %stack.50, bf16[8,1,4,128,8,64]{3,2,5,4,0,1:T(4,128)(2,1)} %stack.49, bf16[8,1,4,128,8,64]{3,2,5,4,0,1:T(4,128)(2,1)} %stack.47, ...), kind=kLoop, calls=%fused_computation.14 | loop fusion | flops 33554432 | bytes 41943040 | tf_op jit(solution)/shard_map/transpose | solution.py:80
  576.9 20.1 %copy.67 = bf16[8,2,4,8,128,64]{5,4,1,0,3,2:T(8,128)(2,1)} copy(bf16[8,2,4,8,128,64]{4,2,5,3,0,1:T(4,128)(2,1)} %fusion.3) | data formatting | bytes 16777216 | tf_op jit(solution)/shard_map/reshape | solution.py:84
  596.9 27.1 %reshape.193 = bf16[1,8,2,32,8192]{4,2,1,0,3:T(2,128)(2,1)} reshape(bf16[8,2,4,8,128,64]{5,4,1,0,3,2:T(8,128)(2,1)} %copy.67) | data formatting | bytes 16777216 | tf_op jit(solution)/shard_map/reshape | solution.py:84
  624.0 9.6 %all-to-all-start.1 = ((bf16[1,8,2,32,8192]{4,2,1,0,3:T(2,128)(2,1)}), bf16[1,8,2,32,8192]{4,2,1,0,3:T(2,128)(2,1)}, u32[]{:S(2)}, u32[]{:S(2)}) async-start(bf16[1,8,2,32,8192]{4,2,1,0,3:T(2,128)(2,1)} %reshape.193), calls=%async_computation.1 | async-start | bytes 16777216 | tf_op jit(solution)/shard_map/all_to_all | solution.py:83
  636.7 177.3 %all-to-all-done.1 = bf16[1,8,2,32,8192]{4,2,1,0,3:T(2,128)(2,1)} async-done(((bf16[1,8,2,32,8192]{4,2,1,0,3:T(2,128)(2,1)}), bf16[1,8,2,32,8192]{4,2,1,0,3:T(2,128)(2,1)}, u32[]{:S(2)}, u32[]{:S(2)}) %all-to-all-start.1) | async-done | bytes 8388640 | tf_op jit(solution)/shard_map/all_to_all | solution.py:83
  814.0 13.1 %reshape.186 = bf16[512,8192]{1,0:T(8,128)(2,1)} reshape(bf16[32,1,8,2,1,8192]{5,3,2,0,4,1:T(2,128)(2,1)} %bitcast.12) | data formatting | bytes 16777216 | tf_op jit(solution)/shard_map/reshape | solution.py:90
  827.1 10.2 %convolution_convert_fusion = bf16[8192,512]{1,0:T(8,128)(2,1)} fusion(bf16[512,8192]{1,0:T(8,128)(2,1)} %reshape.186, bf16[512,512]{1,0:T(8,128)(2,1)S(1)} %convert_element_type.107), kind=kOutput, calls=%fused_computation.6 | convolution fusion | flops 4299161600 | bytes 17301504 | tf_op jit(solution)/shard_map/kn,kt->nt/dot_general | solution.py:91
  (34 shorter events, 67.4 us)
Async XLA Ops:
  27.3 6.8 copy-start.5
  27.3 187.2 %all-to-all-start = ((bf16[256,2,1,8192]{3,1,2,0:T(2,128)(2,1)}), bf16[256,2,1,8192]{3,1,2,0:T(2,128)(2,1)}, u32[]{:S(2)}, u32[]{:S(2)}) async-start(bf16[256,2,1,8192]{3,1,2,0:T(2,128)(2,1)} %bitcast.87), calls=%async_computation | async-start | bytes 16777216 | tf_op jit(solution)/shard_map/all_to_all | solution.py:70
  353.3 11.3 %copy-start = (bf16[8,2,512,512]{3,2,0,1:T(8,128)(2,1)}, bf16[8,2,512,512]{3,2,0,1:T(8,128)(2,1)S(1)}, u32[]{:S(2)}) copy-start(bf16[8,2,512,512]{3,2,0,1:T(8,128)(2,1)S(1)} %fusion.2) | copy-start | bytes 25165828
  386.4 9.2 %copy-start.1 = (bf16[8,2,512,512]{3,2,0,1:T(8,128)(2,1)S(1)}, bf16[8,2,512,512]{3,2,0,1:T(8,128)(2,1)}, u32[]{:S(2)}) copy-start(bf16[8,2,512,512]{3,2,0,1:T(8,128)(2,1)} %copy-done) | copy-start | bytes 25165828
  386.4 9.2 %copy-start.2 = (bf16[8,512,512]{2,1,0:T(8,128)(2,1)S(1)}, bf16[8,512,512]{2,1,0:T(8,128)(2,1)}, u32[]{:S(2)}) copy-start(bf16[8,512,512]{2,1,0:T(8,128)(2,1)} %get-tuple-element.9) | copy-start | bytes 12582916
  395.6 5.8 copy-start.4
  421.2 9.3 %copy-start.3 = (bf16[8,512,512]{2,1,0:T(8,128)(2,1)}, bf16[8,512,512]{2,1,0:T(8,128)(2,1)S(1)}, u32[]{:S(2)}) copy-start(bf16[8,512,512]{2,1,0:T(8,128)(2,1)S(1)} %get-tuple-element.7) | copy-start | bytes 12582916
  624.0 189.9 %all-to-all-start.1 = ((bf16[1,8,2,32,8192]{4,2,1,0,3:T(2,128)(2,1)}), bf16[1,8,2,32,8192]{4,2,1,0,3:T(2,128)(2,1)}, u32[]{:S(2)}, u32[]{:S(2)}) async-start(bf16[1,8,2,32,8192]{4,2,1,0,3:T(2,128)(2,1)} %reshape.193), calls=%async_computation.1 | async-start | bytes 16777216 | tf_op jit(solution)/shard_map/all_to_all | solution.py:83
where the time goes:
time: 854 us; the launch traced here: 838 us
  waiting for transfers between devices  358 us (42%)
  local copies, waits for them, and re-layouts  278 us (33%)
  matrix products  134 us (16%)
  other arithmetic  51.4 us (6%)
  starting transfers between devices  16.4 us (2%)
    all_to_all x1, waiting for transfers between devices, local(): lax.all_to_all(spectrum.reshape(freqs, 2, 1, columns), ('src', 'rcv'), sp...  180 us
    all_to_all x1, waiting for transfers between devices, local(): lax.all_to_all(outgoing.reshape(1, per_group, 2, n_src * n_rcv, columns),...  177 us
    dot_general x12, matrix products, mult(): jnp.einsum('nij,njk->nik', first_op, second_op, preferred_element_type=jn...  114 us
    convert_element_type x5, local copies, waits for them, and re-layouts, predict_block(): blocks.astype(jnp.float32) + jnp.swapaxes(blocks, 2, 3).astype(jnp.float32)  110 us
    another operation x6, local copies, waits for them, and re-layouts, scaled(): jnp.stack([real_k * product[0] - imag_k * product[1], real_k * product[1]...  47.5 us
    reshape x2, local copies, waits for them, and re-layouts, local(): outgoing.reshape(1, per_group, 2, n_src * n_rcv, columns)  47.2 us
    another operation x4, local copies, waits for them, and re-layouts  26.1 us
    transpose x1, other arithmetic, local(): predicted.reshape(per_group, 2, n_src, src_tiles, n_rcv, rcv_tiles)  17.8 us
  transfers between devices with their start and end apart: 2, of which 2 were waited for; matrix products, arithmetic and copies ran while one was open for 0% of the time, Pallas kernels for 0%

commit v1 on v0

--- a/solution.py
+++ b/solution.py
@@ -4,6 +4,10 @@
 import jax.numpy as jnp
 from jax import lax
 from jax.sharding import PartitionSpec as P
+from jax.experimental import pallas as pl
+from jax.experimental.pallas import tpu as pltpu
+import ml_dtypes
+import numpy as np
 
 
 def dft_tables(freqs, samples):
@@ -51,7 +55,7 @@
     return (first.astype(jnp.float32) + second.astype(jnp.float32) + third).astype(jnp.bfloat16)
 
 
-def local(records, surface_operator):
+def local_general(records, surface_operator):
     src_tiles, rcv_tiles, samples = records.shape
     freqs = surface_operator.shape[0]
     n_src = lax.axis_size("src")
@@ -92,8 +96,235 @@
     return result.astype(jnp.bfloat16).reshape(src_tiles, rcv_tiles, samples)
 
 
+NT = (((1,), (1,)), ((), ()))
+TN = (((0,), (0,)), ((), ()))
+VMEM_LIMIT = 56 * 2**20
+ROWS = 16
+
+
+def host_tables(freqs, samples):
+    f = np.arange(freqs)[:, None]
+    t = np.arange(samples)[None, :]
+    angle = (f * t % samples) * (2.0 * math.pi / samples)
+    norming = 1.0 / math.sqrt(samples)
+    cosine = np.cos(angle) * norming
+    sine = np.sin(angle) * norming
+    weights = np.where(f == 0, 1.0, 2.0)
+    forward = np.stack([cosine, -sine], axis=1)
+    inverse = np.stack([weights * cosine, -weights * sine], axis=1)
+    to = lambda x: x.astype(np.float32).astype(ml_dtypes.bfloat16).reshape(2 * freqs, samples)
+    return to(forward), to(inverse)
+
+
+def forward_dft(records, table):
+    sources, receivers, samples = records.shape
+    half = sources // 2
+    width = 2 * receivers
+    rows = table.shape[0]
+
+    def kernel(table_ref, records_ref, out_ref, turned):
+        for p in range(0, ROWS, 2):
+            traces = jnp.concatenate(
+                [records_ref[s, p + d] for d in range(2) for s in range(2)], axis=0
+            )
+            found = lax.dot_general(
+                table_ref[...], traces, NT, preferred_element_type=jnp.float32
+            )
+            turned[p] = found[:, :width]
+            turned[p + 1] = found[:, width:]
+        out_ref[...] = jnp.swapaxes(turned[...], 0, 1).astype(out_ref.dtype)
+
+    return pl.pallas_call(
+        kernel,
+        grid=(half // ROWS,),
+        in_specs=[
+            pl.BlockSpec((rows, samples), lambda i: (0, 0)),
+            pl.BlockSpec((2, ROWS, receivers, samples), lambda i: (0, i, 0, 0)),
+        ],
+        out_specs=pl.BlockSpec((rows, ROWS, width), lambda i: (0, i, 0)),
+        out_shape=jax.ShapeDtypeStruct((rows, half, width), jnp.bfloat16),
+        scratch_shapes=[pltpu.VMEM((ROWS, rows, width), jnp.float32)],
+        compiler_params=pltpu.CompilerParams(vmem_limit_bytes=VMEM_LIMIT),
+        cost_estimate=pl.CostEstimate(
+            flops=2 * rows * records.size,
+            bytes_accessed=2 * (records.size + rows * half * width),
+            transcendentals=0,
+        ),
+    )(table, records.reshape(2, half, receivers, samples))
+
+
+def inverse_dft(spectra, table):
+    rows, half, width = spectra.shape
+    receivers = width // 2
+    samples = table.shape[1]
+
+    def kernel(table_ref, spectra_ref, out_ref, turned):
+        turned[...] = jnp.swapaxes(spectra_ref[...].astype(jnp.float32), 0, 1)
+        for p in range(ROWS):
+            traces = lax.dot_general(
+                turned[p].astype(jnp.bfloat16),
+                table_ref[...],
+                TN,
+                preferred_element_type=jnp.float32,
+            ).astype(out_ref.dtype)
+            out_ref[0, p] = traces[:receivers]
+            out_ref[1, p] = traces[receivers:]
+
+    return pl.pallas_call(
+        kernel,
+        grid=(half // ROWS,),
+        in_specs=[
+            pl.BlockSpec((rows, samples), lambda i: (0, 0)),
+            pl.BlockSpec((rows, ROWS, width), lambda i: (0, i, 0)),
+        ],
+        out_specs=pl.BlockSpec((2, ROWS, receivers, samples), lambda i: (0, i, 0, 0)),
+        out_shape=jax.ShapeDtypeStruct((2, half, receivers, samples), jnp.bfloat16),
+        scratch_shapes=[pltpu.VMEM((ROWS, rows, width), jnp.float32)],
+        compiler_params=pltpu.CompilerParams(vmem_limit_bytes=VMEM_LIMIT),
+        cost_estimate=pl.CostEstimate(
+            flops=2 * rows * half * width * samples,
+            bytes_accessed=2 * (half * width * samples + rows * half * width),
+            transcendentals=0,
+        ),
+    )(table, spectra).reshape(2 * half, receivers, samples)
+
+
+def swap_quarters(block):
+    size = block.shape[0]
+    half = size // 2
+    rolled = pltpu.roll(block, half, 1)
+    left = lax.broadcasted_iota(jnp.int32, (half, size), 1) < half
+    return jnp.concatenate(
+        [
+            jnp.where(left, block[:half], rolled[half:]),
+            jnp.where(left, rolled[:half], block[half:]),
+        ],
+        axis=0,
+    )
+
+
+def dot(left, right):
+    return jnp.dot(left, right, preferred_element_type=jnp.float32)
+
+
+def series(coeff_ref, index, recip, first, out_block):
+    order = recip.shape[-1]
+    real_k = coeff_ref[index, 0]
+    imag_k = coeff_ref[index, 1]
+    panel = min(256, order)
+    wide = jnp.float32
+
+    def scaled(real, imag):
+        return real_k * real - imag_k * imag, real_k * imag + imag_k * real
+
+    for start in range(0, order, panel):
+        rows = pl.ds(start, panel)
+        a, b = recip[0, rows, :], recip[1, rows, :]
+        real, imag = scaled(
+            dot(a, recip[0]) - dot(b, recip[1]), dot(a, recip[1]) + dot(b, recip[0])
+        )
+        first[0, rows, :] = real.astype(jnp.bfloat16)
+        first[1, rows, :] = imag.astype(jnp.bfloat16)
+    for start in range(0, order, panel):
+        rows = pl.ds(start, panel)
+        own = [first[c, rows, :].astype(wide) for c in range(2)]
+        a, b = [(recip[c, rows, :].astype(wide) + own[c]).astype(jnp.bfloat16) for c in range(2)]
+        real, imag = scaled(
+            dot(a, first[0]) - dot(b, first[1]), dot(a, first[1]) + dot(b, first[0])
+        )
+        out_block(start, panel, own[0] + real, own[1] + imag)
+
+
+def predict(moved, coeff):
+    devices, freqs, _, half, tile = moved.shape
+    order = math.isqrt(devices * half * tile)
+    blocks = order // tile
+    pieces = 2 * blocks
+
+    def kernel(coeff_ref, moved_ref, out_ref, recip, first):
+        for c in range(2):
+            for a in range(blocks):
+                for b in range(a + 1):
+
+                    def stacked(i, j):
+                        at = i * pieces + 2 * j
+                        return jnp.concatenate(
+                            [moved_ref[at, 0, c], moved_ref[at + 1, 0, c]], axis=0
+                        ).astype(jnp.float32)
+
+                    mean = 0.5 * (stacked(a, b) + stacked(b, a).T)
+                    block = swap_quarters(mean)
+                    recip[c, a * tile:(a + 1) * tile, b * tile:(b + 1) * tile] = block.astype(
+                        jnp.bfloat16
+                    )
+                    if a != b:
+                        recip[c, b * tile:(b + 1) * tile, a * tile:(a + 1) * tile] = (
+                            block.T.astype(jnp.bfloat16)
+                        )
+
+        def out_block(start, panel, real, imag):
+            for c, value in enumerate((real, imag)):
+                for row in range(0, panel, tile):
+                    a = (start + row) // tile
+                    for b in range(blocks):
+                        block = swap_quarters(
+                            value[row:row + tile, b * tile:(b + 1) * tile]
+                        ).astype(jnp.bfloat16)
+                        at = a * pieces + 2 * b
+                        out_ref[at, 0, c] = block[:half]
+                        out_ref[at + 1, 0, c] = block[half:]
+
+        series(coeff_ref, pl.program_id(0), recip, first, out_block)
+
+    spec = pl.BlockSpec((devices, 1, 2, half, tile), lambda i: (0, i, 0, 0, 0))
+    return pl.pallas_call(
+        kernel,
+        grid=(freqs,),
+        in_specs=[pl.BlockSpec(memory_space=pltpu.SMEM), spec],
+        out_specs=spec,
+        out_shape=jax.ShapeDtypeStruct(moved.shape, jnp.bfloat16),
+        scratch_shapes=[
+            pltpu.VMEM((2, order, order), jnp.bfloat16),
+            pltpu.VMEM((2, order, order), jnp.bfloat16),
+        ],
+        compiler_params=pltpu.CompilerParams(vmem_limit_bytes=VMEM_LIMIT),
+        cost_estimate=pl.CostEstimate(
+            flops=16 * freqs * order**3, bytes_accessed=4 * moved.size, transcendentals=0
+        ),
+    )(coeff / math.sqrt(order), moved)
+
+
+def local_tiles(records, surface_operator):
+    src_tiles, rcv_tiles, samples = records.shape
+    freqs = surface_operator.shape[0]
+    axes = ("src", "rcv")
+    n_src = lax.axis_size("src")
+    n_rcv = lax.axis_size("rcv")
+    devices = n_src * n_rcv
+    per_group = freqs // devices
+    half = src_tiles // 2
+    forward, inverse = host_tables(freqs, samples)
+    group_index = lax.axis_index("src") * n_rcv + lax.axis_index("rcv")
+    coeff = lax.dynamic_slice_in_dim(surface_operator, group_index * per_group, per_group, 0)
+    spectrum = forward_dft(records, jnp.asarray(forward))
+    spectrum = spectrum.reshape(devices, per_group, 2, half, src_tiles)
+    moved = lax.all_to_all(spectrum, axes, split_axis=0, concat_axis=0, tiled=True)
+    predicted = predict(moved, coeff)
+    returned = lax.all_to_all(predicted, axes, split_axis=0, concat_axis=0, tiled=True)
+    return inverse_dft(returned.reshape(2 * freqs, half, src_tiles), jnp.asarray(inverse))
+
+
 def solution(mesh):
     placed = (P("src", "rcv", None), P())
+    n_src, n_rcv = mesh.shape["src"], mesh.shape["rcv"]
+
+    def local(records, surface_operator):
+        src_tiles, rcv_tiles, _ = records.shape
+        whole_lanes = src_tiles % 128 == 0 and rcv_tiles % 32 == 0
+        if n_rcv == 2 * n_src and src_tiles == 2 * rcv_tiles and whole_lanes:
+            return local_tiles(records, surface_operator)
+        return local_general(records, surface_operator)
+
     return jax.shard_map(
         local, mesh=mesh, in_specs=placed, out_specs=P("src", "rcv", None), check_vma=False
     )

time: 854 us -> 434 us (0.51); the launches traced: 838 us -> 431 us
  local copies, waits for them, and re-layouts: 278 us -> 0.16 us
  blocking collectives: 0 us -> 191 us
  waiting for transfers between devices: 358 us -> 180 us
  matrix products: 134 us -> 0 us
  Pallas kernels: 0 us -> 53.1 us
  other arithmetic: 51.4 us -> 0.6 us
  starting transfers between devices: 16.4 us -> 6.06 us
    all_to_all x0 -> x1, blocking collectives: none -> 191 us  [local_tiles(): lax.all_to_all(predicted, axes, split_axis=0, concat_axis=0, tiled=True)]
    all_to_all x2 -> x1, waiting for transfers between devices: 358 us -> 180 us  [local_tiles(): lax.all_to_all(spectrum, axes, split_axis=0, concat_axis=0, tiled=True)]
    dot_general x14 -> x0, matrix products: 134 us -> none  [the longest x12 114 us: mult(): jnp.einsum('nij,njk->nik', first_op, second_op, preferred_element_type=jn...]
    convert_element_type x7 -> x0, local copies, waits for them, and re-layouts: 110 us -> none  [the longest x5 110 us: predict_block(): blocks.astype(jnp.float32) + jnp.swapaxes(blocks, 2, 3).astype(jnp.float32)]
    another operation x12 -> x0, local copies, waits for them, and re-layouts: 74.7 us -> none  [the longest x6 47.5 us: scaled(): jnp.stack([real_k * product[0] - imag_k * product[1], real_k * product[1]...]
    reshape x4 -> x0, local copies, waits for them, and re-layouts: 74.4 us -> none  [the longest x2 47.2 us: local(): outgoing.reshape(1, per_group, 2, n_src * n_rcv, columns)]
    pallas_call x0 -> x3, Pallas kernels: none -> 53.1 us  [the longest x1 30.9 us: predict(): pl.pallas_call(kernel, grid=(freqs,), in_specs=[pl.BlockSpec(memory_space...]
    convert_element_type x2 -> x0, other arithmetic: 29 us -> none  [the longest x1 17 us: predict_block(): blocks.astype(jnp.float32) + jnp.swapaxes(blocks, 2, 3).astype(jnp.float32)]
  transfers between devices with their start and end apart: 2 -> 1, of which waited for: 2 -> 1; matrix products, arithmetic and copies ran while one was open for 0% -> 0% of each run, Pallas kernels for 0% -> 0%
where the time goes in v1:
time: 434 us; the launch traced here: 431 us
  blocking collectives  191 us (44%)
  waiting for transfers between devices  180 us (41%)
  Pallas kernels  53.1 us (12%)
  starting transfers between devices  6.06 us (1%)
    all_to_all x1, blocking collectives, local_tiles(): lax.all_to_all(predicted, axes, split_axis=0, concat_axis=0, tiled=True)  191 us
    all_to_all x1, waiting for transfers between devices, local_tiles(): lax.all_to_all(spectrum, axes, split_axis=0, concat_axis=0, tiled=True)  180 us
    pallas_call x1, Pallas kernels, predict(): pl.pallas_call(kernel, grid=(freqs,), in_specs=[pl.BlockSpec(memory_space...  30.9 us
    pallas_call x1, Pallas kernels, inverse_dft(): pl.pallas_call(kernel, grid=(half // ROWS,), in_specs=[pl.BlockSpec((rows...  11.3 us
    pallas_call x1, Pallas kernels, forward_dft(): pl.pallas_call(kernel, grid=(half // ROWS,), in_specs=[pl.BlockSpec((rows...  10.9 us
  transfers between devices with their start and end apart: 1, of which 1 were waited for; matrix products, arithmetic and copies ran while one was open for 0% of the time, Pallas kernels for 0%

profile of v1, /device:TPU:10, one launch (start us, length us, event | category | flops | bytes accessed | tf_op | source)
XLA Modules:
  0.0 431.0 jit_solution(8572402523360825104)
XLA Ops:
  0.0 0.0 copy-start
  0.0 10.9 %shard_map.46 = bf16[512,64,128]{2,1,0:T(8,128)(2,1)} custom-call(bf16[512,512]{1,0:T(8,128)(2,1)} %constant.21.clone.table_ref, bf16[2,64,64,512]{3,2,1,0:T(8,128)(2,1)} %bitcast.6), custom_call_target="tpu_custom_call" | custom-call | flops 4294967296 | bytes 16777216 | tf_op jit(solution)/shard_map/pallas_call | solution.py:137
  10.9 6.1 %all-to-all-start = ((bf16[32,8,2,64,128]{4,3,2,1,0:T(8,128)(2,1)}), bf16[32,8,2,64,128]{4,3,2,1,0:T(8,128)(2,1)}, u32[]{:S(2)}, u32[]{:S(2)}) async-start(bf16[32,8,2,64,128]{4,3,2,1,0:T(8,128)(2,1)} %bitcast.4), calls=%async_computation | async-start | bytes 16777216 | tf_op jit(solution)/shard_map/all_to_all | solution.py:311
  16.9 0.0 copy-done
  17.0 0.1 constant_dynamic-slice_fusion
  17.0 0.1 copy.6
  17.1 0.6 broadcast_multiply_fusion.coeff_ref
  17.7 179.8 %all-to-all-done.moved_ref = bf16[32,8,2,64,128]{4,3,2,1,0:T(8,128)(2,1)} async-done(((bf16[32,8,2,64,128]{4,3,2,1,0:T(8,128)(2,1)}), bf16[32,8,2,64,128]{4,3,2,1,0:T(8,128)(2,1)}, u32[]{:S(2)}, u32[]{:S(2)}) %all-to-all-start) | async-done | bytes 8388640 | tf_op jit(solution)/shard_map/all_to_all | solution.py:311
  197.5 30.9 %shard_map.47 = bf16[32,8,2,64,128]{4,3,2,1,0:T(8,128)(2,1)} custom-call(f32[8,2]{1,0:T(8,128)} %broadcast_multiply_fusion.coeff_ref, bf16[32,8,2,64,128]{4,3,2,1,0:T(8,128)(2,1)} %all-to-all-done.moved_ref), custom_call_target="tpu_custom_call" | custom-call | flops 17179869184 | bytes 16777216 | tf_op jit(solution)/shard_map/pallas_call | solution.py:280
  228.4 191.2 %all_to_all.10 = bf16[32,8,2,64,128]{4,3,2,1,0:T(8,128)(2,1)} all-to-all(bf16[32,8,2,64,128]{4,3,2,1,0:T(8,128)(2,1)} %shard_map.47), channel_id=1, replica_groups=mesh['src'=4,'rcv'=8] {'src','rcv'}, dimensions={0} | all-to-all | bytes 16777216 | tf_op jit(solution)/shard_map/all_to_all | solution.py:313
  419.6 11.3 %shard_map.48 = bf16[2,64,64,512]{3,2,1,0:T(8,128)(2,1)} custom-call(bf16[512,512]{1,0:T(8,128)(2,1)} %constant.22.clone.table_ref, bf16[512,64,128]{2,1,0:T(8,128)(2,1)} %bitcast.5), custom_call_target="tpu_custom_call" | custom-call | flops 4294967296 | bytes 16777216 | tf_op jit(solution)/shard_map/pallas_call | solution.py:173
Async XLA Ops:
  0.0 17.0 %copy-start = (f32[256,2]{0,1:T(2,128)S(1)}, f32[256,2]{0,1:T(2,128)}, u32[]{:S(2)}) copy-start(f32[256,2]{0,1:T(2,128)} %param.5) | copy-start | bytes 6148
  10.9 186.7 %all-to-all-start = ((bf16[32,8,2,64,128]{4,3,2,1,0:T(8,128)(2,1)}), bf16[32,8,2,64,128]{4,3,2,1,0:T(8,128)(2,1)}, u32[]{:S(2)}, u32[]{:S(2)}) async-start(bf16[32,8,2,64,128]{4,3,2,1,0:T(8,128)(2,1)} %bitcast.4), calls=%async_computation | async-start | bytes 16777216 | tf_op jit(solution)/shard_map/all_to_all | solution.py:311

commit v2 on v0

--- a/solution.py
+++ b/solution.py
@@ -4,6 +4,10 @@
 import jax.numpy as jnp
 from jax import lax
 from jax.sharding import PartitionSpec as P
+from jax.experimental import pallas as pl
+from jax.experimental.pallas import tpu as pltpu
+import ml_dtypes
+import numpy as np
 
 
 def dft_tables(freqs, samples):
@@ -51,7 +55,7 @@
     return (first.astype(jnp.float32) + second.astype(jnp.float32) + third).astype(jnp.bfloat16)
 
 
-def local(records, surface_operator):
+def local_general(records, surface_operator):
     src_tiles, rcv_tiles, samples = records.shape
     freqs = surface_operator.shape[0]
     n_src = lax.axis_size("src")
@@ -92,8 +96,568 @@
     return result.astype(jnp.bfloat16).reshape(src_tiles, rcv_tiles, samples)
 
 
+NT = (((1,), (1,)), ((), ()))
+TN = (((0,), (0,)), ((), ()))
+VMEM_LIMIT = 56 * 2**20
+ROWS = 16
+WIDE = jnp.float32
+NARROW = jnp.bfloat16
+IN_VMEM = pl.BlockSpec(memory_space=pltpu.VMEM)
+IN_SMEM = pl.BlockSpec(memory_space=pltpu.SMEM)
+UNREAD = pl.BlockSpec(memory_space=pl.ANY)
+
+
+def host_tables(freqs, samples):
+    f = np.arange(freqs)[:, None]
+    t = np.arange(samples)[None, :]
+    angle = (f * t % samples) * (2.0 * math.pi / samples)
+    norming = 1.0 / math.sqrt(samples)
+    cosine = np.cos(angle) * norming
+    sine = np.sin(angle) * norming
+    weights = np.where(f == 0, 1.0, 2.0)
+    forward = np.stack([cosine, -sine], axis=1)
+    inverse = np.stack([weights * cosine, -weights * sine], axis=1)
+    return [x.astype(np.float32).astype(ml_dtypes.bfloat16) for x in (forward, inverse)]
+
+
+def params():
+    return pltpu.CompilerParams(vmem_limit_bytes=VMEM_LIMIT)
+
+
+def cost(flops, moved):
+    return pl.CostEstimate(flops=0, bytes_accessed=0, transcendentals=0)
+
+
+def shaped(*shape):
+    return jax.ShapeDtypeStruct(shape, NARROW)
+
+
+def forward_dft(place, records, tables, after):
+    sources, receivers, samples = records.shape
+    half = sources // 2
+    width = 2 * receivers
+    sizes = [table.shape[1] for table in tables for _ in range(table.shape[0])]
+    rows = sum(sizes)
+
+    def kernel(place_ref, after_ref, *refs):
+        table_refs, records_ref = refs[:len(tables)], refs[len(tables)]
+        out_refs, (turned, table) = refs[len(tables) + 1:-2], refs[-2:]
+
+        @pl.when(pl.program_id(0) == 0)
+        def _():
+            at = 0
+            for ref in table_refs:
+                parts, size, _ = ref.shape
+                for part in range(parts):
+                    which = (place_ref[0] ^ part) if parts > 1 else 0
+                    table[at:at + size, :] = ref[which]
+                    at += size
+
+        for p in range(0, ROWS, 2):
+            traces = jnp.concatenate(
+                [records_ref[s, p + d] for d in range(2) for s in range(2)], axis=0
+            )
+            found = lax.dot_general(table[...], traces, NT, preferred_element_type=WIDE)
+            turned[p] = found[:, :width]
+            turned[p + 1] = found[:, width:]
+        at = 0
+        for out_ref, size in zip(out_refs, sizes):
+            out_ref[...] = jnp.swapaxes(turned[:, at:at + size, :], 0, 1).astype(NARROW)
+            at += size
+
+    return pl.pallas_call(
+        kernel,
+        grid=(half // ROWS,),
+        in_specs=[IN_SMEM, UNREAD]
+        + [pl.BlockSpec(table.shape, lambda i: (0, 0, 0)) for table in tables]
+        + [pl.BlockSpec((2, ROWS, receivers, samples), lambda i: (0, i, 0, 0))],
+        out_specs=[pl.BlockSpec((size, ROWS, width), lambda i: (0, i, 0)) for size in sizes],
+        out_shape=[shaped(size, half, width) for size in sizes],
+        scratch_shapes=[
+            pltpu.VMEM((ROWS, rows, width), WIDE),
+            pltpu.VMEM((rows, samples), NARROW),
+        ],
+        compiler_params=params(),
+        cost_estimate=cost(2 * rows * records.size, 2 * (records.size + rows * half * width)),
+    )(place, after, *tables, records.reshape(2, half, receivers, samples))
+
+
+def inverse_dft(place, pieces, tables):
+    half, width = pieces[0][0].shape[1:]
+    receivers = width // 2
+    samples = tables[0].shape[-1]
+    spectra = [piece for group in pieces for piece in group]
+    sizes = [piece.shape[0] for piece in spectra]
+    rows = sum(sizes)
+
+    def kernel(place_ref, *refs):
+        table_refs = refs[:len(tables)]
+        spectra_refs = refs[len(tables):len(tables) + len(spectra)]
+        out_ref, turned, table = refs[len(tables) + len(spectra):]
+
+        @pl.when(pl.program_id(0) == 0)
+        def _():
+            at = 0
+            for table_ref, group in zip(table_refs, pieces):
+                for part, piece in enumerate(group):
+                    size = piece.shape[0]
+                    which = (place_ref[0] ^ part) if len(group) > 1 else 0
+                    table[at:at + size, :] = table_ref[which]
+                    at += size
+
+        at = 0
+        for ref, size in zip(spectra_refs, sizes):
+            turned[:, at:at + size, :] = jnp.swapaxes(ref[...].astype(WIDE), 0, 1)
+            at += size
+        for p in range(ROWS):
+            traces = lax.dot_general(
+                turned[p].astype(NARROW), table[...], TN, preferred_element_type=WIDE
+            ).astype(out_ref.dtype)
+            out_ref[0, p] = traces[:receivers]
+            out_ref[1, p] = traces[receivers:]
+
+    return pl.pallas_call(
+        kernel,
+        grid=(half // ROWS,),
+        in_specs=[IN_SMEM]
+        + [pl.BlockSpec(table.shape, lambda i: (0, 0, 0)) for table in tables]
+        + [pl.BlockSpec((size, ROWS, width), lambda i: (0, i, 0)) for size in sizes],
+        out_specs=pl.BlockSpec((2, ROWS, receivers, samples), lambda i: (0, i, 0, 0)),
+        out_shape=shaped(2, half, receivers, samples),
+        scratch_shapes=[
+            pltpu.VMEM((ROWS, rows, width), WIDE),
+            pltpu.VMEM((rows, samples), NARROW),
+        ],
+        compiler_params=params(),
+        cost_estimate=cost(
+            2 * rows * half * width * samples, 2 * half * width * (samples + rows)
+        ),
+    )(place, *tables, *spectra).reshape(2 * half, receivers, samples)
+
+
+def swap_quarters(block):
+    size = block.shape[0]
+    half = size // 2
+    rolled = pltpu.roll(block, half, 1)
+    left = left_half(half, size)
+    return jnp.concatenate(
+        [
+            jnp.where(left, block[:half], rolled[half:]),
+            jnp.where(left, rolled[:half], block[half:]),
+        ],
+        axis=0,
+    )
+
+
+def left_half(rows, lanes):
+    return lax.broadcasted_iota(jnp.int32, (rows, lanes), 1) < lanes // 2
+
+
+def pack_diagonals(real, imag):
+    half, size = real.shape[0] // 2, real.shape[0]
+    last = jnp.where(left_half(half, size), pltpu.roll(real[half:], half, 1), imag[half:])
+    return real[:half], imag[:half], last
+
+
+def unpack_diagonal(top, last, c):
+    half, size = top.shape
+    if c == 0:
+        last = pltpu.roll(last, half, 1)
+    mirrored = jnp.concatenate([top, top], axis=0).T
+    return jnp.concatenate([top, jnp.where(left_half(half, size), mirrored[half:], last)], axis=0)
+
+
+def square(ref, *at):
+    halves = ref[at] if at else ref[...]
+    return halves.astype(WIDE).reshape(2 * halves.shape[-2], halves.shape[-1])
+
+
+def dot(left, right):
+    return jnp.dot(left, right, preferred_element_type=WIDE)
+
+
+def series(real_k, imag_k, recip, first, out_block, tile):
+    order = recip.shape[-1]
+    panel = min(2 * tile, order)
+
+    def scaled(real, imag):
+        return real_k * real - imag_k * imag, real_k * imag + imag_k * real
+
+    for start in range(0, order, panel):
+        rows = pl.ds(start, panel)
+        a, b = recip[0, rows, :], recip[1, rows, :]
+        real, imag = scaled(
+            dot(a, recip[0]) - dot(b, recip[1]), dot(a, recip[1]) + dot(b, recip[0])
+        )
+        first[0, rows, :] = real.astype(NARROW)
+        first[1, rows, :] = imag.astype(NARROW)
+    for start in range(0, order, panel):
+        rows = pl.ds(start, panel)
+        own = [first[c, rows, :].astype(WIDE) for c in range(2)]
+        a, b = [(recip[c, rows, :].astype(WIDE) + own[c]).astype(NARROW) for c in range(2)]
+        real, imag = scaled(
+            dot(a, first[0]) - dot(b, first[1]), dot(a, first[1]) + dot(b, first[0])
+        )
+        real, imag = own[0] + real, own[1] + imag
+        for row in range(0, panel, tile):
+            for b in range(order // tile):
+                at = (slice(row, row + tile), slice(b * tile, (b + 1) * tile))
+                out_block(
+                    (start + row) // tile, b, swap_quarters(real[at]), swap_quarters(imag[at])
+                )
+
+
+def far_units(n):
+    pair = 4 * (n - 2)
+    return pair, pair + 2, pair + 5
+
+
+def predict(place, coeff, moved, n, direct_in, direct_out, start, stop, after):
+    freqs = stop - start
+    half, tile = moved[0].shape[-2:]
+    order = n * tile
+    pair_at, diagonal_at, units = far_units(n)
+
+    def kernel(place_ref, coeff_ref, after_ref, *refs):
+        count = 1 if direct_in else n
+        moved_refs, refs = refs[:count], refs[count:]
+        count = 1 if direct_out else n
+        out_refs, (recip, first) = refs[:count], refs[count:]
+        me = place_ref[0]
+        odd = me % 2 == 1
+
+        def stacked(c, i, j):
+            if direct_in:
+                return square(moved_refs[0], pl.ds((j ^ me) * 2, 2), i, 0, c)
+            if i < 2:
+                return square(moved_refs[i], i ^ j, 0, c)
+            return square(moved_refs[i], 0, pl.ds(((i ^ j) - 2) * 4 + 2 * c, 2))
+
+        def mean(c, a, b):
+            if direct_in or a < 2 or (a ^ b) >= 2:
+                return 0.5 * (stacked(c, a, b) + stacked(c, b, a).T)
+            if a == b:
+                ref = moved_refs[a]
+                top = ref[0, diagonal_at + c].astype(WIDE)
+                return unpack_diagonal(top, ref[0, diagonal_at + 2].astype(WIDE), c)
+            here = square(moved_refs[a], 0, pl.ds(pair_at, 2))
+            there = square(moved_refs[b], 0, pl.ds(pair_at, 2)).T
+            return jnp.where(odd == (c == 0), here, there)
+
+        for c in range(2):
+            for a in range(n):
+                for b in range(a + 1):
+                    block = swap_quarters(mean(c, a, b))
+                    rows, columns = slice(a * tile, (a + 1) * tile), slice(b * tile, (b + 1) * tile)
+                    recip[c, rows, columns] = block.astype(NARROW)
+                    if a != b:
+                        recip[c, columns, rows] = block.T.astype(NARROW)
+
+        def out_block(a, b, real, imag):
+            gap = a ^ b
+            if not direct_out and a >= 2 and gap == 1:
+                own = jnp.where(odd == (a % 2 == 0), imag, real).astype(NARROW)
+                out_refs[a][0, pair_at] = own[:half]
+                out_refs[a][0, pair_at + 1] = own[half:]
+                return
+            if not direct_out and a >= 2 and gap == 0:
+                for unit, value in enumerate(pack_diagonals(real, imag)):
+                    out_refs[a][0, diagonal_at + unit] = value.astype(NARROW)
+                return
+            for c, value in enumerate((real, imag)):
+                value = value.astype(NARROW)
+                for h in range(2):
+                    part = value[h * half:(h + 1) * half]
+                    if direct_out:
+                        out_refs[0][(b ^ me) * 2 + h, a, 0, c] = part
+                    elif a < 2:
+                        out_refs[a][gap, 0, c, h] = part
+                    else:
+                        out_refs[a][0, (gap - 2) * 4 + 2 * c + h] = part
+
+        index = pl.program_id(0) + start
+        series(coeff_ref[index, 0], coeff_ref[index, 1], recip, first, out_block, tile)
+
+    whole = (2 * n, n, freqs, 2, half, tile)
+    close = (n, freqs, 2, 2, half, tile)
+    far = (freqs, units, half, tile)
+    split_shapes = [shaped(*close)] * 2 + [shaped(*far)] * (n - 2)
+
+    def specs(direct, first):
+        if direct:
+            block = (2 * n, n, 1, 2, half, tile)
+            return [pl.BlockSpec(block, lambda i: (0, 0, i + first, 0, 0, 0))]
+        close = pl.BlockSpec((n, 1, 2, 2, half, tile), lambda i: (0, i + first, 0, 0, 0, 0))
+        far = pl.BlockSpec((1, units, half, tile), lambda i: (i + first, 0, 0, 0))
+        return [close] * 2 + [far] * (n - 2)
+
+    return pl.pallas_call(
+        kernel,
+        grid=(freqs,),
+        in_specs=[IN_SMEM, IN_SMEM, UNREAD] + specs(direct_in, start),
+        out_specs=specs(direct_out, 0),
+        out_shape=[shaped(*whole)] if direct_out else split_shapes,
+        scratch_shapes=[pltpu.VMEM((2, order, order), NARROW)] * 2,
+        compiler_params=params(),
+        cost_estimate=cost(16 * freqs * order**3, 16 * freqs * order**2),
+    )(place, coeff / math.sqrt(order), after, *moved)
+
+
+def gather_rows(place, moved, pairs, n, after):
+    _, _, freqs, _, half, tile = moved.shape
+    pair_at, diagonal_at, units = far_units(n)
+
+    def kernel(place_ref, after_ref, moved_ref, pairs_ref, *out_refs):
+        me = place_ref[0]
+        mine = me % 2
+
+        def halves(block):
+            return pl.ds((me ^ block) * 2, 2)
+
+        for d in range(2):
+            for block in range(n):
+                for f in range(freqs):
+                    for c in range(2):
+                        out_refs[d][block, f, c] = moved_ref[halves(block), me ^ d, f, c]
+        for d in range(2, n):
+            for f in range(freqs):
+                for block in range(2, n):
+                    for c in range(2):
+                        at = (block - 2) * 4 + 2 * c
+                        out_refs[d][f, at:at + 2] = moved_ref[halves(block), me ^ d, f, c]
+                here = square(moved_ref, halves(1), me ^ d, f, mine)
+                there = square(pairs_ref, (d ^ 1) - 2, slice(None), f)
+                mean = (0.5 * (here + there.T)).astype(NARROW)
+                out_refs[d][f, pair_at] = mean[:half]
+                out_refs[d][f, pair_at + 1] = mean[half:]
+                means = []
+                for c in range(2):
+                    block = square(moved_ref, halves(0), me ^ d, f, c)
+                    means.append(0.5 * (block + block.T))
+                for unit, value in enumerate(pack_diagonals(*means)):
+                    out_refs[d][f, diagonal_at + unit] = value.astype(NARROW)
+
+    close, far = shaped(n, freqs, 2, 2, half, tile), shaped(freqs, units, half, tile)
+    return pl.pallas_call(
+        kernel,
+        in_specs=[IN_SMEM, UNREAD] + [IN_VMEM] * 2,
+        out_specs=[IN_VMEM] * n,
+        out_shape=[close] * 2 + [far] * (n - 2),
+        compiler_params=params(),
+        cost_estimate=cost(0, 4 * moved.size),
+    )(place, after, moved, pairs)
+
+
+def scatter_rows(place, groups, pairs, n, after):
+    half, tile = pairs.shape[-2:]
+    counts = [rows[0].shape[1] for rows in groups]
+    freqs = sum(counts)
+    pair_at, diagonal_at, units = far_units(n)
+
+    def kernel(place_ref, after_ref, *refs):
+        pairs_ref, out_ref = refs[-2:]
+        me = place_ref[0]
+        mine = me % 2
+
+        def put(block, d, f, c, value):
+            value = value.astype(NARROW)
+            at = (me ^ block) * 2
+            out_ref[at, me ^ d, f, c] = value[:half]
+            out_ref[at + 1, me ^ d, f, c] = value[half:]
+
+        def put_all(row_refs, d, f, own):
+            ref = row_refs[d]
+            if d < 2:
+                for block in range(n):
+                    for c in range(2):
+                        put(block, d, f, c, square(ref, block, own, c))
+                return
+            for block in range(2, n):
+                for c in range(2):
+                    at = (block - 2) * 4 + 2 * c
+                    put(block, d, f, c, square(ref, own, pl.ds(at, 2)))
+            put(1, d, f, mine, square(ref, own, pl.ds(pair_at, 2)))
+            put(1, d, f, 1 - mine, square(pairs_ref, (d ^ 1) - 2, f).T)
+            last = ref[own, diagonal_at + 2].astype(WIDE)
+            for c in range(2):
+                put(0, d, f, c, unpack_diagonal(ref[own, diagonal_at + c].astype(WIDE), last, c))
+
+        f = 0
+        for group, count in enumerate(counts):
+            for own in range(count):
+                for d in range(n):
+                    put_all(refs[group * n:(group + 1) * n], d, f, own)
+                f += 1
+
+    arrays = [array for rows in groups for array in rows]
+    return pl.pallas_call(
+        kernel,
+        in_specs=[IN_SMEM, UNREAD] + [IN_VMEM] * (len(arrays) + 1),
+        out_specs=IN_VMEM,
+        out_shape=shaped(2 * n, n, freqs, 2, half, tile),
+        compiler_params=params(),
+        cost_estimate=cost(0, 0),
+    )(place, after, *arrays, pairs)
+
+
+def side_by_side(parts, after):
+    shape = parts[0].shape
+    n = len(parts)
+
+    def kernel(after_ref, *refs):
+        for part, ref in enumerate(refs[:n]):
+            refs[n][:, part] = ref[...]
+
+    return pl.pallas_call(
+        kernel,
+        in_specs=[UNREAD] + [IN_VMEM] * n,
+        out_specs=IN_VMEM,
+        out_shape=shaped(shape[0], n, *shape[1:]),
+        compiler_params=params(),
+        cost_estimate=cost(0, 4 * n * parts[0].size),
+    )(after, *parts)
+
+
+def apart(moved, start):
+    shape = moved.shape
+    n, freqs = shape[1], shape[2] - start
+
+    def kernel(moved_ref, *out_refs):
+        for part, ref in enumerate(out_refs):
+            ref[...] = moved_ref[:, part, start:]
+
+    return pl.pallas_call(
+        kernel,
+        in_specs=[IN_VMEM],
+        out_specs=[IN_VMEM] * n,
+        out_shape=[shaped(shape[0], freqs, *shape[3:])] * n,
+        compiler_params=params(),
+        cost_estimate=cost(0, 0),
+    )(moved)
+
+
+def gate(value, *after):
+    return lax.optimization_barrier((value, *after))[0]
+
+
+def chunk_sizes(per_group):
+    return [per_group // 2, per_group - per_group // 2]
+
+
+def swapped(value, gap):
+    size = lax.axis_size("src")
+    return lax.ppermute(value, "src", [(i, i ^ gap) for i in range(size)])
+
+
+def spread(value):
+    return lax.all_to_all(value, "rcv", split_axis=0, concat_axis=0, tiled=True)
+
+
+def local_tiles(records, surface_operator):
+    src_tiles, rcv_tiles, samples = records.shape
+    freqs = surface_operator.shape[0]
+    n = lax.axis_size("src")
+    devices = 2 * n * n
+    half = src_tiles // 2
+    me, column = lax.axis_index("src"), lax.axis_index("rcv")
+    place = me.astype(jnp.int32)[None]
+    sizes = chunk_sizes(freqs // devices)
+    starts = [devices * sum(sizes[:q]) for q in range(len(sizes))]
+
+    forward, inverse = host_tables(freqs, samples)
+
+    def rows_of(table, q):
+        return table[starts[q]:starts[q] + devices * sizes[q]]
+
+    def by_owner(table, q):
+        rows = rows_of(table, q).reshape(2 * n, n, sizes[q] * 2, samples)
+        return rows.swapaxes(0, 1).reshape(n, -1, samples)
+
+    coeffs = []
+    for q, size in enumerate(sizes):
+        at = starts[q] + (column * n + me) * size
+        coeffs.append(lax.dynamic_slice_in_dim(surface_operator, at, size, 0))
+
+    def first_part(q):
+        if q == 0:
+            return jnp.asarray(by_owner(forward, 0))
+        return jnp.asarray(rows_of(forward, q).reshape(1, -1, samples))
+
+    def over_src(rows):
+        return [rows[0]] + [swapped(rows[d], d) for d in range(1, n)]
+
+    def pair_of(moved, q):
+        theirs = 1 - me % 2
+        pairs = []
+        for d in range(2, n):
+            at = ((me ^ 1) * 2, me ^ d, 0, theirs, 0, 0)
+            pair = lax.dynamic_slice(moved, at, (2, 1, sizes[q], 1, half, src_tiles))
+            pairs.append(pair.reshape(2, sizes[q], half, src_tiles))
+        return swapped(jnp.stack(pairs), 1)
+
+    def spread_chunk(spectrum, q):
+        return spread(spectrum.reshape(2 * n, n, sizes[q], 2, half, src_tiles))
+
+    def gather(moved, q, after):
+        return gather_rows(place, moved, pair_of(moved, q), n, after)
+
+    def pairs_of(groups):
+        pair_at = far_units(n)[0]
+        return jnp.stack(
+            [
+                jnp.concatenate([rows[d][:, pair_at:pair_at + 2] for rows in groups])
+                for d in range(2, n)
+            ]
+        )
+
+    def flat(moved):
+        return moved.reshape(-1, half, src_tiles)
+
+    *early, spectrum = forward_dft(place, records, [first_part(0), first_part(1)], place)
+    early = over_src(early)
+    moved1 = spread_chunk(spectrum, 1)
+    sent1 = gather(moved1, 1, place)
+    rows1 = over_src(sent1)
+    parts = [part.reshape(2 * n, sizes[0], 2, half, src_tiles) for part in early]
+    moved0 = spread(side_by_side(parts, sent1[0]))
+    rest0 = predict(place, coeffs[0], [moved0], n, True, False, 1, sizes[0], sent1[0])
+    sent0 = rest0[0]
+    first0 = predict(place, coeffs[0], [moved0], n, True, False, 0, 1, sent0)
+    sent0 = first0[0]
+    first0 = over_src(first0)
+    rest0 = over_src(rest0)
+    back1 = predict(place, coeffs[1], rows1, n, False, True, 0, sizes[1], sent0)[0]
+    moved = spread(gate(back1, *first0[1:]))
+    first1 = over_src([moved[:, d, :1] for d in range(n)])
+    rest1 = apart(moved, 1)
+    sent1 = rest1[0]
+    rest1 = over_src(rest1)
+    pairs = swapped(pairs_of([first0, rest0]), 1)
+    home0 = scatter_rows(place, [first0, rest0], pairs, n, sent1)
+    home0 = spread(gate(home0, *first1[1:]))
+    pieces = [[flat(home0)], [flat(x) for x in first1], [flat(x) for x in rest1]]
+    last = by_owner(inverse, 1).reshape(n, 2 * n, sizes[1], 2, samples)
+    tables = [
+        jnp.asarray(rows_of(inverse, 0).reshape(1, -1, samples)),
+        jnp.asarray(last[:, :, :1].reshape(n, -1, samples)),
+        jnp.asarray(last[:, :, 1:].reshape(n, -1, samples)),
+    ]
+    return inverse_dft(place, pieces, tables)
+
+
 def solution(mesh):
     placed = (P("src", "rcv", None), P())
+    n_src, n_rcv = mesh.shape["src"], mesh.shape["rcv"]
+
+    def local(records, surface_operator):
+        src_tiles, rcv_tiles, _ = records.shape
+        per_group = surface_operator.shape[0] // (n_src * n_rcv)
+        square_tiles = n_rcv == 2 * n_src and src_tiles == 2 * rcv_tiles
+        whole_lanes = src_tiles % 128 == 0 and n_src >= 4 and n_src & (n_src - 1) == 0
+        if square_tiles and whole_lanes and per_group >= 4:
+            return local_tiles(records, surface_operator)
+        return local_general(records, surface_operator)
+
     return jax.shard_map(
         local, mesh=mesh, in_specs=placed, out_specs=P("src", "rcv", None), check_vma=False
     )

time: 854 us -> 403 us (0.47); the launches traced: 838 us -> 402 us
  local copies, waits for them, and re-layouts: 278 us -> 9.81 us
  matrix products: 134 us -> 0 us
  waiting for transfers between devices: 358 us -> 273 us
  Pallas kernels: 0 us -> 75.2 us
  other arithmetic: 51.4 us -> 1.28 us
  starting transfers between devices: 16.4 us -> 42.8 us
    all_to_all x2 -> x4, waiting for transfers between devices: 358 us -> 87.7 us  [spread(): return lax.all_to_all(value, 'rcv', split_axis=0, concat_axis=0, tiled=True)]
    ppermute x0 -> x20, waiting for transfers between devices: none -> 185 us  [swapped(): return lax.ppermute(value, 'src', [(i, i ^ gap) for i in range(size)])]
    dot_general x14 -> x0, matrix products: 134 us -> none  [the longest x12 114 us: mult(): jnp.einsum('nij,njk->nik', first_op, second_op, preferred_element_type=jn...]
    convert_element_type x7 -> x0, local copies, waits for them, and re-layouts: 110 us -> none  [the longest x5 110 us: predict_block(): blocks.astype(jnp.float32) + jnp.swapaxes(blocks, 2, 3).astype(jnp.float32)]
    pallas_call x0 -> x9, Pallas kernels: none -> 75.2 us  [the longest x3 35.2 us: predict(): pl.pallas_call(kernel, grid=(freqs,), in_specs=[IN_SMEM, IN_SMEM, UNREAD]...]
    reshape x4 -> x0, local copies, waits for them, and re-layouts: 74.4 us -> none  [the longest x2 47.2 us: local(): outgoing.reshape(1, per_group, 2, n_src * n_rcv, columns)]
    another operation x12 -> x1, local copies, waits for them, and re-layouts: 74.7 us -> 0.99 us  [pair_of(): return swapped(jnp.stack(pairs), 1)]
    convert_element_type x2 -> x0, other arithmetic: 29 us -> none  [the longest x1 17 us: predict_block(): blocks.astype(jnp.float32) + jnp.swapaxes(blocks, 2, 3).astype(jnp.float32)]
  transfers between devices with their start and end apart: 2 -> 24, of which waited for: 2 -> 12; matrix products, arithmetic and copies ran while one was open for 0% -> 1% of each run, Pallas kernels for 0% -> 12%
where the time goes in v2:
time: 403 us; the launch traced here: 402 us
  waiting for transfers between devices  273 us (68%)
  Pallas kernels  75.2 us (19%)
  starting transfers between devices  42.8 us (11%)
  local copies, waits for them, and re-layouts  9.81 us (2%)
    ppermute x20, waiting for transfers between devices, swapped(): return lax.ppermute(value, 'src', [(i, i ^ gap) for i in range(size)])  185 us
    all_to_all x4, waiting for transfers between devices, spread(): return lax.all_to_all(value, 'rcv', split_axis=0, concat_axis=0, tiled=True)  87.7 us
    pallas_call x3, Pallas kernels, predict(): pl.pallas_call(kernel, grid=(freqs,), in_specs=[IN_SMEM, IN_SMEM, UNREAD]...  35.2 us
    ppermute x20, starting transfers between devices, swapped(): return lax.ppermute(value, 'src', [(i, i ^ gap) for i in range(size)])  23.3 us
    all_to_all x4, starting transfers between devices, spread(): return lax.all_to_all(value, 'rcv', split_axis=0, concat_axis=0, tiled=True)  19.5 us
    pallas_call x1, Pallas kernels, inverse_dft(): pl.pallas_call(kernel, grid=(half // ROWS,), in_specs=[IN_SMEM] + [pl.Blo...  11.3 us
    pallas_call x1, Pallas kernels, forward_dft(): pl.pallas_call(kernel, grid=(half // ROWS,), in_specs=[IN_SMEM, UNREAD] +...  10.9 us
  transfers between devices with their start and end apart: 24, of which 12 were waited for; matrix products, arithmetic and copies ran while one was open for 1% of the time, Pallas kernels for 12%

profile of v2, /device:TPU:10, one launch (start us, length us, event | category | flops | bytes accessed | tf_op | source)
XLA Modules:
  0.0 402.3 jit_solution(3321109494844464219)
XLA Ops:
  0.0 10.9 %shard_map.73 = (bf16[64,64,128]{2,1,0:T(8,128)(2,1)}, bf16[64,64,128]{2,1,0:T(8,128)(2,1)}, bf16[64,64,128]{2,1,0:T(8,128)(2,1)}, bf16[64,64,128]{2,1,0:T(8,128)(2,1)}, bf16[256,64,128]{2,1,0:T(8,128)(2,1)}) custom-call(s32[1]{0:T(128)} %bitcast.place_ref.after_ref, s32[1]{0:T(128)} %bitcast.place_ref.after_ref, ...), custom_call_target="tpu_custom_call" | custom-call | tf_op jit(solution)/shard_map/pallas_call | solution.py:168
  10.9 5.0 %all-to-all-start = ((bf16[8,4,4,2,64,128]{5,4,3,2,1,0:T(8,128)(2,1)}), bf16[8,4,4,2,64,128]{5,4,3,2,1,0:T(8,128)(2,1)}, u32[]{:S(2)}, u32[]{:S(2)}) async-start(bf16[8,4,4,2,64,128]{5,4,3,2,1,0:T(8,128)(2,1)} %bitcast.32), calls=%async_computation | async-start | bytes 8388608 | tf_op jit(solution)/shard_map/all_to_all | solution.py:553
  15.9 3.0 collective-permute-start.2
  19.4 44.2 %all-to-all-done.moved_ref = bf16[8,4,4,2,64,128]{5,4,3,2,1,0:T(8,128)(2,1)} async-done(((bf16[8,4,4,2,64,128]{5,4,3,2,1,0:T(8,128)(2,1)}), bf16[8,4,4,2,64,128]{5,4,3,2,1,0:T(8,128)(2,1)}, u32[]{:S(2)}, u32[]{:S(2)}) %all-to-all-start) | async-done | bytes 4194336 | tf_op jit(solution)/shard_map/all_to_all | solution.py:553
  64.7 27.9 %collective-permute-done.pairs_ref = bf16[2,2,4,64,128]{4,3,2,1,0:T(8,128)(2,1)S(1)} collective-permute-done((bf16[2,2,4,64,128]{4,3,2,1,0:T(8,128)(2,1)S(1)}, bf16[2,2,4,64,128]{4,3,2,1,0:T(8,128)(2,1)S(1)}, u32[]{:S(2)}, u32[]{:S(2)}) %collective-permute-start) | collective-permute-done | bytes 262176 | tf_op jit(solution)/shard_map/ppermute | solution.py:549
  93.3 4.5 %shard_map.74 = (bf16[4,4,2,2,64,128]{5,4,3,2,1,0:T(8,128)(2,1)}, bf16[4,4,2,2,64,128]{5,4,3,2,1,0:T(8,128)(2,1)}, bf16[4,13,64,128]{3,2,1,0:T(8,128)(2,1)}, bf16[4,13,64,128]{3,2,1,0:T(8,128)(2,1)}) custom-call(s32[1]{0:T(128)} %bitcast.place_ref.after_ref, s32[1]{0:T(128)} %bitcast.place_ref.after_ref, ...), custom_call_target="tpu_custom_call" | custom-call | tf_op jit(solution)/shard_map/pallas_call | solution.py:441
  97.8 12.2 %collective-permute-done.3 = bf16[64,64,128]{2,1,0:T(8,128)(2,1)S(1)} collective-permute-done((bf16[64,64,128]{2,1,0:T(8,128)(2,1)}, bf16[64,64,128]{2,1,0:T(8,128)(2,1)S(1)}, u32[]{:S(2)}, u32[]{:S(2)}) %collective-permute-start.3) | collective-permute-done | bytes 1048608 | tf_op jit(solution)/shard_map/ppermute | solution.py:549
  111.0 4.5 %shard_map.75 = bf16[8,4,4,2,64,128]{5,4,3,2,1,0:T(8,128)(2,1)} custom-call(bf16[4,4,2,2,64,128]{5,4,3,2,1,0:T(8,128)(2,1)} %get-tuple-element.29.after_ref.refs_0_, bf16[8,4,2,64,128]{4,3,2,1,0:T(8,128)(2,1)} %bitcast.35, bf16[8,4,2,64,128]{4,3,2,1,0:T(8,128)(2,1)} %bitcast.36, bf16[8,4,2,64,128]{4,3,2,1,0:T(8,128)(2,1)} %bitcast.37, ...), custom_call_target="tpu_custom_call" | custom-call | tf_op jit(solution)/shard_map/pallas_call | solution.py:511
  115.4 4.9 %all-to-all-start.1 = ((bf16[8,4,4,2,64,128]{5,4,3,2,1,0:T(8,128)(2,1)}), bf16[8,4,4,2,64,128]{5,4,3,2,1,0:T(8,128)(2,1)}, u32[]{:S(2)}, u32[]{:S(2)}) async-start(bf16[8,4,4,2,64,128]{5,4,3,2,1,0:T(8,128)(2,1)} %shard_map.75), calls=%async_computation.1 | async-start | bytes 8388608 | tf_op jit(solution)/shard_map/all_to_all | solution.py:553
  120.4 3.0 collective-permute-start.4
  124.7 43.5 %all-to-all-done.1.refs_0_ = bf16[8,4,4,2,64,128]{5,4,3,2,1,0:T(8,128)(2,1)} async-done(((bf16[8,4,4,2,64,128]{5,4,3,2,1,0:T(8,128)(2,1)}), bf16[8,4,4,2,64,128]{5,4,3,2,1,0:T(8,128)(2,1)}, u32[]{:S(2)}, u32[]{:S(2)}) %all-to-all-start.1) | async-done | bytes 4194336 | tf_op jit(solution)/shard_map/all_to_all | solution.py:553
  168.1 12.9 %shard_map.76 = (bf16[4,3,2,2,64,128]{5,4,3,2,1,0:T(8,128)(2,1)}, bf16[4,3,2,2,64,128]{5,4,3,2,1,0:T(8,128)(2,1)}, bf16[3,13,64,128]{3,2,1,0:T(8,128)(2,1)}, bf16[3,13,64,128]{3,2,1,0:T(8,128)(2,1)}) custom-call(s32[1]{0:T(128)} %bitcast.place_ref.after_ref, f32[4,2]{1,0:T(4,128)} %broadcast_multiply_fusion.coeff_ref, ...), custom_call_target="tpu_custom_call" | custom-call | tf_op jit(solution)/shard_map/pallas_call | solution.py:394
  181.0 5.5 %shard_map.77 = (bf16[4,1,2,2,64,128]{5,4,3,2,1,0:T(8,128)(2,1)}, bf16[4,1,2,2,64,128]{5,4,3,2,1,0:T(8,128)(2,1)}, bf16[1,13,64,128]{3,2,1,0:T(8,128)(2,1)}, bf16[1,13,64,128]{3,2,1,0:T(8,128)(2,1)}) custom-call(s32[1]{0:T(128)} %bitcast.place_ref.after_ref, f32[4,2]{1,0:T(4,128)} %broadcast_multiply_fusion.coeff_ref, ...), custom_call_target="tpu_custom_call" | custom-call | tf_op jit(solution)/shard_map/pallas_call | solution.py:394
  186.6 3.0 collective-permute-start.8
  190.7 15.2 %collective-permute-done.6.refs_3_ = bf16[4,13,64,128]{3,2,1,0:T(8,128)(2,1)S(1)} collective-permute-done((bf16[4,13,64,128]{3,2,1,0:T(8,128)(2,1)}, bf16[4,13,64,128]{3,2,1,0:T(8,128)(2,1)S(1)}, u32[]{:S(2)}, u32[]{:S(2)}) %collective-permute-start.6) | collective-permute-done | bytes 852000 | tf_op jit(solution)/shard_map/ppermute | solution.py:549
  207.1 16.8 %shard_map.78 = bf16[8,4,4,2,64,128]{5,4,3,2,1,0:T(8,128)(2,1)} custom-call(s32[1]{0:T(128)} %bitcast.place_ref.after_ref, f32[4,2]{1,0:T(4,128)} %broadcast_multiply_fusion.1.coeff_ref, bf16[4,1,2,2,64,128]{5,4,3,2,1,0:T(8,128)(2,1)} %get-tuple-element.35.after_ref.refs_0_, bf16[4,4,2,2,64,128]{5,4,3,2,1,0:T(8,128)(2,1)} %get-tuple-element.29.after_ref.refs_0_, ...), custom_call_target="tpu_custom_call" | custom-call | tf_op jit(solution)/shard_map/pallas_call | solution.py:394
  224.8 4.8 %all-to-all-start.2 = ((bf16[8,4,4,2,64,128]{5,4,3,2,1,0:T(8,128)(2,1)}), bf16[8,4,4,2,64,128]{5,4,3,2,1,0:T(8,128)(2,1)}, u32[]{:S(2)}, u32[]{:S(2)}) async-start(bf16[8,4,4,2,64,128]{5,4,3,2,1,0:T(8,128)(2,1)} %shard_map.78), calls=%async_computation.2 | async-start | bytes 8388608 | tf_op jit(solution)/shard_map/all_to_all | solution.py:553
  230.1 3.9 collective-permute-start.10
  234.0 38.0 %collective-permute-done.11.refs_6_ = bf16[3,13,64,128]{3,2,1,0:T(8,128)(2,1)S(1)} collective-permute-done((bf16[3,13,64,128]{3,2,1,0:T(8,128)(2,1)}, bf16[3,13,64,128]{3,2,1,0:T(8,128)(2,1)S(1)}, u32[]{:S(2)}, u32[]{:S(2)}) %collective-permute-start.11) | collective-permute-done | bytes 639008 | tf_op jit(solution)/shard_map/ppermute | solution.py:549
  272.1 14.0 %collective-permute-done.12.refs_7_ = bf16[3,13,64,128]{3,2,1,0:T(8,128)(2,1)S(1)} collective-permute-done((bf16[3,13,64,128]{3,2,1,0:T(8,128)(2,1)}, bf16[3,13,64,128]{3,2,1,0:T(8,128)(2,1)S(1)}, u32[]{:S(2)}, u32[]{:S(2)}) %collective-permute-start.12) | collective-permute-done | bytes 639008 | tf_op jit(solution)/shard_map/ppermute | solution.py:549
  286.2 2.1 fusion
  289.9 2.7 collective-permute-start.15
  292.7 4.0 shard_map.79
  297.7 4.9 %shard_map.80 = bf16[8,4,4,2,64,128]{5,4,3,2,1,0:T(8,128)(2,1)} custom-call(s32[1]{0:T(128)} %bitcast.place_ref.after_ref, bf16[8,3,2,64,128]{4,3,2,1,0:T(8,128)(2,1)} %get-tuple-element.43.after_ref, bf16[4,1,2,2,64,128]{5,4,3,2,1,0:T(8,128)(2,1)} %get-tuple-element.35.after_ref.refs_0_, bf16[4,1,2,2,64,128]{5,4,3,2,1,0:T(8,128)(2,1)} %copy-done.17, ...), custom_call_target="tpu_custom_call" | custom-call | tf_op jit(solution)/shard_map/pallas_call | solution.py:493
  302.6 6.2 %collective-permute-done.16 = bf16[8,1,2,64,128]{4,3,2,0,1:T(8,128)(2,1)S(1)} collective-permute-done((bf16[8,1,2,64,128]{4,3,2,0,1:T(8,128)(2,1)S(1)}, bf16[8,1,2,64,128]{4,3,2,0,1:T(8,128)(2,1)S(1)}, u32[]{:S(2)}, u32[]{:S(2)}) %collective-permute-start.16) | collective-permute-done | bytes 262176 | tf_op jit(solution)/shard_map/ppermute | solution.py:549
  308.8 3.3 collective-permute-done.15
  313.0 4.7 %all-to-all-start.3 = ((bf16[8,4,4,2,64,128]{5,4,3,2,1,0:T(8,128)(2,1)}), bf16[8,4,4,2,64,128]{5,4,3,2,1,0:T(8,128)(2,1)}, u32[]{:S(2)}, u32[]{:S(2)}) async-start(bf16[8,4,4,2,64,128]{5,4,3,2,1,0:T(8,128)(2,1)} %shard_map.80), calls=%async_computation.3 | async-start | bytes 8388608 | tf_op jit(solution)/shard_map/all_to_all | solution.py:553
  317.7 2.4 collective-permute-start.17
  321.7 32.2 %collective-permute-done.17 = bf16[8,3,2,64,128]{4,3,2,1,0:T(8,128)(2,1)S(1)} collective-permute-done((bf16[8,3,2,64,128]{4,3,2,1,0:T(8,128)(2,1)}, bf16[8,3,2,64,128]{4,3,2,1,0:T(8,128)(2,1)S(1)}, u32[]{:S(2)}, u32[]{:S(2)}) %collective-permute-start.17) | collective-permute-done | bytes 786464 | tf_op jit(solution)/shard_map/ppermute | solution.py:549
  353.9 19.2 %collective-permute-done.18 = bf16[8,3,2,64,128]{4,3,2,1,0:T(8,128)(2,1)S(1)} collective-permute-done((bf16[8,3,2,64,128]{4,3,2,1,0:T(8,128)(2,1)}, bf16[8,3,2,64,128]{4,3,2,1,0:T(8,128)(2,1)S(1)}, u32[]{:S(2)}, u32[]{:S(2)}) %collective-permute-start.18) | collective-permute-done | bytes 786464 | tf_op jit(solution)/shard_map/ppermute | solution.py:549
  373.1 17.0 %collective-permute-done.19 = bf16[8,3,2,64,128]{4,3,2,1,0:T(8,128)(2,1)S(1)} collective-permute-done((bf16[8,3,2,64,128]{4,3,2,1,0:T(8,128)(2,1)}, bf16[8,3,2,64,128]{4,3,2,1,0:T(8,128)(2,1)S(1)}, u32[]{:S(2)}, u32[]{:S(2)}) %collective-permute-start.19) | collective-permute-done | bytes 786464 | tf_op jit(solution)/shard_map/ppermute | solution.py:549
  390.9 11.3 %shard_map.81 = bf16[2,64,64,512]{3,2,1,0:T(8,128)(2,1)} custom-call(s32[1]{0:T(128)} %bitcast.place_ref.after_ref, bf16[1,256,512]{2,1,0:T(8,128)(2,1)} %constant.52.clone.refs_0_, bf16[4,16,512]{2,1,0:T(8,128)(2,1)} %constant.53.clone.refs_1_, bf16[4,48,512]{2,1,0:T(8,128)(2,1)} %constant.54.clone.refs_2_, bf16[256,64,128]{2,1,0:T(8,128)(2,1)} %bitcast.14.refs_3_, ...), custom_call_target="tpu_custom_call" | custom-call | tf_op jit(solution)/shard_map/pallas_call | solution.py:219
  (82 shorter events, 14.4 us)
Async XLA Ops:
  10.9 52.7 %all-to-all-start = ((bf16[8,4,4,2,64,128]{5,4,3,2,1,0:T(8,128)(2,1)}), bf16[8,4,4,2,64,128]{5,4,3,2,1,0:T(8,128)(2,1)}, u32[]{:S(2)}, u32[]{:S(2)}) async-start(bf16[8,4,4,2,64,128]{5,4,3,2,1,0:T(8,128)(2,1)} %bitcast.32), calls=%async_computation | async-start | bytes 8388608 | tf_op jit(solution)/shard_map/all_to_all | solution.py:553
  15.9 81.9 %collective-permute-start.1 = (bf16[64,64,128]{2,1,0:T(8,128)(2,1)}, bf16[64,64,128]{2,1,0:T(8,128)(2,1)S(1)}, u32[]{:S(2)}, u32[]{:S(2)}) collective-permute-start(bf16[64,64,128]{2,1,0:T(8,128)(2,1)} %get-tuple-element.31), channel_id=1, source_target_pairs={{0,8},{8,0},{16,24},{24,16},{1,9},{9,1},{17,25},{25,17},{2,10},{10... | collective-permute-start | bytes 3145736 | tf_op jit(solution)/shard_map/ppermute | solution.py:549
  15.9 81.8 %collective-permute-start.2 = (bf16[64,64,128]{2,1,0:T(8,128)(2,1)}, bf16[64,64,128]{2,1,0:T(8,128)(2,1)S(1)}, u32[]{:S(2)}, u32[]{:S(2)}) collective-permute-start(bf16[64,64,128]{2,1,0:T(8,128)(2,1)} %get-tuple-element.32), channel_id=1, source_target_pairs={{0,16},{8,24},{16,0},{24,8},{1,17},{9,25},{17,1},{25,9},{2,18},{10... | collective-permute-start | bytes 3145736 | tf_op jit(solution)/shard_map/ppermute | solution.py:549
  18.9 91.1 %collective-permute-start.3 = (bf16[64,64,128]{2,1,0:T(8,128)(2,1)}, bf16[64,64,128]{2,1,0:T(8,128)(2,1)S(1)}, u32[]{:S(2)}, u32[]{:S(2)}) collective-permute-start(bf16[64,64,128]{2,1,0:T(8,128)(2,1)} %get-tuple-element.33), channel_id=1, source_target_pairs={{0,24},{8,16},{16,8},{24,0},{1,25},{9,17},{17,9},{25,1},{2,26},{10... | collective-permute-start | bytes 3145736 | tf_op jit(solution)/shard_map/ppermute | solution.py:549
  64.6 27.9 %collective-permute-start = (bf16[2,2,4,64,128]{4,3,2,1,0:T(8,128)(2,1)S(1)}, bf16[2,2,4,64,128]{4,3,2,1,0:T(8,128)(2,1)S(1)}, u32[]{:S(2)}, u32[]{:S(2)}) collective-permute-start(bf16[2,2,4,64,128]{4,3,2,1,0:T(8,128)(2,1)S(1)} %pad_maximum_fusion), channel_id=1, source_target_pairs={{0,8},{8,0},{16,24},{24,16},{1,9},{9,1},{17,25},{25,17},{2,10},{10... | collective-permute-start | bytes 786440 | tf_op jit(solution)/shard_map/ppermute | solution.py:549
  97.8 12.2 %copy-start = (bf16[64,64,128]{2,1,0:T(8,128)(2,1)}, bf16[64,64,128]{2,1,0:T(8,128)(2,1)S(1)}, u32[]{:S(2)}) copy-start(bf16[64,64,128]{2,1,0:T(8,128)(2,1)S(1)} %collective-permute-done.1) | copy-start | bytes 3145732
  97.8 12.2 %copy-start.1 = (bf16[64,64,128]{2,1,0:T(8,128)(2,1)}, bf16[64,64,128]{2,1,0:T(8,128)(2,1)S(1)}, u32[]{:S(2)}) copy-start(bf16[64,64,128]{2,1,0:T(8,128)(2,1)S(1)} %collective-permute-done.2) | copy-start | bytes 3145732
  115.4 52.7 %all-to-all-start.1 = ((bf16[8,4,4,2,64,128]{5,4,3,2,1,0:T(8,128)(2,1)}), bf16[8,4,4,2,64,128]{5,4,3,2,1,0:T(8,128)(2,1)}, u32[]{:S(2)}, u32[]{:S(2)}) async-start(bf16[8,4,4,2,64,128]{5,4,3,2,1,0:T(8,128)(2,1)} %shard_map.75), calls=%async_computation.1 | async-start | bytes 8388608 | tf_op jit(solution)/shard_map/all_to_all | solution.py:553
  120.4 69.2 %collective-permute-start.5 = (bf16[4,13,64,128]{3,2,1,0:T(8,128)(2,1)}, bf16[4,13,64,128]{3,2,1,0:T(8,128)(2,1)S(1)}, u32[]{:S(2)}, u32[]{:S(2)}) collective-permute-start(bf16[4,13,64,128]{3,2,1,0:T(8,128)(2,1)} %get-tuple-element.37), channel_id=1, source_target_pairs={{0,16},{8,24},{16,0},{24,8},{1,17},{9,25},{17,1},{25,9},{2,18},{10... | collective-permute-start | bytes 2555912 | tf_op jit(solution)/shard_map/ppermute | solution.py:549
  120.4 85.5 %collective-permute-start.4 = (bf16[4,4,2,2,64,128]{5,4,3,2,1,0:T(8,128)(2,1)}, bf16[4,4,2,2,64,128]{5,4,3,2,1,0:T(8,128)(2,1)S(1)}, u32[]{:S(2)}, u32[]{:S(2)}) collective-permute-start(bf16[4,4,2,2,64,128]{5,4,3,2,1,0:T(8,128)(2,1)} %get-tuple-element.36), channel_id=1, source_target_pairs={{0,8},{8,0},{16,24},{24,16},{1,9},{9,1},{17,25},{25,17},{2,10},{10... | collective-permute-start | bytes 3145736 | tf_op jit(solution)/shard_map/ppermute | solution.py:549
  123.4 82.4 %collective-permute-start.6 = (bf16[4,13,64,128]{3,2,1,0:T(8,128)(2,1)}, bf16[4,13,64,128]{3,2,1,0:T(8,128)(2,1)S(1)}, u32[]{:S(2)}, u32[]{:S(2)}) collective-permute-start(bf16[4,13,64,128]{3,2,1,0:T(8,128)(2,1)} %get-tuple-element.38), channel_id=1, source_target_pairs={{0,24},{8,16},{16,8},{24,0},{1,25},{9,17},{17,9},{25,1},{2,26},{10... | collective-permute-start | bytes 2555912 | tf_op jit(solution)/shard_map/ppermute | solution.py:549
  186.5 37.5 %collective-permute-start.7 = (bf16[4,1,2,2,64,128]{5,4,3,2,1,0:T(8,128)(2,1)}, bf16[4,1,2,2,64,128]{5,4,3,2,1,0:T(8,128)(2,1)S(1)}, u32[]{:S(2)}, u32[]{:S(2)}) collective-permute-start(bf16[4,1,2,2,64,128]{5,4,3,2,1,0:T(8,128)(2,1)} %get-tuple-element.39), channel_id=1, source_target_pairs={{0,8},{8,0},{16,24},{24,16},{1,9},{9,1},{17,25},{25,17},{2,10},{10... | collective-permute-start | bytes 786440 | tf_op jit(solution)/shard_map/ppermute | solution.py:549
  186.6 37.4 %collective-permute-start.8 = (bf16[1,13,64,128]{3,2,1,0:T(8,128)(2,1)}, bf16[1,13,64,128]{3,2,1,0:T(8,128)(2,1)S(1)}, u32[]{:S(2)}, u32[]{:S(2)}) collective-permute-start(bf16[1,13,64,128]{3,2,1,0:T(8,128)(2,1)} %get-tuple-element.40), channel_id=1, source_target_pairs={{0,16},{8,24},{16,0},{24,8},{1,17},{9,25},{17,1},{25,9},{2,18},{10... | collective-permute-start | bytes 638984 | tf_op jit(solution)/shard_map/ppermute | solution.py:549
  189.6 16.2 %copy-start.4 = (bf16[4,13,64,128]{3,2,1,0:T(8,128)(2,1)}, bf16[4,13,64,128]{3,2,1,0:T(8,128)(2,1)S(1)}, u32[]{:S(2)}) copy-start(bf16[4,13,64,128]{3,2,1,0:T(8,128)(2,1)S(1)} %collective-permute-done.5.refs_2_) | copy-start | bytes 2555908
  189.6 34.4 %collective-permute-start.9 = (bf16[1,13,64,128]{3,2,1,0:T(8,128)(2,1)}, bf16[1,13,64,128]{3,2,1,0:T(8,128)(2,1)S(1)}, u32[]{:S(2)}, u32[]{:S(2)}) collective-permute-start(bf16[1,13,64,128]{3,2,1,0:T(8,128)(2,1)} %get-tuple-element.41), channel_id=1, source_target_pairs={{0,24},{8,16},{16,8},{24,0},{1,25},{9,17},{17,9},{25,1},{2,26},{10... | collective-permute-start | bytes 638984 | tf_op jit(solution)/shard_map/ppermute | solution.py:549
  224.0 10.0 %copy-start.12 = (bf16[1,13,64,128]{3,2,1,0:T(8,128)(2,1)}, bf16[1,13,64,128]{3,2,1,0:T(8,128)(2,1)S(1)}, u32[]{:S(2)}) copy-start(bf16[1,13,64,128]{3,2,1,0:T(8,128)(2,1)S(1)} %collective-permute-done.8.refs_2_) | copy-start | bytes 638980
  224.8 61.5 %all-to-all-start.2 = ((bf16[8,4,4,2,64,128]{5,4,3,2,1,0:T(8,128)(2,1)}), bf16[8,4,4,2,64,128]{5,4,3,2,1,0:T(8,128)(2,1)}, u32[]{:S(2)}, u32[]{:S(2)}) async-start(bf16[8,4,4,2,64,128]{5,4,3,2,1,0:T(8,128)(2,1)} %shard_map.78), calls=%async_computation.2 | async-start | bytes 8388608 | tf_op jit(solution)/shard_map/all_to_all | solution.py:553
  229.6 42.5 %collective-permute-start.11 = (bf16[3,13,64,128]{3,2,1,0:T(8,128)(2,1)}, bf16[3,13,64,128]{3,2,1,0:T(8,128)(2,1)S(1)}, u32[]{:S(2)}, u32[]{:S(2)}) collective-permute-start(bf16[3,13,64,128]{3,2,1,0:T(8,128)(2,1)} %get-tuple-element.45), channel_id=1, source_target_pairs={{0,16},{8,24},{16,0},{24,8},{1,17},{9,25},{17,1},{25,9},{2,18},{10... | collective-permute-start | bytes 1916936 | tf_op jit(solution)/shard_map/ppermute | solution.py:549
  229.6 56.5 %collective-permute-start.12 = (bf16[3,13,64,128]{3,2,1,0:T(8,128)(2,1)}, bf16[3,13,64,128]{3,2,1,0:T(8,128)(2,1)S(1)}, u32[]{:S(2)}, u32[]{:S(2)}) collective-permute-start(bf16[3,13,64,128]{3,2,1,0:T(8,128)(2,1)} %get-tuple-element.46), channel_id=1, source_target_pairs={{0,24},{8,16},{16,8},{24,0},{1,25},{9,17},{17,9},{25,1},{2,26},{10... | collective-permute-start | bytes 1916936 | tf_op jit(solution)/shard_map/ppermute | solution.py:549
  230.1 66.6 %collective-permute-start.10 = (bf16[4,3,2,2,64,128]{5,4,3,2,1,0:T(8,128)(2,1)}, bf16[4,3,2,2,64,128]{5,4,3,2,1,0:T(8,128)(2,1)S(1)}, u32[]{:S(2)}, u32[]{:S(2)}) collective-permute-start(bf16[4,3,2,2,64,128]{5,4,3,2,1,0:T(8,128)(2,1)} %get-tuple-element.44), channel_id=1, source_target_pairs={{0,8},{8,0},{16,24},{24,16},{1,9},{9,1},{17,25},{25,17},{2,10},{10... | collective-permute-start | bytes 2359304 | tf_op jit(solution)/shard_map/ppermute | solution.py:549
  272.1 24.7 %copy-start.6 = (bf16[3,13,64,128]{3,2,1,0:T(8,128)(2,1)}, bf16[3,13,64,128]{3,2,1,0:T(8,128)(2,1)S(1)}, u32[]{:S(2)}) copy-start(bf16[3,13,64,128]{3,2,1,0:T(8,128)(2,1)S(1)} %collective-permute-done.11.refs_6_) | copy-start | bytes 1916932
  286.1 10.7 %copy-start.7 = (bf16[3,13,64,128]{3,2,1,0:T(8,128)(2,1)}, bf16[3,13,64,128]{3,2,1,0:T(8,128)(2,1)S(1)}, u32[]{:S(2)}) copy-start(bf16[3,13,64,128]{3,2,1,0:T(8,128)(2,1)S(1)} %collective-permute-done.12.refs_7_) | copy-start | bytes 1916932
  286.2 10.6 %collective-permute-start.13 = (bf16[2,4,2,64,128]{4,3,2,1,0:T(8,128)(2,1)S(1)}, bf16[2,4,2,64,128]{4,3,2,1,0:T(8,128)(2,1)S(1)}, u32[]{:S(2)}, u32[]{:S(2)}) collective-permute-start(bf16[2,4,2,64,128]{4,3,2,1,0:T(8,128)(2,1)S(1)} %pad_maximum_fusion.1), channel_id=1, source_target_pairs={{0,8},{8,0},{16,24},{24,16},{1,9},{9,1},{17,25},{25,17},{2,10},{10... | collective-permute-start | bytes 786440 | tf_op jit(solution)/shard_map/ppermute | solution.py:549
  288.3 20.5 %collective-permute-start.16 = (bf16[8,1,2,64,128]{4,3,2,0,1:T(8,128)(2,1)S(1)}, bf16[8,1,2,64,128]{4,3,2,0,1:T(8,128)(2,1)S(1)}, u32[]{:S(2)}, u32[]{:S(2)}) collective-permute-start(bf16[8,1,2,64,128]{4,3,2,0,1:T(8,128)(2,1)S(1)} %get-tuple-element.52), channel_id=1, source_target_pairs={{0,24},{8,16},{16,8},{24,0},{1,25},{9,17},{17,9},{25,1},{2,26},{10... | collective-permute-start | bytes 786440 | tf_op jit(solution)/shard_map/ppermute | solution.py:549
  289.9 22.2 %collective-permute-start.15 = (bf16[8,1,2,64,128]{4,3,2,0,1:T(8,128)(2,1)S(1)}, bf16[8,1,2,64,128]{4,3,2,0,1:T(8,128)(2,1)S(1)}, u32[]{:S(2)}, u32[]{:S(2)}) collective-permute-start(bf16[8,1,2,64,128]{4,3,2,0,1:T(8,128)(2,1)S(1)} %get-tuple-element.53), channel_id=1, source_target_pairs={{0,16},{8,24},{16,0},{24,8},{1,17},{9,25},{17,1},{25,9},{2,18},{10... | collective-permute-start | bytes 786440 | tf_op jit(solution)/shard_map/ppermute | solution.py:549
  292.6 19.5 %collective-permute-start.14 = (bf16[8,1,2,64,128]{4,3,2,0,1:T(8,128)(2,1)S(1)}, bf16[8,1,2,64,128]{4,3,2,0,1:T(8,128)(2,1)S(1)}, u32[]{:S(2)}, u32[]{:S(2)}) collective-permute-start(bf16[8,1,2,64,128]{4,3,2,0,1:T(8,128)(2,1)S(1)} %get-tuple-element.54), channel_id=1, source_target_pairs={{0,8},{8,0},{16,24},{24,16},{1,9},{9,1},{17,25},{25,17},{2,10},{10... | collective-permute-start | bytes 786440 | tf_op jit(solution)/shard_map/ppermute | solution.py:549
  313.0 77.1 %all-to-all-start.3 = ((bf16[8,4,4,2,64,128]{5,4,3,2,1,0:T(8,128)(2,1)}), bf16[8,4,4,2,64,128]{5,4,3,2,1,0:T(8,128)(2,1)}, u32[]{:S(2)}, u32[]{:S(2)}) async-start(bf16[8,4,4,2,64,128]{5,4,3,2,1,0:T(8,128)(2,1)} %shard_map.80), calls=%async_computation.3 | async-start | bytes 8388608 | tf_op jit(solution)/shard_map/all_to_all | solution.py:553
  317.7 36.2 %collective-permute-start.17 = (bf16[8,3,2,64,128]{4,3,2,1,0:T(8,128)(2,1)}, bf16[8,3,2,64,128]{4,3,2,1,0:T(8,128)(2,1)S(1)}, u32[]{:S(2)}, u32[]{:S(2)}) collective-permute-start(bf16[8,3,2,64,128]{4,3,2,1,0:T(8,128)(2,1)} %get-tuple-element.48), channel_id=1, source_target_pairs={{0,8},{8,0},{16,24},{24,16},{1,9},{9,1},{17,25},{25,17},{2,10},{10... | collective-permute-start | bytes 2359304 | tf_op jit(solution)/shard_map/ppermute | solution.py:549
  320.1 53.0 %collective-permute-start.18 = (bf16[8,3,2,64,128]{4,3,2,1,0:T(8,128)(2,1)}, bf16[8,3,2,64,128]{4,3,2,1,0:T(8,128)(2,1)S(1)}, u32[]{:S(2)}, u32[]{:S(2)}) collective-permute-start(bf16[8,3,2,64,128]{4,3,2,1,0:T(8,128)(2,1)} %get-tuple-element.49), channel_id=1, source_target_pairs={{0,16},{8,24},{16,0},{24,8},{1,17},{9,25},{17,1},{25,9},{2,18},{10... | collective-permute-start | bytes 2359304 | tf_op jit(solution)/shard_map/ppermute | solution.py:549
  321.1 69.0 %collective-permute-start.19 = (bf16[8,3,2,64,128]{4,3,2,1,0:T(8,128)(2,1)}, bf16[8,3,2,64,128]{4,3,2,1,0:T(8,128)(2,1)S(1)}, u32[]{:S(2)}, u32[]{:S(2)}) collective-permute-start(bf16[8,3,2,64,128]{4,3,2,1,0:T(8,128)(2,1)} %get-tuple-element.50), channel_id=1, source_target_pairs={{0,24},{8,16},{16,8},{24,0},{1,25},{9,17},{17,9},{25,1},{2,26},{10... | collective-permute-start | bytes 2359304 | tf_op jit(solution)/shard_map/ppermute | solution.py:549
  353.9 36.2 %copy-start.8 = (bf16[8,3,2,64,128]{4,3,2,1,0:T(8,128)(2,1)}, bf16[8,3,2,64,128]{4,3,2,1,0:T(8,128)(2,1)S(1)}, u32[]{:S(2)}) copy-start(bf16[8,3,2,64,128]{4,3,2,1,0:T(8,128)(2,1)S(1)} %collective-permute-done.17) | copy-start | bytes 2359300
  373.1 17.0 %copy-start.9 = (bf16[8,3,2,64,128]{4,3,2,1,0:T(8,128)(2,1)}, bf16[8,3,2,64,128]{4,3,2,1,0:T(8,128)(2,1)S(1)}, u32[]{:S(2)}) copy-start(bf16[8,3,2,64,128]{4,3,2,1,0:T(8,128)(2,1)S(1)} %collective-permute-done.18) | copy-start | bytes 2359300
  (13 other events, 30.9 us)

commit v3 on v2

--- a/solution.py
+++ b/solution.py
@@ -100,6 +100,7 @@
 TN = (((0,), (0,)), ((), ()))
 VMEM_LIMIT = 56 * 2**20
 ROWS = 16
+BATCH = 4
 WIDE = jnp.float32
 NARROW = jnp.bfloat16
 IN_VMEM = pl.BlockSpec(memory_space=pltpu.VMEM)
@@ -158,11 +159,12 @@
                 [records_ref[s, p + d] for d in range(2) for s in range(2)], axis=0
             )
             found = lax.dot_general(table[...], traces, NT, preferred_element_type=WIDE)
+            found = found.astype(NARROW)
             turned[p] = found[:, :width]
             turned[p + 1] = found[:, width:]
         at = 0
         for out_ref, size in zip(out_refs, sizes):
-            out_ref[...] = jnp.swapaxes(turned[:, at:at + size, :], 0, 1).astype(NARROW)
+            out_ref[...] = jnp.swapaxes(turned[:, at:at + size, :], 0, 1)
             at += size
 
     return pl.pallas_call(
@@ -174,7 +176,7 @@
         out_specs=[pl.BlockSpec((size, ROWS, width), lambda i: (0, i, 0)) for size in sizes],
         out_shape=[shaped(size, half, width) for size in sizes],
         scratch_shapes=[
-            pltpu.VMEM((ROWS, rows, width), WIDE),
+            pltpu.VMEM((ROWS, rows, width), NARROW),
             pltpu.VMEM((rows, samples), NARROW),
         ],
         compiler_params=params(),
@@ -207,14 +209,16 @@
 
         at = 0
         for ref, size in zip(spectra_refs, sizes):
-            turned[:, at:at + size, :] = jnp.swapaxes(ref[...].astype(WIDE), 0, 1)
+            turned[:, at:at + size, :] = jnp.swapaxes(ref[...], 0, 1)
             at += size
-        for p in range(ROWS):
+        for p in range(0, ROWS, BATCH):
+            columns = [turned[p + q] for q in range(BATCH)]
             traces = lax.dot_general(
-                turned[p].astype(NARROW), table[...], TN, preferred_element_type=WIDE
+                jnp.concatenate(columns, axis=1), table[...], TN, preferred_element_type=WIDE
             ).astype(out_ref.dtype)
-            out_ref[0, p] = traces[:receivers]
-            out_ref[1, p] = traces[receivers:]
+            for q in range(BATCH):
+                out_ref[0, p + q] = traces[q * width:q * width + receivers]
+                out_ref[1, p + q] = traces[q * width + receivers:(q + 1) * width]
 
     return pl.pallas_call(
         kernel,
@@ -225,7 +229,7 @@
         out_specs=pl.BlockSpec((2, ROWS, receivers, samples), lambda i: (0, i, 0, 0)),
         out_shape=shaped(2, half, receivers, samples),
         scratch_shapes=[
-            pltpu.VMEM((ROWS, rows, width), WIDE),
+            pltpu.VMEM((ROWS, rows, width), NARROW),
             pltpu.VMEM((rows, samples), NARROW),
         ],
         compiler_params=params(),
@@ -253,18 +257,38 @@
     return lax.broadcasted_iota(jnp.int32, (rows, lanes), 1) < lanes // 2
 
 
+def places(half):
+    shape = (half, 2 * half)
+    rows = lax.broadcasted_iota(jnp.int32, shape, 0)
+    lanes = lax.broadcasted_iota(jnp.int32, shape, 1)
+    left = lanes < half
+    return rows, jnp.where(left, lanes, lanes - half), left
+
+
 def pack_diagonals(real, imag):
-    half, size = real.shape[0] // 2, real.shape[0]
-    last = jnp.where(left_half(half, size), pltpu.roll(real[half:], half, 1), imag[half:])
-    return real[:half], imag[:half], last
-
-
-def unpack_diagonal(top, last, c):
-    half, size = top.shape
+    half = real.shape[0] // 2
+    rows, lanes, left = places(half)
+    packed, diagonals = [], []
+    for block in (real, imag):
+        lower = pltpu.roll(block[half:], half, 1)
+        packed.append(jnp.where(left & (rows > lanes), lower, block[:half]))
+        diagonals.append(jnp.where(rows == lanes, block[half:], 0.0))
+    both = jnp.where(left, pltpu.roll(diagonals[0], half, 1), diagonals[1])
+    both = jnp.sum(both, axis=0, keepdims=True)
+    return packed[0], packed[1], jnp.broadcast_to(both, (ROWS, 2 * half))
+
+
+def unpack_diagonal(packed, diagonals, c):
+    half, size = packed.shape
+    rows, lanes, left = places(half)
+    mirrored = jnp.concatenate([packed, packed], axis=0).T
+    diagonal = diagonals[:1]
     if c == 0:
-        last = pltpu.roll(last, half, 1)
-    mirrored = jnp.concatenate([top, top], axis=0).T
-    return jnp.concatenate([top, jnp.where(left_half(half, size), mirrored[half:], last)], axis=0)
+        diagonal = pltpu.roll(jnp.broadcast_to(diagonal, (8, size)), half, 1)[:1]
+    top = jnp.where(left & (rows > lanes), mirrored[:half], packed)
+    last = jnp.where(rows > lanes, pltpu.roll(packed, half, 1), mirrored[:half])
+    last = jnp.where(rows == lanes, diagonal, last)
+    return jnp.concatenate([top, jnp.where(left, mirrored[half:], last)], axis=0)
 
 
 def square(ref, *at):
@@ -307,16 +331,21 @@
                 )
 
 
-def far_units(n):
-    pair = 4 * (n - 2)
-    return pair, pair + 2, pair + 5
+def far_rows(n, tile):
+    pair = 2 * (n - 2) * tile
+    return pair, pair + tile, pair + 2 * tile, pair + 2 * tile + ROWS
+
+
+def other_rows(block, c, tile):
+    at = (2 * (block - 2) + c) * tile
+    return slice(at, at + tile)
 
 
 def predict(place, coeff, moved, n, direct_in, direct_out, start, stop, after):
     freqs = stop - start
     half, tile = moved[0].shape[-2:]
     order = n * tile
-    pair_at, diagonal_at, units = far_units(n)
+    pair_at, diagonal_at, last_at, length = far_rows(n, tile)
 
     def kernel(place_ref, coeff_ref, after_ref, *refs):
         count = 1 if direct_in else n
@@ -331,17 +360,18 @@
                 return square(moved_refs[0], pl.ds((j ^ me) * 2, 2), i, 0, c)
             if i < 2:
                 return square(moved_refs[i], i ^ j, 0, c)
-            return square(moved_refs[i], 0, pl.ds(((i ^ j) - 2) * 4 + 2 * c, 2))
+            return moved_refs[i][0, other_rows(i ^ j, c, tile)].astype(WIDE)
 
         def mean(c, a, b):
             if direct_in or a < 2 or (a ^ b) >= 2:
                 return 0.5 * (stacked(c, a, b) + stacked(c, b, a).T)
             if a == b:
                 ref = moved_refs[a]
-                top = ref[0, diagonal_at + c].astype(WIDE)
-                return unpack_diagonal(top, ref[0, diagonal_at + 2].astype(WIDE), c)
-            here = square(moved_refs[a], 0, pl.ds(pair_at, 2))
-            there = square(moved_refs[b], 0, pl.ds(pair_at, 2)).T
+                packed = ref[0, diagonal_at + c * half:diagonal_at + (c + 1) * half]
+                diagonals = ref[0, last_at:length]
+                return unpack_diagonal(packed.astype(WIDE), diagonals.astype(WIDE), c)
+            here = moved_refs[a][0, pair_at:pair_at + tile].astype(WIDE)
+            there = moved_refs[b][0, pair_at:pair_at + tile].astype(WIDE).T
             return jnp.where(odd == (c == 0), here, there)
 
         for c in range(2):
@@ -357,30 +387,32 @@
             gap = a ^ b
             if not direct_out and a >= 2 and gap == 1:
                 own = jnp.where(odd == (a % 2 == 0), imag, real).astype(NARROW)
-                out_refs[a][0, pair_at] = own[:half]
-                out_refs[a][0, pair_at + 1] = own[half:]
+                out_refs[a][0, pair_at:pair_at + tile] = own
                 return
             if not direct_out and a >= 2 and gap == 0:
-                for unit, value in enumerate(pack_diagonals(real, imag)):
-                    out_refs[a][0, diagonal_at + unit] = value.astype(NARROW)
+                at = diagonal_at
+                for value in pack_diagonals(real, imag):
+                    out_refs[a][0, at:at + value.shape[0]] = value.astype(NARROW)
+                    at += value.shape[0]
                 return
             for c, value in enumerate((real, imag)):
                 value = value.astype(NARROW)
+                if not direct_out and a >= 2:
+                    out_refs[a][0, other_rows(gap, c, tile)] = value
+                    continue
                 for h in range(2):
                     part = value[h * half:(h + 1) * half]
                     if direct_out:
                         out_refs[0][(b ^ me) * 2 + h, a, 0, c] = part
-                    elif a < 2:
+                    else:
                         out_refs[a][gap, 0, c, h] = part
-                    else:
-                        out_refs[a][0, (gap - 2) * 4 + 2 * c + h] = part
 
         index = pl.program_id(0) + start
         series(coeff_ref[index, 0], coeff_ref[index, 1], recip, first, out_block, tile)
 
     whole = (2 * n, n, freqs, 2, half, tile)
     close = (n, freqs, 2, 2, half, tile)
-    far = (freqs, units, half, tile)
+    far = (freqs, length, tile)
     split_shapes = [shaped(*close)] * 2 + [shaped(*far)] * (n - 2)
 
     def specs(direct, first):
@@ -388,7 +420,7 @@
             block = (2 * n, n, 1, 2, half, tile)
             return [pl.BlockSpec(block, lambda i: (0, 0, i + first, 0, 0, 0))]
         close = pl.BlockSpec((n, 1, 2, 2, half, tile), lambda i: (0, i + first, 0, 0, 0, 0))
-        far = pl.BlockSpec((1, units, half, tile), lambda i: (i + first, 0, 0, 0))
+        far = pl.BlockSpec((1, length, tile), lambda i: (i + first, 0, 0))
         return [close] * 2 + [far] * (n - 2)
 
     return pl.pallas_call(
@@ -405,7 +437,7 @@
 
 def gather_rows(place, moved, pairs, n, after):
     _, _, freqs, _, half, tile = moved.shape
-    pair_at, diagonal_at, units = far_units(n)
+    pair_at, diagonal_at, last_at, length = far_rows(n, tile)
 
     def kernel(place_ref, after_ref, moved_ref, pairs_ref, *out_refs):
         me = place_ref[0]
@@ -423,21 +455,22 @@
             for f in range(freqs):
                 for block in range(2, n):
                     for c in range(2):
-                        at = (block - 2) * 4 + 2 * c
-                        out_refs[d][f, at:at + 2] = moved_ref[halves(block), me ^ d, f, c]
+                        rows = moved_ref[halves(block), me ^ d, f, c].reshape(tile, tile)
+                        out_refs[d][f, other_rows(block, c, tile)] = rows
                 here = square(moved_ref, halves(1), me ^ d, f, mine)
                 there = square(pairs_ref, (d ^ 1) - 2, slice(None), f)
                 mean = (0.5 * (here + there.T)).astype(NARROW)
-                out_refs[d][f, pair_at] = mean[:half]
-                out_refs[d][f, pair_at + 1] = mean[half:]
+                out_refs[d][f, pair_at:pair_at + tile] = mean
                 means = []
                 for c in range(2):
                     block = square(moved_ref, halves(0), me ^ d, f, c)
                     means.append(0.5 * (block + block.T))
-                for unit, value in enumerate(pack_diagonals(*means)):
-                    out_refs[d][f, diagonal_at + unit] = value.astype(NARROW)
-
-    close, far = shaped(n, freqs, 2, 2, half, tile), shaped(freqs, units, half, tile)
+                at = diagonal_at
+                for value in pack_diagonals(*means):
+                    out_refs[d][f, at:at + value.shape[0]] = value.astype(NARROW)
+                    at += value.shape[0]
+
+    close, far = shaped(n, freqs, 2, 2, half, tile), shaped(freqs, length, tile)
     return pl.pallas_call(
         kernel,
         in_specs=[IN_SMEM, UNREAD] + [IN_VMEM] * 2,
@@ -449,10 +482,11 @@
 
 
 def scatter_rows(place, groups, pairs, n, after):
-    half, tile = pairs.shape[-2:]
+    tile = pairs.shape[-1]
+    half = tile // 2
     counts = [rows[0].shape[1] for rows in groups]
     freqs = sum(counts)
-    pair_at, diagonal_at, units = far_units(n)
+    pair_at, diagonal_at, last_at, length = far_rows(n, tile)
 
     def kernel(place_ref, after_ref, *refs):
         pairs_ref, out_ref = refs[-2:]
@@ -474,13 +508,13 @@
                 return
             for block in range(2, n):
                 for c in range(2):
-                    at = (block - 2) * 4 + 2 * c
-                    put(block, d, f, c, square(ref, own, pl.ds(at, 2)))
-            put(1, d, f, mine, square(ref, own, pl.ds(pair_at, 2)))
-            put(1, d, f, 1 - mine, square(pairs_ref, (d ^ 1) - 2, f).T)
-            last = ref[own, diagonal_at + 2].astype(WIDE)
+                    put(block, d, f, c, ref[own, other_rows(block, c, tile)])
+            put(1, d, f, mine, ref[own, pair_at:pair_at + tile])
+            put(1, d, f, 1 - mine, pairs_ref[(d ^ 1) - 2, f].astype(WIDE).T)
+            last = ref[own, last_at:length].astype(WIDE)
             for c in range(2):
-                put(0, d, f, c, unpack_diagonal(ref[own, diagonal_at + c].astype(WIDE), last, c))
+                packed = ref[own, diagonal_at + c * half:diagonal_at + (c + 1) * half]
+                put(0, d, f, c, unpack_diagonal(packed.astype(WIDE), last, c))
 
         f = 0
         for group, count in enumerate(counts):
@@ -602,10 +636,10 @@
         return gather_rows(place, moved, pair_of(moved, q), n, after)
 
     def pairs_of(groups):
-        pair_at = far_units(n)[0]
+        pair_at = far_rows(n, src_tiles)[0]
         return jnp.stack(
             [
-                jnp.concatenate([rows[d][:, pair_at:pair_at + 2] for rows in groups])
+                jnp.concatenate([rows[d][:, pair_at:pair_at + src_tiles] for rows in groups])
                 for d in range(2, n)
             ]
         )

time: 403 us -> 396 us (0.983)
  waiting for transfers between devices: 273 us -> 258 us
  starting transfers between devices: 42.8 us -> 52.3 us
    ppermute x20, waiting for transfers between devices: 185 us -> 170 us  [swapped(): return lax.ppermute(value, 'src', [(i, i ^ gap) for i in range(size)])]
    all_to_all x4, starting transfers between devices: 19.5 us -> 28.1 us  [spread(): return lax.all_to_all(value, 'rcv', split_axis=0, concat_axis=0, tiled=True)]
  transfers between devices with their start and end apart: 24 -> 24, of which waited for: 12 -> 12; matrix products, arithmetic and copies ran while one was open for 1% -> 1% of each run, Pallas kernels for 12% -> 13%
where the time goes in v3:
time: 396 us; the launch traced here: 395 us
  waiting for transfers between devices  258 us (65%)
  Pallas kernels  73.5 us (19%)
  starting transfers between devices  52.3 us (13%)
  local copies, waits for them, and re-layouts  9.75 us (2%)
    ppermute x20, waiting for transfers between devices, swapped(): return lax.ppermute(value, 'src', [(i, i ^ gap) for i in range(size)])  170 us
    all_to_all x4, waiting for transfers between devices, spread(): return lax.all_to_all(value, 'rcv', split_axis=0, concat_axis=0, tiled=True)  87.8 us
    pallas_call x3, Pallas kernels, predict(): pl.pallas_call(kernel, grid=(freqs,), in_specs=[IN_SMEM, IN_SMEM, UNREAD]...  35.9 us
    all_to_all x4, starting transfers between devices, spread(): return lax.all_to_all(value, 'rcv', split_axis=0, concat_axis=0, tiled=True)  28.1 us
    ppermute x20, starting transfers between devices, swapped(): return lax.ppermute(value, 'src', [(i, i ^ gap) for i in range(size)])  24.3 us
    pallas_call x1, Pallas kernels, inverse_dft(): pl.pallas_call(kernel, grid=(half // ROWS,), in_specs=[IN_SMEM] + [pl.Blo...  10.2 us
    pallas_call x1, Pallas kernels, forward_dft(): pl.pallas_call(kernel, grid=(half // ROWS,), in_specs=[IN_SMEM, UNREAD] +...  9.49 us
  transfers between devices with their start and end apart: 24, of which 12 were waited for; matrix products, arithmetic and copies ran while one was open for 1% of the time, Pallas kernels for 13%

profile of v3, /device:TPU:10, one launch (start us, length us, event | category | flops | bytes accessed | tf_op | source)
XLA Modules:
  0.0 394.9 jit_solution(17921262645092567595)
XLA Ops:
  0.0 9.5 %shard_map.73 = (bf16[64,64,128]{2,1,0:T(8,128)(2,1)}, bf16[64,64,128]{2,1,0:T(8,128)(2,1)}, bf16[64,64,128]{2,1,0:T(8,128)(2,1)}, bf16[64,64,128]{2,1,0:T(8,128)(2,1)}, bf16[256,64,128]{2,1,0:T(8,128)(2,1)}) custom-call(s32[1]{0:T(128)} %bitcast.place_ref.after_ref, s32[1]{0:T(128)} %bitcast.place_ref.after_ref, ...), custom_call_target="tpu_custom_call" | custom-call | tf_op jit(solution)/shard_map/pallas_call | solution.py:170
  9.5 5.0 %all-to-all-start = ((bf16[8,4,4,2,64,128]{5,4,3,2,1,0:T(8,128)(2,1)}), bf16[8,4,4,2,64,128]{5,4,3,2,1,0:T(8,128)(2,1)}, u32[]{:S(2)}, u32[]{:S(2)}) async-start(bf16[8,4,4,2,64,128]{5,4,3,2,1,0:T(8,128)(2,1)} %bitcast.32), calls=%async_computation | async-start | bytes 8388608 | tf_op jit(solution)/shard_map/all_to_all | solution.py:587
  14.5 3.0 collective-permute-start.2
  18.0 44.2 %all-to-all-done.moved_ref = bf16[8,4,4,2,64,128]{5,4,3,2,1,0:T(8,128)(2,1)} async-done(((bf16[8,4,4,2,64,128]{5,4,3,2,1,0:T(8,128)(2,1)}), bf16[8,4,4,2,64,128]{5,4,3,2,1,0:T(8,128)(2,1)}, u32[]{:S(2)}, u32[]{:S(2)}) %all-to-all-start) | async-done | bytes 4194336 | tf_op jit(solution)/shard_map/all_to_all | solution.py:587
  63.3 27.9 %collective-permute-done.pairs_ref = bf16[2,2,4,64,128]{4,3,2,1,0:T(8,128)(2,1)S(1)} collective-permute-done((bf16[2,2,4,64,128]{4,3,2,1,0:T(8,128)(2,1)S(1)}, bf16[2,2,4,64,128]{4,3,2,1,0:T(8,128)(2,1)S(1)}, u32[]{:S(2)}, u32[]{:S(2)}) %collective-permute-start) | collective-permute-done | bytes 262176 | tf_op jit(solution)/shard_map/ppermute | solution.py:583
  91.9 4.6 %shard_map.74 = (bf16[4,4,2,2,64,128]{5,4,3,2,1,0:T(8,128)(2,1)}, bf16[4,4,2,2,64,128]{5,4,3,2,1,0:T(8,128)(2,1)}, bf16[4,784,128]{2,1,0:T(8,128)(2,1)}, bf16[4,784,128]{2,1,0:T(8,128)(2,1)}) custom-call(s32[1]{0:T(128)} %bitcast.place_ref.after_ref, s32[1]{0:T(128)} %bitcast.place_ref.after_ref, bf16[8,4,4,2,64,128]{5,4,3,2,1,0:T(8,128)(2,1)} %all-to-all-done.moved_ref, ...), custom_call_target="tpu_custom_call" | custom-call | tf_op jit(solution)/shard_map/pallas_call | solution.py:474
  96.5 12.1 %collective-permute-done.3 = bf16[64,64,128]{2,1,0:T(8,128)(2,1)S(1)} collective-permute-done((bf16[64,64,128]{2,1,0:T(8,128)(2,1)}, bf16[64,64,128]{2,1,0:T(8,128)(2,1)S(1)}, u32[]{:S(2)}, u32[]{:S(2)}) %collective-permute-start.3) | collective-permute-done | bytes 1048608 | tf_op jit(solution)/shard_map/ppermute | solution.py:583
  109.6 4.5 %shard_map.75 = bf16[8,4,4,2,64,128]{5,4,3,2,1,0:T(8,128)(2,1)} custom-call(bf16[4,4,2,2,64,128]{5,4,3,2,1,0:T(8,128)(2,1)} %get-tuple-element.29.after_ref.refs_0_, bf16[8,4,2,64,128]{4,3,2,1,0:T(8,128)(2,1)} %bitcast.35, bf16[8,4,2,64,128]{4,3,2,1,0:T(8,128)(2,1)} %bitcast.36, bf16[8,4,2,64,128]{4,3,2,1,0:T(8,128)(2,1)} %bitcast.37, ...), custom_call_target="tpu_custom_call" | custom-call | tf_op jit(solution)/shard_map/pallas_call | solution.py:545
  114.0 4.9 %all-to-all-start.1 = ((bf16[8,4,4,2,64,128]{5,4,3,2,1,0:T(8,128)(2,1)}), bf16[8,4,4,2,64,128]{5,4,3,2,1,0:T(8,128)(2,1)}, u32[]{:S(2)}, u32[]{:S(2)}) async-start(bf16[8,4,4,2,64,128]{5,4,3,2,1,0:T(8,128)(2,1)} %shard_map.75), calls=%async_computation.1 | async-start | bytes 8388608 | tf_op jit(solution)/shard_map/all_to_all | solution.py:587
  119.0 3.0 collective-permute-start.5
  123.2 43.5 %all-to-all-done.1.refs_0_ = bf16[8,4,4,2,64,128]{5,4,3,2,1,0:T(8,128)(2,1)} async-done(((bf16[8,4,4,2,64,128]{5,4,3,2,1,0:T(8,128)(2,1)}), bf16[8,4,4,2,64,128]{5,4,3,2,1,0:T(8,128)(2,1)}, u32[]{:S(2)}, u32[]{:S(2)}) %all-to-all-start.1) | async-done | bytes 4194336 | tf_op jit(solution)/shard_map/all_to_all | solution.py:587
  166.7 13.2 %shard_map.76 = (bf16[4,3,2,2,64,128]{5,4,3,2,1,0:T(8,128)(2,1)}, bf16[4,3,2,2,64,128]{5,4,3,2,1,0:T(8,128)(2,1)}, bf16[3,784,128]{2,1,0:T(8,128)(2,1)}, bf16[3,784,128]{2,1,0:T(8,128)(2,1)}) custom-call(s32[1]{0:T(128)} %bitcast.place_ref.after_ref, f32[4,2]{1,0:T(4,128)} %broadcast_multiply_fusion.coeff_ref, ...), custom_call_target="tpu_custom_call" | custom-call | tf_op jit(solution)/shard_map/pallas_call | solution.py:426
  179.9 5.6 %shard_map.77 = (bf16[4,1,2,2,64,128]{5,4,3,2,1,0:T(8,128)(2,1)}, bf16[4,1,2,2,64,128]{5,4,3,2,1,0:T(8,128)(2,1)}, bf16[1,784,128]{2,1,0:T(8,128)(2,1)}, bf16[1,784,128]{2,1,0:T(8,128)(2,1)}) custom-call(s32[1]{0:T(128)} %bitcast.place_ref.after_ref, f32[4,2]{1,0:T(4,128)} %broadcast_multiply_fusion.coeff_ref, ...), custom_call_target="tpu_custom_call" | custom-call | tf_op jit(solution)/shard_map/pallas_call | solution.py:426
  185.6 3.0 collective-permute-start.8
  189.7 3.4 collective-permute-done.6.refs_3_
  194.3 17.1 %shard_map.78 = bf16[8,4,4,2,64,128]{5,4,3,2,1,0:T(8,128)(2,1)} custom-call(s32[1]{0:T(128)} %bitcast.place_ref.after_ref, f32[4,2]{1,0:T(4,128)} %broadcast_multiply_fusion.1.coeff_ref, bf16[4,1,2,2,64,128]{5,4,3,2,1,0:T(8,128)(2,1)} %get-tuple-element.35.after_ref.refs_0_, bf16[4,4,2,2,64,128]{5,4,3,2,1,0:T(8,128)(2,1)} %get-tuple-element.29.after_ref.refs_0_, ...), custom_call_target="tpu_custom_call" | custom-call | tf_op jit(solution)/shard_map/pallas_call | solution.py:426
  212.1 13.4 %all-to-all-start.2 = ((bf16[8,4,4,2,64,128]{5,4,3,2,1,0:T(8,128)(2,1)}), bf16[8,4,4,2,64,128]{5,4,3,2,1,0:T(8,128)(2,1)}, u32[]{:S(2)}, u32[]{:S(2)}) async-start(bf16[8,4,4,2,64,128]{5,4,3,2,1,0:T(8,128)(2,1)} %shard_map.78), calls=%async_computation.2 | async-start | bytes 8388608 | tf_op jit(solution)/shard_map/all_to_all | solution.py:587
  227.1 2.8 collective-permute-start.10
  230.0 35.7 %collective-permute-done.11.refs_6_ = bf16[3,784,128]{2,1,0:T(8,128)(2,1)S(1)} collective-permute-done((bf16[3,784,128]{2,1,0:T(8,128)(2,1)}, bf16[3,784,128]{2,1,0:T(8,128)(2,1)S(1)}, u32[]{:S(2)}, u32[]{:S(2)}) %collective-permute-start.11) | collective-permute-done | bytes 602144 | tf_op jit(solution)/shard_map/ppermute | solution.py:583
  265.7 14.3 %collective-permute-done.12.refs_7_ = bf16[3,784,128]{2,1,0:T(8,128)(2,1)S(1)} collective-permute-done((bf16[3,784,128]{2,1,0:T(8,128)(2,1)}, bf16[3,784,128]{2,1,0:T(8,128)(2,1)S(1)}, u32[]{:S(2)}, u32[]{:S(2)}) %collective-permute-start.12) | collective-permute-done | bytes 602144 | tf_op jit(solution)/shard_map/ppermute | solution.py:583
  280.2 2.1 fusion
  282.7 3.9 collective-permute-start.15
  286.5 4.0 %shard_map.79 = (bf16[8,3,2,64,128]{4,3,2,1,0:T(8,128)(2,1)}, bf16[8,3,2,64,128]{4,3,2,1,0:T(8,128)(2,1)}, bf16[8,3,2,64,128]{4,3,2,1,0:T(8,128)(2,1)}, bf16[8,3,2,64,128]{4,3,2,1,0:T(8,128)(2,1)}) custom-call(bf16[8,4,4,2,64,128]{5,4,3,2,1,0:T(8,128)(2,1)} %all-to-all-done.2.moved_ref), custom_call_target="tpu_custom_call" | custom-call | tf_op jit(solution)/shard_map/pallas_call | solution.py:563
  291.5 5.0 %shard_map.80 = bf16[8,4,4,2,64,128]{5,4,3,2,1,0:T(8,128)(2,1)} custom-call(s32[1]{0:T(128)} %bitcast.place_ref.after_ref, bf16[8,3,2,64,128]{4,3,2,1,0:T(8,128)(2,1)} %get-tuple-element.43.after_ref, bf16[4,1,2,2,64,128]{5,4,3,2,1,0:T(8,128)(2,1)} %get-tuple-element.35.after_ref.refs_0_, bf16[4,1,2,2,64,128]{5,4,3,2,1,0:T(8,128)(2,1)} %copy-done.17, ...), custom_call_target="tpu_custom_call" | custom-call | tf_op jit(solution)/shard_map/pallas_call | solution.py:527
  296.5 6.2 %collective-permute-done.16 = bf16[8,1,2,64,128]{4,3,2,0,1:T(8,128)(2,1)S(1)} collective-permute-done((bf16[8,1,2,64,128]{4,3,2,0,1:T(8,128)(2,1)S(1)}, bf16[8,1,2,64,128]{4,3,2,0,1:T(8,128)(2,1)S(1)}, u32[]{:S(2)}, u32[]{:S(2)}) %collective-permute-start.16) | collective-permute-done | bytes 262176 | tf_op jit(solution)/shard_map/ppermute | solution.py:583
  302.7 2.2 collective-permute-done.15
  305.7 4.7 %all-to-all-start.3 = ((bf16[8,4,4,2,64,128]{5,4,3,2,1,0:T(8,128)(2,1)}), bf16[8,4,4,2,64,128]{5,4,3,2,1,0:T(8,128)(2,1)}, u32[]{:S(2)}, u32[]{:S(2)}) async-start(bf16[8,4,4,2,64,128]{5,4,3,2,1,0:T(8,128)(2,1)} %shard_map.80), calls=%async_computation.3 | async-start | bytes 8388608 | tf_op jit(solution)/shard_map/all_to_all | solution.py:587
  310.5 3.5 collective-permute-start.17
  315.4 31.6 %collective-permute-done.17 = bf16[8,3,2,64,128]{4,3,2,1,0:T(8,128)(2,1)S(1)} collective-permute-done((bf16[8,3,2,64,128]{4,3,2,1,0:T(8,128)(2,1)}, bf16[8,3,2,64,128]{4,3,2,1,0:T(8,128)(2,1)S(1)}, u32[]{:S(2)}, u32[]{:S(2)}) %collective-permute-start.17) | collective-permute-done | bytes 786464 | tf_op jit(solution)/shard_map/ppermute | solution.py:583
  347.0 18.9 %collective-permute-done.18 = bf16[8,3,2,64,128]{4,3,2,1,0:T(8,128)(2,1)S(1)} collective-permute-done((bf16[8,3,2,64,128]{4,3,2,1,0:T(8,128)(2,1)}, bf16[8,3,2,64,128]{4,3,2,1,0:T(8,128)(2,1)S(1)}, u32[]{:S(2)}, u32[]{:S(2)}) %collective-permute-start.18) | collective-permute-done | bytes 786464 | tf_op jit(solution)/shard_map/ppermute | solution.py:583
  366.0 17.9 %collective-permute-done.19 = bf16[8,3,2,64,128]{4,3,2,1,0:T(8,128)(2,1)S(1)} collective-permute-done((bf16[8,3,2,64,128]{4,3,2,1,0:T(8,128)(2,1)}, bf16[8,3,2,64,128]{4,3,2,1,0:T(8,128)(2,1)S(1)}, u32[]{:S(2)}, u32[]{:S(2)}) %collective-permute-start.19) | collective-permute-done | bytes 786464 | tf_op jit(solution)/shard_map/ppermute | solution.py:583
  384.7 10.2 %shard_map.81 = bf16[2,64,64,512]{3,2,1,0:T(8,128)(2,1)} custom-call(s32[1]{0:T(128)} %bitcast.place_ref.after_ref, bf16[1,256,512]{2,1,0:T(8,128)(2,1)} %constant.52.clone.refs_0_, bf16[4,16,512]{2,1,0:T(8,128)(2,1)} %constant.53.clone.refs_1_, bf16[4,48,512]{2,1,0:T(8,128)(2,1)} %constant.54.clone.refs_2_, bf16[256,64,128]{2,1,0:T(8,128)(2,1)} %bitcast.14.refs_3_, ...), custom_call_target="tpu_custom_call" | custom-call | tf_op jit(solution)/shard_map/pallas_call | solution.py:223
  (82 shorter events, 13.9 us)
Async XLA Ops:
  9.5 52.7 %all-to-all-start = ((bf16[8,4,4,2,64,128]{5,4,3,2,1,0:T(8,128)(2,1)}), bf16[8,4,4,2,64,128]{5,4,3,2,1,0:T(8,128)(2,1)}, u32[]{:S(2)}, u32[]{:S(2)}) async-start(bf16[8,4,4,2,64,128]{5,4,3,2,1,0:T(8,128)(2,1)} %bitcast.32), calls=%async_computation | async-start | bytes 8388608 | tf_op jit(solution)/shard_map/all_to_all | solution.py:587
  14.5 82.0 %collective-permute-start.1 = (bf16[64,64,128]{2,1,0:T(8,128)(2,1)}, bf16[64,64,128]{2,1,0:T(8,128)(2,1)S(1)}, u32[]{:S(2)}, u32[]{:S(2)}) collective-permute-start(bf16[64,64,128]{2,1,0:T(8,128)(2,1)} %get-tuple-element.31), channel_id=1, source_target_pairs={{0,8},{8,0},{16,24},{24,16},{1,9},{9,1},{17,25},{25,17},{2,10},{10... | collective-permute-start | bytes 3145736 | tf_op jit(solution)/shard_map/ppermute | solution.py:583
  14.5 81.9 %collective-permute-start.2 = (bf16[64,64,128]{2,1,0:T(8,128)(2,1)}, bf16[64,64,128]{2,1,0:T(8,128)(2,1)S(1)}, u32[]{:S(2)}, u32[]{:S(2)}) collective-permute-start(bf16[64,64,128]{2,1,0:T(8,128)(2,1)} %get-tuple-element.32), channel_id=1, source_target_pairs={{0,16},{8,24},{16,0},{24,8},{1,17},{9,25},{17,1},{25,9},{2,18},{10... | collective-permute-start | bytes 3145736 | tf_op jit(solution)/shard_map/ppermute | solution.py:583
  17.5 91.1 %collective-permute-start.3 = (bf16[64,64,128]{2,1,0:T(8,128)(2,1)}, bf16[64,64,128]{2,1,0:T(8,128)(2,1)S(1)}, u32[]{:S(2)}, u32[]{:S(2)}) collective-permute-start(bf16[64,64,128]{2,1,0:T(8,128)(2,1)} %get-tuple-element.33), channel_id=1, source_target_pairs={{0,24},{8,16},{16,8},{24,0},{1,25},{9,17},{17,9},{25,1},{2,26},{10... | collective-permute-start | bytes 3145736 | tf_op jit(solution)/shard_map/ppermute | solution.py:583
  63.2 27.9 %collective-permute-start = (bf16[2,2,4,64,128]{4,3,2,1,0:T(8,128)(2,1)S(1)}, bf16[2,2,4,64,128]{4,3,2,1,0:T(8,128)(2,1)S(1)}, u32[]{:S(2)}, u32[]{:S(2)}) collective-permute-start(bf16[2,2,4,64,128]{4,3,2,1,0:T(8,128)(2,1)S(1)} %pad_maximum_fusion), channel_id=1, source_target_pairs={{0,8},{8,0},{16,24},{24,16},{1,9},{9,1},{17,25},{25,17},{2,10},{10... | collective-permute-start | bytes 786440 | tf_op jit(solution)/shard_map/ppermute | solution.py:583
  96.4 12.1 %copy-start = (bf16[64,64,128]{2,1,0:T(8,128)(2,1)}, bf16[64,64,128]{2,1,0:T(8,128)(2,1)S(1)}, u32[]{:S(2)}) copy-start(bf16[64,64,128]{2,1,0:T(8,128)(2,1)S(1)} %collective-permute-done.1) | copy-start | bytes 3145732
  96.4 12.1 %copy-start.1 = (bf16[64,64,128]{2,1,0:T(8,128)(2,1)}, bf16[64,64,128]{2,1,0:T(8,128)(2,1)S(1)}, u32[]{:S(2)}) copy-start(bf16[64,64,128]{2,1,0:T(8,128)(2,1)S(1)} %collective-permute-done.2) | copy-start | bytes 3145732
  114.0 52.7 %all-to-all-start.1 = ((bf16[8,4,4,2,64,128]{5,4,3,2,1,0:T(8,128)(2,1)}), bf16[8,4,4,2,64,128]{5,4,3,2,1,0:T(8,128)(2,1)}, u32[]{:S(2)}, u32[]{:S(2)}) async-start(bf16[8,4,4,2,64,128]{5,4,3,2,1,0:T(8,128)(2,1)} %shard_map.75), calls=%async_computation.1 | async-start | bytes 8388608 | tf_op jit(solution)/shard_map/all_to_all | solution.py:587
  119.0 74.1 %collective-permute-start.4 = (bf16[4,4,2,2,64,128]{5,4,3,2,1,0:T(8,128)(2,1)}, bf16[4,4,2,2,64,128]{5,4,3,2,1,0:T(8,128)(2,1)S(1)}, u32[]{:S(2)}, u32[]{:S(2)}) collective-permute-start(bf16[4,4,2,2,64,128]{5,4,3,2,1,0:T(8,128)(2,1)} %get-tuple-element.36), channel_id=1, source_target_pairs={{0,8},{8,0},{16,24},{24,16},{1,9},{9,1},{17,25},{25,17},{2,10},{10... | collective-permute-start | bytes 3145736 | tf_op jit(solution)/shard_map/ppermute | solution.py:583
  119.0 69.7 %collective-permute-start.5 = (bf16[4,784,128]{2,1,0:T(8,128)(2,1)}, bf16[4,784,128]{2,1,0:T(8,128)(2,1)S(1)}, u32[]{:S(2)}, u32[]{:S(2)}) collective-permute-start(bf16[4,784,128]{2,1,0:T(8,128)(2,1)} %get-tuple-element.37), channel_id=1, source_target_pairs={{0,16},{8,24},{16,0},{24,8},{1,17},{9,25},{17,1},{25,9},{2,18},{10... | collective-permute-start | bytes 2408456 | tf_op jit(solution)/shard_map/ppermute | solution.py:583
  122.0 71.0 %collective-permute-start.6 = (bf16[4,784,128]{2,1,0:T(8,128)(2,1)}, bf16[4,784,128]{2,1,0:T(8,128)(2,1)S(1)}, u32[]{:S(2)}, u32[]{:S(2)}) collective-permute-start(bf16[4,784,128]{2,1,0:T(8,128)(2,1)} %get-tuple-element.38), channel_id=1, source_target_pairs={{0,24},{8,16},{16,8},{24,0},{1,25},{9,17},{17,9},{25,1},{2,26},{10... | collective-permute-start | bytes 2408456 | tf_op jit(solution)/shard_map/ppermute | solution.py:583
  185.5 25.8 %collective-permute-start.7 = (bf16[4,1,2,2,64,128]{5,4,3,2,1,0:T(8,128)(2,1)}, bf16[4,1,2,2,64,128]{5,4,3,2,1,0:T(8,128)(2,1)S(1)}, u32[]{:S(2)}, u32[]{:S(2)}) collective-permute-start(bf16[4,1,2,2,64,128]{5,4,3,2,1,0:T(8,128)(2,1)} %get-tuple-element.39), channel_id=1, source_target_pairs={{0,8},{8,0},{16,24},{24,16},{1,9},{9,1},{17,25},{25,17},{2,10},{10... | collective-permute-start | bytes 786440 | tf_op jit(solution)/shard_map/ppermute | solution.py:583
  185.6 25.7 %collective-permute-start.8 = (bf16[1,784,128]{2,1,0:T(8,128)(2,1)}, bf16[1,784,128]{2,1,0:T(8,128)(2,1)S(1)}, u32[]{:S(2)}, u32[]{:S(2)}) collective-permute-start(bf16[1,784,128]{2,1,0:T(8,128)(2,1)} %get-tuple-element.40), channel_id=1, source_target_pairs={{0,16},{8,24},{16,0},{24,8},{1,17},{9,25},{17,1},{25,9},{2,18},{10... | collective-permute-start | bytes 602120 | tf_op jit(solution)/shard_map/ppermute | solution.py:583
  188.7 22.7 %collective-permute-start.9 = (bf16[1,784,128]{2,1,0:T(8,128)(2,1)}, bf16[1,784,128]{2,1,0:T(8,128)(2,1)S(1)}, u32[]{:S(2)}, u32[]{:S(2)}) collective-permute-start(bf16[1,784,128]{2,1,0:T(8,128)(2,1)} %get-tuple-element.41), channel_id=1, source_target_pairs={{0,24},{8,16},{16,8},{24,0},{1,25},{9,17},{17,9},{25,1},{2,26},{10... | collective-permute-start | bytes 602120 | tf_op jit(solution)/shard_map/ppermute | solution.py:583
  211.3 18.6 %copy-start.12 = (bf16[1,784,128]{2,1,0:T(8,128)(2,1)}, bf16[1,784,128]{2,1,0:T(8,128)(2,1)S(1)}, u32[]{:S(2)}) copy-start(bf16[1,784,128]{2,1,0:T(8,128)(2,1)S(1)} %collective-permute-done.8.refs_2_) | copy-start | bytes 602116
  211.3 18.6 %copy-start.13 = (bf16[1,784,128]{2,1,0:T(8,128)(2,1)}, bf16[1,784,128]{2,1,0:T(8,128)(2,1)S(1)}, u32[]{:S(2)}) copy-start(bf16[1,784,128]{2,1,0:T(8,128)(2,1)S(1)} %collective-permute-done.9.refs_3_) | copy-start | bytes 602116
  212.1 68.0 %all-to-all-start.2 = ((bf16[8,4,4,2,64,128]{5,4,3,2,1,0:T(8,128)(2,1)}), bf16[8,4,4,2,64,128]{5,4,3,2,1,0:T(8,128)(2,1)}, u32[]{:S(2)}, u32[]{:S(2)}) async-start(bf16[8,4,4,2,64,128]{5,4,3,2,1,0:T(8,128)(2,1)} %shard_map.78), calls=%async_computation.2 | async-start | bytes 8388608 | tf_op jit(solution)/shard_map/all_to_all | solution.py:587
  225.6 40.1 %collective-permute-start.11 = (bf16[3,784,128]{2,1,0:T(8,128)(2,1)}, bf16[3,784,128]{2,1,0:T(8,128)(2,1)S(1)}, u32[]{:S(2)}, u32[]{:S(2)}) collective-permute-start(bf16[3,784,128]{2,1,0:T(8,128)(2,1)} %get-tuple-element.45), channel_id=1, source_target_pairs={{0,16},{8,24},{16,0},{24,8},{1,17},{9,25},{17,1},{25,9},{2,18},{10... | collective-permute-start | bytes 1806344 | tf_op jit(solution)/shard_map/ppermute | solution.py:583
  225.6 54.4 %collective-permute-start.12 = (bf16[3,784,128]{2,1,0:T(8,128)(2,1)}, bf16[3,784,128]{2,1,0:T(8,128)(2,1)S(1)}, u32[]{:S(2)}, u32[]{:S(2)}) collective-permute-start(bf16[3,784,128]{2,1,0:T(8,128)(2,1)} %get-tuple-element.46), channel_id=1, source_target_pairs={{0,24},{8,16},{16,8},{24,0},{1,25},{9,17},{17,9},{25,1},{2,26},{10... | collective-permute-start | bytes 1806344 | tf_op jit(solution)/shard_map/ppermute | solution.py:583
  227.1 63.4 %collective-permute-start.10 = (bf16[4,3,2,2,64,128]{5,4,3,2,1,0:T(8,128)(2,1)}, bf16[4,3,2,2,64,128]{5,4,3,2,1,0:T(8,128)(2,1)S(1)}, u32[]{:S(2)}, u32[]{:S(2)}) collective-permute-start(bf16[4,3,2,2,64,128]{5,4,3,2,1,0:T(8,128)(2,1)} %get-tuple-element.44), channel_id=1, source_target_pairs={{0,8},{8,0},{16,24},{24,16},{1,9},{9,1},{17,25},{25,17},{2,10},{10... | collective-permute-start | bytes 2359304 | tf_op jit(solution)/shard_map/ppermute | solution.py:583
  265.6 24.9 %copy-start.4 = (bf16[3,784,128]{2,1,0:T(8,128)(2,1)}, bf16[3,784,128]{2,1,0:T(8,128)(2,1)S(1)}, u32[]{:S(2)}) copy-start(bf16[3,784,128]{2,1,0:T(8,128)(2,1)S(1)} %collective-permute-done.11.refs_6_) | copy-start | bytes 1806340
  280.0 10.5 %copy-start.5 = (bf16[3,784,128]{2,1,0:T(8,128)(2,1)}, bf16[3,784,128]{2,1,0:T(8,128)(2,1)S(1)}, u32[]{:S(2)}) copy-start(bf16[3,784,128]{2,1,0:T(8,128)(2,1)S(1)} %collective-permute-done.12.refs_7_) | copy-start | bytes 1806340
  280.1 10.4 %collective-permute-start.13 = (bf16[2,4,128,128]{3,2,1,0:T(8,128)(2,1)S(1)}, bf16[2,4,128,128]{3,2,1,0:T(8,128)(2,1)S(1)}, u32[]{:S(2)}, u32[]{:S(2)}) collective-permute-start(bf16[2,4,128,128]{3,2,1,0:T(8,128)(2,1)S(1)} %pad_maximum_fusion.1), channel_id=1, source_target_pairs={{0,8},{8,0},{16,24},{24,16},{1,9},{9,1},{17,25},{25,17},{2,10},{10... | collective-permute-start | bytes 786440 | tf_op jit(solution)/shard_map/ppermute | solution.py:583
  282.2 20.5 %collective-permute-start.16 = (bf16[8,1,2,64,128]{4,3,2,0,1:T(8,128)(2,1)S(1)}, bf16[8,1,2,64,128]{4,3,2,0,1:T(8,128)(2,1)S(1)}, u32[]{:S(2)}, u32[]{:S(2)}) collective-permute-start(bf16[8,1,2,64,128]{4,3,2,0,1:T(8,128)(2,1)S(1)} %get-tuple-element.52), channel_id=1, source_target_pairs={{0,24},{8,16},{16,8},{24,0},{1,25},{9,17},{17,9},{25,1},{2,26},{10... | collective-permute-start | bytes 786440 | tf_op jit(solution)/shard_map/ppermute | solution.py:583
  282.7 22.2 %collective-permute-start.15 = (bf16[8,1,2,64,128]{4,3,2,0,1:T(8,128)(2,1)S(1)}, bf16[8,1,2,64,128]{4,3,2,0,1:T(8,128)(2,1)S(1)}, u32[]{:S(2)}, u32[]{:S(2)}) collective-permute-start(bf16[8,1,2,64,128]{4,3,2,0,1:T(8,128)(2,1)S(1)} %get-tuple-element.53), channel_id=1, source_target_pairs={{0,16},{8,24},{16,0},{24,8},{1,17},{9,25},{17,1},{25,9},{2,18},{10... | collective-permute-start | bytes 786440 | tf_op jit(solution)/shard_map/ppermute | solution.py:583
  286.5 18.4 %collective-permute-start.14 = (bf16[8,1,2,64,128]{4,3,2,0,1:T(8,128)(2,1)S(1)}, bf16[8,1,2,64,128]{4,3,2,0,1:T(8,128)(2,1)S(1)}, u32[]{:S(2)}, u32[]{:S(2)}) collective-permute-start(bf16[8,1,2,64,128]{4,3,2,0,1:T(8,128)(2,1)S(1)} %get-tuple-element.54), channel_id=1, source_target_pairs={{0,8},{8,0},{16,24},{24,16},{1,9},{9,1},{17,25},{25,17},{2,10},{10... | collective-permute-start | bytes 786440 | tf_op jit(solution)/shard_map/ppermute | solution.py:583
  305.7 78.1 %all-to-all-start.3 = ((bf16[8,4,4,2,64,128]{5,4,3,2,1,0:T(8,128)(2,1)}), bf16[8,4,4,2,64,128]{5,4,3,2,1,0:T(8,128)(2,1)}, u32[]{:S(2)}, u32[]{:S(2)}) async-start(bf16[8,4,4,2,64,128]{5,4,3,2,1,0:T(8,128)(2,1)} %shard_map.80), calls=%async_computation.3 | async-start | bytes 8388608 | tf_op jit(solution)/shard_map/all_to_all | solution.py:587
  310.5 36.5 %collective-permute-start.17 = (bf16[8,3,2,64,128]{4,3,2,1,0:T(8,128)(2,1)}, bf16[8,3,2,64,128]{4,3,2,1,0:T(8,128)(2,1)S(1)}, u32[]{:S(2)}, u32[]{:S(2)}) collective-permute-start(bf16[8,3,2,64,128]{4,3,2,1,0:T(8,128)(2,1)} %get-tuple-element.48), channel_id=1, source_target_pairs={{0,8},{8,0},{16,24},{24,16},{1,9},{9,1},{17,25},{25,17},{2,10},{10... | collective-permute-start | bytes 2359304 | tf_op jit(solution)/shard_map/ppermute | solution.py:583
  314.0 52.0 %collective-permute-start.18 = (bf16[8,3,2,64,128]{4,3,2,1,0:T(8,128)(2,1)}, bf16[8,3,2,64,128]{4,3,2,1,0:T(8,128)(2,1)S(1)}, u32[]{:S(2)}, u32[]{:S(2)}) collective-permute-start(bf16[8,3,2,64,128]{4,3,2,1,0:T(8,128)(2,1)} %get-tuple-element.49), channel_id=1, source_target_pairs={{0,16},{8,24},{16,0},{24,8},{1,17},{9,25},{17,1},{25,9},{2,18},{10... | collective-permute-start | bytes 2359304 | tf_op jit(solution)/shard_map/ppermute | solution.py:583
  314.0 69.8 %collective-permute-start.19 = (bf16[8,3,2,64,128]{4,3,2,1,0:T(8,128)(2,1)}, bf16[8,3,2,64,128]{4,3,2,1,0:T(8,128)(2,1)S(1)}, u32[]{:S(2)}, u32[]{:S(2)}) collective-permute-start(bf16[8,3,2,64,128]{4,3,2,1,0:T(8,128)(2,1)} %get-tuple-element.50), channel_id=1, source_target_pairs={{0,24},{8,16},{16,8},{24,0},{1,25},{9,17},{17,9},{25,1},{2,26},{10... | collective-permute-start | bytes 2359304 | tf_op jit(solution)/shard_map/ppermute | solution.py:583
  347.0 36.8 %copy-start.8 = (bf16[8,3,2,64,128]{4,3,2,1,0:T(8,128)(2,1)}, bf16[8,3,2,64,128]{4,3,2,1,0:T(8,128)(2,1)S(1)}, u32[]{:S(2)}) copy-start(bf16[8,3,2,64,128]{4,3,2,1,0:T(8,128)(2,1)S(1)} %collective-permute-done.17) | copy-start | bytes 2359300
  365.9 17.9 %copy-start.9 = (bf16[8,3,2,64,128]{4,3,2,1,0:T(8,128)(2,1)}, bf16[8,3,2,64,128]{4,3,2,1,0:T(8,128)(2,1)S(1)}, u32[]{:S(2)}) copy-start(bf16[8,3,2,64,128]{4,3,2,1,0:T(8,128)(2,1)S(1)} %collective-permute-done.18) | copy-start | bytes 2359300
  (13 other events, 24.1 us)

commit v4 on v3

--- a/solution.py
+++ b/solution.py
@@ -240,14 +240,11 @@
 
 
 def swap_quarters(block):
-    size = block.shape[0]
-    half = size // 2
-    rolled = pltpu.roll(block, half, 1)
-    left = left_half(half, size)
+    half = block.shape[0] // 2
     return jnp.concatenate(
         [
-            jnp.where(left, block[:half], rolled[half:]),
-            jnp.where(left, rolled[:half], block[half:]),
+            jnp.concatenate([block[:half, :half], block[half:, :half]], axis=1),
+            jnp.concatenate([block[:half, half:], block[half:, half:]], axis=1),
         ],
         axis=0,
     )
@@ -327,7 +324,7 @@
             for b in range(order // tile):
                 at = (slice(row, row + tile), slice(b * tile, (b + 1) * tile))
                 out_block(
-                    (start + row) // tile, b, swap_quarters(real[at]), swap_quarters(imag[at])
+                    (start + row) // tile, b, swap_quarters(real[at].astype(NARROW)), swap_quarters(imag[at].astype(NARROW))
                 )
 
 
@@ -348,8 +345,16 @@
     pair_at, diagonal_at, last_at, length = far_rows(n, tile)
 
     def kernel(place_ref, coeff_ref, after_ref, *refs):
-        count = 1 if direct_in else n
+        count = 1 if direct_in else n + 1
         moved_refs, refs = refs[:count], refs[count:]
+        ahead = pl.program_id(0) == 0
+
+        def far(i, rows):
+            if i > 2:
+                return moved_refs[i + 1][0, rows].astype(WIDE)
+            one, other = (moved_refs[k][0, rows].astype(WIDE) for k in (2, 3))
+            return jnp.where(ahead, one, other)
+
         count = 1 if direct_out else n
         out_refs, (recip, first) = refs[:count], refs[count:]
         me = place_ref[0]
@@ -360,28 +365,28 @@
                 return square(moved_refs[0], pl.ds((j ^ me) * 2, 2), i, 0, c)
             if i < 2:
                 return square(moved_refs[i], i ^ j, 0, c)
-            return moved_refs[i][0, other_rows(i ^ j, c, tile)].astype(WIDE)
+            return far(i, other_rows(i ^ j, c, tile))
 
         def mean(c, a, b):
             if direct_in or a < 2 or (a ^ b) >= 2:
-                return 0.5 * (stacked(c, a, b) + stacked(c, b, a).T)
+                turned = stacked(c, b, a).astype(NARROW).T.astype(WIDE)
+                return 0.5 * (stacked(c, a, b) + turned)
             if a == b:
-                ref = moved_refs[a]
-                packed = ref[0, diagonal_at + c * half:diagonal_at + (c + 1) * half]
-                diagonals = ref[0, last_at:length]
-                return unpack_diagonal(packed.astype(WIDE), diagonals.astype(WIDE), c)
-            here = moved_refs[a][0, pair_at:pair_at + tile].astype(WIDE)
-            there = moved_refs[b][0, pair_at:pair_at + tile].astype(WIDE).T
+                at = diagonal_at + c * half
+                packed = far(a, slice(at, at + half))
+                return unpack_diagonal(packed, far(a, slice(last_at, length)), c)
+            here = far(a, slice(pair_at, pair_at + tile))
+            there = far(b, slice(pair_at, pair_at + tile)).T
             return jnp.where(odd == (c == 0), here, there)
 
         for c in range(2):
             for a in range(n):
                 for b in range(a + 1):
-                    block = swap_quarters(mean(c, a, b))
+                    block = swap_quarters(mean(c, a, b).astype(NARROW))
                     rows, columns = slice(a * tile, (a + 1) * tile), slice(b * tile, (b + 1) * tile)
                     recip[c, rows, columns] = block.astype(NARROW)
                     if a != b:
-                        recip[c, columns, rows] = block.T.astype(NARROW)
+                        recip[c, columns, rows] = block.astype(NARROW).T
 
         def out_block(a, b, real, imag):
             gap = a ^ b
@@ -391,7 +396,7 @@
                 return
             if not direct_out and a >= 2 and gap == 0:
                 at = diagonal_at
-                for value in pack_diagonals(real, imag):
+                for value in pack_diagonals(real.astype(WIDE), imag.astype(WIDE)):
                     out_refs[a][0, at:at + value.shape[0]] = value.astype(NARROW)
                     at += value.shape[0]
                 return
@@ -415,19 +420,23 @@
     far = (freqs, length, tile)
     split_shapes = [shaped(*close)] * 2 + [shaped(*far)] * (n - 2)
 
-    def specs(direct, first):
+    def specs(direct, first, split):
         if direct:
             block = (2 * n, n, 1, 2, half, tile)
             return [pl.BlockSpec(block, lambda i: (0, 0, i + first, 0, 0, 0))]
         close = pl.BlockSpec((n, 1, 2, 2, half, tile), lambda i: (0, i + first, 0, 0, 0, 0))
         far = pl.BlockSpec((1, length, tile), lambda i: (i + first, 0, 0))
-        return [close] * 2 + [far] * (n - 2)
+        if not split:
+            return [close] * 2 + [far] * (n - 2)
+        one = pl.BlockSpec((1, length, tile), lambda i: (0, 0, 0))
+        others = pl.BlockSpec((1, length, tile), lambda i: (jnp.maximum(i - 1, 0), 0, 0))
+        return [close] * 2 + [one, others] + [far] * (n - 3)
 
     return pl.pallas_call(
         kernel,
         grid=(freqs,),
-        in_specs=[IN_SMEM, IN_SMEM, UNREAD] + specs(direct_in, start),
-        out_specs=specs(direct_out, 0),
+        in_specs=[IN_SMEM, IN_SMEM, UNREAD] + specs(direct_in, start, True),
+        out_specs=specs(direct_out, 0, False),
         out_shape=[shaped(*whole)] if direct_out else split_shapes,
         scratch_shapes=[pltpu.VMEM((2, order, order), NARROW)] * 2,
         compiler_params=params(),
@@ -453,29 +462,32 @@
                         out_refs[d][block, f, c] = moved_ref[halves(block), me ^ d, f, c]
         for d in range(2, n):
             for f in range(freqs):
+                out_ref, own = (out_refs[d + 1], f) if d > 2 or f else (out_refs[2], 0)
+                own = f - 1 if d == 2 and f else own
                 for block in range(2, n):
                     for c in range(2):
                         rows = moved_ref[halves(block), me ^ d, f, c].reshape(tile, tile)
-                        out_refs[d][f, other_rows(block, c, tile)] = rows
+                        out_ref[own, other_rows(block, c, tile)] = rows
                 here = square(moved_ref, halves(1), me ^ d, f, mine)
                 there = square(pairs_ref, (d ^ 1) - 2, slice(None), f)
                 mean = (0.5 * (here + there.T)).astype(NARROW)
-                out_refs[d][f, pair_at:pair_at + tile] = mean
+                out_ref[own, pair_at:pair_at + tile] = mean
                 means = []
                 for c in range(2):
                     block = square(moved_ref, halves(0), me ^ d, f, c)
                     means.append(0.5 * (block + block.T))
                 at = diagonal_at
                 for value in pack_diagonals(*means):
-                    out_refs[d][f, at:at + value.shape[0]] = value.astype(NARROW)
+                    out_ref[own, at:at + value.shape[0]] = value.astype(NARROW)
                     at += value.shape[0]
 
     close, far = shaped(n, freqs, 2, 2, half, tile), shaped(freqs, length, tile)
+    split = [shaped(count, length, tile) for count in (1, freqs - 1)]
     return pl.pallas_call(
         kernel,
         in_specs=[IN_SMEM, UNREAD] + [IN_VMEM] * 2,
-        out_specs=[IN_VMEM] * n,
-        out_shape=[close] * 2 + [far] * (n - 2),
+        out_specs=[IN_VMEM] * (n + 1),
+        out_shape=[close] * 2 + split + [far] * (n - 3),
         compiler_params=params(),
         cost_estimate=cost(0, 4 * moved.size),
     )(place, after, moved, pairs)
@@ -651,9 +663,11 @@
     early = over_src(early)
     moved1 = spread_chunk(spectrum, 1)
     sent1 = gather(moved1, 1, place)
-    rows1 = over_src(sent1)
+    first, others = (swapped(rows, 2) for rows in sent1[2:4])
+    rows1 = [sent1[0], swapped(sent1[1], 1), first, others]
+    rows1 += [swapped(sent1[d + 1], d) for d in range(3, n)]
     parts = [part.reshape(2 * n, sizes[0], 2, half, src_tiles) for part in early]
-    moved0 = spread(side_by_side(parts, sent1[0]))
+    moved0 = spread(gate(side_by_side(parts, sent1[0]), first))
     rest0 = predict(place, coeffs[0], [moved0], n, True, False, 1, sizes[0], sent1[0])
     sent0 = rest0[0]
     first0 = predict(place, coeffs[0], [moved0], n, True, False, 0, 1, sent0)

time: 396 us -> 390 us (0.985)
  starting transfers between devices: 52.3 us -> 47.1 us
    all_to_all x4, starting transfers between devices: 28.1 us -> 20.5 us  [spread(): return lax.all_to_all(value, 'rcv', split_axis=0, concat_axis=0, tiled=True)]
    ppermute x20 -> x21, starting transfers between devices: 24.3 us -> 26.5 us  [swapped(): return lax.ppermute(value, 'src', [(i, i ^ gap) for i in range(size)])]
    ppermute x20 -> x21, waiting for transfers between devices: 170 us -> 171 us  [swapped(): return lax.ppermute(value, 'src', [(i, i ^ gap) for i in range(size)])]
  transfers between devices with their start and end apart: 24 -> 25, of which waited for: 12 -> 11; matrix products, arithmetic and copies ran while one was open for 1% -> 1% of each run, Pallas kernels for 13% -> 14%
where the time goes in v4:
time: 390 us; the launch traced here: 389 us
  waiting for transfers between devices  258 us (66%)
  Pallas kernels  72.3 us (19%)
  starting transfers between devices  47.1 us (12%)
  local copies, waits for them, and re-layouts  9.76 us (3%)
    ppermute x21, waiting for transfers between devices, swapped(): return lax.ppermute(value, 'src', [(i, i ^ gap) for i in range(size)])  171 us
    all_to_all x4, waiting for transfers between devices, spread(): return lax.all_to_all(value, 'rcv', split_axis=0, concat_axis=0, tiled=True)  87.7 us
    pallas_call x3, Pallas kernels, predict(): pl.pallas_call(kernel, grid=(freqs,), in_specs=[IN_SMEM, IN_SMEM, UNREAD]...  34.7 us
    ppermute x21, starting transfers between devices, swapped(): return lax.ppermute(value, 'src', [(i, i ^ gap) for i in range(size)])  26.5 us
    all_to_all x4, starting transfers between devices, spread(): return lax.all_to_all(value, 'rcv', split_axis=0, concat_axis=0, tiled=True)  20.5 us
    pallas_call x1, Pallas kernels, inverse_dft(): pl.pallas_call(kernel, grid=(half // ROWS,), in_specs=[IN_SMEM] + [pl.Blo...  10.2 us
    pallas_call x1, Pallas kernels, forward_dft(): pl.pallas_call(kernel, grid=(half // ROWS,), in_specs=[IN_SMEM, UNREAD] +...  9.49 us
  transfers between devices with their start and end apart: 25, of which 11 were waited for; matrix products, arithmetic and copies ran while one was open for 1% of the time, Pallas kernels for 14%

profile of v4, /device:TPU:10, one launch (start us, length us, event | category | flops | bytes accessed | tf_op | source)
XLA Modules:
  0.0 388.9 jit_solution(6099398801210019535)
XLA Ops:
  0.0 9.5 %shard_map.73 = (bf16[64,64,128]{2,1,0:T(8,128)(2,1)}, bf16[64,64,128]{2,1,0:T(8,128)(2,1)}, bf16[64,64,128]{2,1,0:T(8,128)(2,1)}, bf16[64,64,128]{2,1,0:T(8,128)(2,1)}, bf16[256,64,128]{2,1,0:T(8,128)(2,1)}) custom-call(s32[1]{0:T(128)} %bitcast.place_ref.after_ref, s32[1]{0:T(128)} %bitcast.place_ref.after_ref, ...), custom_call_target="tpu_custom_call" | custom-call | tf_op jit(solution)/shard_map/pallas_call | solution.py:170
  9.5 5.0 %all-to-all-start = ((bf16[8,4,4,2,64,128]{5,4,3,2,1,0:T(8,128)(2,1)}), bf16[8,4,4,2,64,128]{5,4,3,2,1,0:T(8,128)(2,1)}, u32[]{:S(2)}, u32[]{:S(2)}) async-start(bf16[8,4,4,2,64,128]{5,4,3,2,1,0:T(8,128)(2,1)} %bitcast.32), calls=%async_computation | async-start | bytes 8388608 | tf_op jit(solution)/shard_map/all_to_all | solution.py:599
  14.5 3.0 collective-permute-start.2
  17.9 44.2 %all-to-all-done.moved_ref = bf16[8,4,4,2,64,128]{5,4,3,2,1,0:T(8,128)(2,1)} async-done(((bf16[8,4,4,2,64,128]{5,4,3,2,1,0:T(8,128)(2,1)}), bf16[8,4,4,2,64,128]{5,4,3,2,1,0:T(8,128)(2,1)}, u32[]{:S(2)}, u32[]{:S(2)}) %all-to-all-start) | async-done | bytes 4194336 | tf_op jit(solution)/shard_map/all_to_all | solution.py:599
  63.3 27.9 %collective-permute-done.pairs_ref = bf16[2,2,4,64,128]{4,3,2,1,0:T(8,128)(2,1)S(1)} collective-permute-done((bf16[2,2,4,64,128]{4,3,2,1,0:T(8,128)(2,1)S(1)}, bf16[2,2,4,64,128]{4,3,2,1,0:T(8,128)(2,1)S(1)}, u32[]{:S(2)}, u32[]{:S(2)}) %collective-permute-start) | collective-permute-done | bytes 262176 | tf_op jit(solution)/shard_map/ppermute | solution.py:595
  91.9 4.6 %shard_map.74 = (bf16[4,4,2,2,64,128]{5,4,3,2,1,0:T(8,128)(2,1)}, bf16[4,4,2,2,64,128]{5,4,3,2,1,0:T(8,128)(2,1)}, bf16[1,784,128]{2,1,0:T(8,128)(2,1)}, bf16[3,...) custom-call(s32[1]{0:T(128)} %bitcast.place_ref.after_ref, s32[1]{0:T(128)} %bitcast.place_ref.after_ref, ...), custom_call_target="tpu_custom_call" | custom-call | tf_op jit(solution)/shard_map/pallas_call | solution.py:486
  96.5 3.0 collective-permute-start.4
  99.5 14.4 %collective-permute-done.3 = bf16[64,64,128]{2,1,0:T(8,128)(2,1)S(1)} collective-permute-done((bf16[64,64,128]{2,1,0:T(8,128)(2,1)}, bf16[64,64,128]{2,1,0:T(8,128)(2,1)S(1)}, u32[]{:S(2)}, u32[]{:S(2)}) %collective-permute-start.3) | collective-permute-done | bytes 1048608 | tf_op jit(solution)/shard_map/ppermute | solution.py:595
  114.9 4.5 %shard_map.75 = bf16[8,4,4,2,64,128]{5,4,3,2,1,0:T(8,128)(2,1)} custom-call(bf16[4,4,2,2,64,128]{5,4,3,2,1,0:T(8,128)(2,1)} %get-tuple-element.31.after_ref.refs_0_, bf16[8,4,2,64,128]{4,3,2,1,0:T(8,128)(2,1)} %bitcast.35, bf16[8,4,2,64,128]{4,3,2,1,0:T(8,128)(2,1)} %bitcast.36, bf16[8,4,2,64,128]{4,3,2,1,0:T(8,128)(2,1)} %bitcast.37, ...), custom_call_target="tpu_custom_call" | custom-call | tf_op jit(solution)/shard_map/pallas_call | solution.py:557
  119.4 4.8 %all-to-all-start.1 = ((bf16[8,4,4,2,64,128]{5,4,3,2,1,0:T(8,128)(2,1)}), bf16[8,4,4,2,64,128]{5,4,3,2,1,0:T(8,128)(2,1)}, u32[]{:S(2)}, u32[]{:S(2)}) async-start(bf16[8,4,4,2,64,128]{5,4,3,2,1,0:T(8,128)(2,1)} %shard_map.75), calls=%async_computation.1 | async-start | bytes 8388608 | tf_op jit(solution)/shard_map/all_to_all | solution.py:599
  124.3 3.0 collective-permute-start.6
  128.5 43.4 %all-to-all-done.1.refs_0_ = bf16[8,4,4,2,64,128]{5,4,3,2,1,0:T(8,128)(2,1)} async-done(((bf16[8,4,4,2,64,128]{5,4,3,2,1,0:T(8,128)(2,1)}), bf16[8,4,4,2,64,128]{5,4,3,2,1,0:T(8,128)(2,1)}, u32[]{:S(2)}, u32[]{:S(2)}) %all-to-all-start.1) | async-done | bytes 4194336 | tf_op jit(solution)/shard_map/all_to_all | solution.py:599
  171.9 12.5 %shard_map.76 = (bf16[4,3,2,2,64,128]{5,4,3,2,1,0:T(8,128)(2,1)}, bf16[4,3,2,2,64,128]{5,4,3,2,1,0:T(8,128)(2,1)}, bf16[3,784,128]{2,1,0:T(8,128)(2,1)}, bf16[3,784,128]{2,1,0:T(8,128)(2,1)}) custom-call(s32[1]{0:T(128)} %bitcast.place_ref.after_ref, f32[4,2]{1,0:T(4,128)} %broadcast_multiply_fusion.coeff_ref, ...), custom_call_target="tpu_custom_call" | custom-call | tf_op jit(solution)/shard_map/pallas_call | solution.py:435
  184.4 5.4 %shard_map.77 = (bf16[4,1,2,2,64,128]{5,4,3,2,1,0:T(8,128)(2,1)}, bf16[4,1,2,2,64,128]{5,4,3,2,1,0:T(8,128)(2,1)}, bf16[1,784,128]{2,1,0:T(8,128)(2,1)}, bf16[1,784,128]{2,1,0:T(8,128)(2,1)}) custom-call(s32[1]{0:T(128)} %bitcast.place_ref.after_ref, f32[4,2]{1,0:T(4,128)} %broadcast_multiply_fusion.coeff_ref, ...), custom_call_target="tpu_custom_call" | custom-call | tf_op jit(solution)/shard_map/pallas_call | solution.py:435
  189.9 3.0 collective-permute-start.9
  195.2 16.8 %shard_map.78 = bf16[8,4,4,2,64,128]{5,4,3,2,1,0:T(8,128)(2,1)} custom-call(s32[1]{0:T(128)} %bitcast.place_ref.after_ref, f32[4,2]{1,0:T(4,128)} %broadcast_multiply_fusion.1.coeff_ref, bf16[4,1,2,2,64,128]{5,4,3,2,1,0:T(8,128)(2,1)} %get-tuple-element.39.after_ref.refs_0_, bf16[4,4,2,2,64,128]{5,4,3,2,1,0:T(8,128)(2,1)} %get-tuple-element.31.after_ref.refs_0_, ...), custom_call_target="tpu_custom_call" | custom-call | tf_op jit(solution)/shard_map/pallas_call | solution.py:435
  212.8 6.0 %all-to-all-start.2 = ((bf16[8,4,4,2,64,128]{5,4,3,2,1,0:T(8,128)(2,1)}), bf16[8,4,4,2,64,128]{5,4,3,2,1,0:T(8,128)(2,1)}, u32[]{:S(2)}, u32[]{:S(2)}) async-start(bf16[8,4,4,2,64,128]{5,4,3,2,1,0:T(8,128)(2,1)} %shard_map.78), calls=%async_computation.2 | async-start | bytes 8388608 | tf_op jit(solution)/shard_map/all_to_all | solution.py:599
  218.8 1.9 collective-permute-start.12
  223.2 37.5 %collective-permute-done.12.refs_6_ = bf16[3,784,128]{2,1,0:T(8,128)(2,1)S(1)} collective-permute-done((bf16[3,784,128]{2,1,0:T(8,128)(2,1)}, bf16[3,784,128]{2,1,0:T(8,128)(2,1)S(1)}, u32[]{:S(2)}, u32[]{:S(2)}) %collective-permute-start.12) | collective-permute-done | bytes 602144 | tf_op jit(solution)/shard_map/ppermute | solution.py:595
  260.7 13.2 %collective-permute-done.13.refs_7_ = bf16[3,784,128]{2,1,0:T(8,128)(2,1)S(1)} collective-permute-done((bf16[3,784,128]{2,1,0:T(8,128)(2,1)}, bf16[3,784,128]{2,1,0:T(8,128)(2,1)S(1)}, u32[]{:S(2)}, u32[]{:S(2)}) %collective-permute-start.13) | collective-permute-done | bytes 602144 | tf_op jit(solution)/shard_map/ppermute | solution.py:595
  274.1 2.1 fusion
  277.5 2.9 collective-permute-start.16
  280.4 3.9 %shard_map.79 = (bf16[8,3,2,64,128]{4,3,2,1,0:T(8,128)(2,1)}, bf16[8,3,2,64,128]{4,3,2,1,0:T(8,128)(2,1)}, bf16[8,3,2,64,128]{4,3,2,1,0:T(8,128)(2,1)}, bf16[8,3,2,64,128]{4,3,2,1,0:T(8,128)(2,1)}) custom-call(bf16[8,4,4,2,64,128]{5,4,3,2,1,0:T(8,128)(2,1)} %all-to-all-done.2.moved_ref), custom_call_target="tpu_custom_call" | custom-call | tf_op jit(solution)/shard_map/pallas_call | solution.py:575
  285.4 5.0 %shard_map.80 = bf16[8,4,4,2,64,128]{5,4,3,2,1,0:T(8,128)(2,1)} custom-call(s32[1]{0:T(128)} %bitcast.place_ref.after_ref, bf16[8,3,2,64,128]{4,3,2,1,0:T(8,128)(2,1)} %get-tuple-element.47.after_ref, bf16[4,1,2,2,64,128]{5,4,3,2,1,0:T(8,128)(2,1)} %get-tuple-element.39.after_ref.refs_0_, bf16[4,1,2,2,64,128]{5,4,3,2,1,0:T(8,128)(2,1)} %copy-done.17, ...), custom_call_target="tpu_custom_call" | custom-call | tf_op jit(solution)/shard_map/pallas_call | solution.py:539
  290.3 6.2 %collective-permute-done.17 = bf16[8,1,2,64,128]{4,3,2,0,1:T(8,128)(2,1)S(1)} collective-permute-done((bf16[8,1,2,64,128]{4,3,2,0,1:T(8,128)(2,1)S(1)}, bf16[8,1,2,64,128]{4,3,2,0,1:T(8,128)(2,1)S(1)}, u32[]{:S(2)}, u32[]{:S(2)}) %collective-permute-start.17) | collective-permute-done | bytes 262176 | tf_op jit(solution)/shard_map/ppermute | solution.py:595
  296.6 3.0 collective-permute-done.16
  300.4 4.8 %all-to-all-start.3 = ((bf16[8,4,4,2,64,128]{5,4,3,2,1,0:T(8,128)(2,1)}), bf16[8,4,4,2,64,128]{5,4,3,2,1,0:T(8,128)(2,1)}, u32[]{:S(2)}, u32[]{:S(2)}) async-start(bf16[8,4,4,2,64,128]{5,4,3,2,1,0:T(8,128)(2,1)} %shard_map.80), calls=%async_computation.3 | async-start | bytes 8388608 | tf_op jit(solution)/shard_map/all_to_all | solution.py:599
  305.2 2.7 collective-permute-start.18
  309.4 32.2 %collective-permute-done.18 = bf16[8,3,2,64,128]{4,3,2,1,0:T(8,128)(2,1)S(1)} collective-permute-done((bf16[8,3,2,64,128]{4,3,2,1,0:T(8,128)(2,1)}, bf16[8,3,2,64,128]{4,3,2,1,0:T(8,128)(2,1)S(1)}, u32[]{:S(2)}, u32[]{:S(2)}) %collective-permute-start.18) | collective-permute-done | bytes 786464 | tf_op jit(solution)/shard_map/ppermute | solution.py:595
  341.6 19.0 %collective-permute-done.19 = bf16[8,3,2,64,128]{4,3,2,1,0:T(8,128)(2,1)S(1)} collective-permute-done((bf16[8,3,2,64,128]{4,3,2,1,0:T(8,128)(2,1)}, bf16[8,3,2,64,128]{4,3,2,1,0:T(8,128)(2,1)S(1)}, u32[]{:S(2)}, u32[]{:S(2)}) %collective-permute-start.19) | collective-permute-done | bytes 786464 | tf_op jit(solution)/shard_map/ppermute | solution.py:595
  360.6 17.2 %collective-permute-done.20 = bf16[8,3,2,64,128]{4,3,2,1,0:T(8,128)(2,1)S(1)} collective-permute-done((bf16[8,3,2,64,128]{4,3,2,1,0:T(8,128)(2,1)}, bf16[8,3,2,64,128]{4,3,2,1,0:T(8,128)(2,1)S(1)}, u32[]{:S(2)}, u32[]{:S(2)}) %collective-permute-start.20) | collective-permute-done | bytes 786464 | tf_op jit(solution)/shard_map/ppermute | solution.py:595
  378.7 10.2 %shard_map.81 = bf16[2,64,64,512]{3,2,1,0:T(8,128)(2,1)} custom-call(s32[1]{0:T(128)} %bitcast.place_ref.after_ref, bf16[1,256,512]{2,1,0:T(8,128)(2,1)} %constant.52.clone.refs_0_, bf16[4,16,512]{2,1,0:T(8,128)(2,1)} %constant.53.clone.refs_1_, bf16[4,48,512]{2,1,0:T(8,128)(2,1)} %constant.54.clone.refs_2_, bf16[256,64,128]{2,1,0:T(8,128)(2,1)} %bitcast.14.refs_3_, ...), custom_call_target="tpu_custom_call" | custom-call | tf_op jit(solution)/shard_map/pallas_call | solution.py:223
  (84 shorter events, 15.8 us)
Async XLA Ops:
  9.5 52.7 %all-to-all-start = ((bf16[8,4,4,2,64,128]{5,4,3,2,1,0:T(8,128)(2,1)}), bf16[8,4,4,2,64,128]{5,4,3,2,1,0:T(8,128)(2,1)}, u32[]{:S(2)}, u32[]{:S(2)}) async-start(bf16[8,4,4,2,64,128]{5,4,3,2,1,0:T(8,128)(2,1)} %bitcast.32), calls=%async_computation | async-start | bytes 8388608 | tf_op jit(solution)/shard_map/all_to_all | solution.py:599
  14.5 85.0 %collective-permute-start.1 = (bf16[64,64,128]{2,1,0:T(8,128)(2,1)}, bf16[64,64,128]{2,1,0:T(8,128)(2,1)S(1)}, u32[]{:S(2)}, u32[]{:S(2)}) collective-permute-start(bf16[64,64,128]{2,1,0:T(8,128)(2,1)} %get-tuple-element.33), channel_id=1, source_target_pairs={{0,8},{8,0},{16,24},{24,16},{1,9},{9,1},{17,25},{25,17},{2,10},{10... | collective-permute-start | bytes 3145736 | tf_op jit(solution)/shard_map/ppermute | solution.py:595
  14.5 85.0 %collective-permute-start.2 = (bf16[64,64,128]{2,1,0:T(8,128)(2,1)}, bf16[64,64,128]{2,1,0:T(8,128)(2,1)S(1)}, u32[]{:S(2)}, u32[]{:S(2)}) collective-permute-start(bf16[64,64,128]{2,1,0:T(8,128)(2,1)} %get-tuple-element.34), channel_id=1, source_target_pairs={{0,16},{8,24},{16,0},{24,8},{1,17},{9,25},{17,1},{25,9},{2,18},{10... | collective-permute-start | bytes 3145736 | tf_op jit(solution)/shard_map/ppermute | solution.py:595
  17.5 96.4 %collective-permute-start.3 = (bf16[64,64,128]{2,1,0:T(8,128)(2,1)}, bf16[64,64,128]{2,1,0:T(8,128)(2,1)S(1)}, u32[]{:S(2)}, u32[]{:S(2)}) collective-permute-start(bf16[64,64,128]{2,1,0:T(8,128)(2,1)} %get-tuple-element.35), channel_id=1, source_target_pairs={{0,24},{8,16},{16,8},{24,0},{1,25},{9,17},{17,9},{25,1},{2,26},{10... | collective-permute-start | bytes 3145736 | tf_op jit(solution)/shard_map/ppermute | solution.py:595
  63.2 27.9 %collective-permute-start = (bf16[2,2,4,64,128]{4,3,2,1,0:T(8,128)(2,1)S(1)}, bf16[2,2,4,64,128]{4,3,2,1,0:T(8,128)(2,1)S(1)}, u32[]{:S(2)}, u32[]{:S(2)}) collective-permute-start(bf16[2,2,4,64,128]{4,3,2,1,0:T(8,128)(2,1)S(1)} %pad_maximum_fusion), channel_id=1, source_target_pairs={{0,8},{8,0},{16,24},{24,16},{1,9},{9,1},{17,25},{25,17},{2,10},{10... | collective-permute-start | bytes 786440 | tf_op jit(solution)/shard_map/ppermute | solution.py:595
  96.5 22.9 %collective-permute-start.4 = (bf16[1,784,128]{2,1,0:T(8,128)(2,1)}, bf16[1,784,128]{2,1,0:T(8,128)(2,1)}, u32[]{:S(2)}, u32[]{:S(2)}) collective-permute-start(bf16[1,784,128]{2,1,0:T(8,128)(2,1)} %get-tuple-element.36), channel_id=1, source_target_pairs={{0,16},{8,24},{16,0},{24,8},{1,17},{9,25},{17,1},{25,9},{2,18},{10... | collective-permute-start | bytes 602120 | tf_op jit(solution)/shard_map/ppermute | solution.py:595
  99.5 14.4 %copy-start = (bf16[64,64,128]{2,1,0:T(8,128)(2,1)}, bf16[64,64,128]{2,1,0:T(8,128)(2,1)S(1)}, u32[]{:S(2)}) copy-start(bf16[64,64,128]{2,1,0:T(8,128)(2,1)S(1)} %collective-permute-done.1) | copy-start | bytes 3145732
  99.5 14.4 %copy-start.1 = (bf16[64,64,128]{2,1,0:T(8,128)(2,1)}, bf16[64,64,128]{2,1,0:T(8,128)(2,1)S(1)}, u32[]{:S(2)}) copy-start(bf16[64,64,128]{2,1,0:T(8,128)(2,1)S(1)} %collective-permute-done.2) | copy-start | bytes 3145732
  119.4 52.5 %all-to-all-start.1 = ((bf16[8,4,4,2,64,128]{5,4,3,2,1,0:T(8,128)(2,1)}), bf16[8,4,4,2,64,128]{5,4,3,2,1,0:T(8,128)(2,1)}, u32[]{:S(2)}, u32[]{:S(2)}) async-start(bf16[8,4,4,2,64,128]{5,4,3,2,1,0:T(8,128)(2,1)} %shard_map.75), calls=%async_computation.1 | async-start | bytes 8388608 | tf_op jit(solution)/shard_map/all_to_all | solution.py:599
  124.2 69.8 %collective-permute-start.5 = (bf16[4,4,2,2,64,128]{5,4,3,2,1,0:T(8,128)(2,1)}, bf16[4,4,2,2,64,128]{5,4,3,2,1,0:T(8,128)(2,1)S(1)}, u32[]{:S(2)}, u32[]{:S(2)}) collective-permute-start(bf16[4,4,2,2,64,128]{5,4,3,2,1,0:T(8,128)(2,1)} %get-tuple-element.40), channel_id=1, source_target_pairs={{0,8},{8,0},{16,24},{24,16},{1,9},{9,1},{17,25},{25,17},{2,10},{10... | collective-permute-start | bytes 3145736 | tf_op jit(solution)/shard_map/ppermute | solution.py:595
  124.3 68.7 %collective-permute-start.6 = (bf16[3,784,128]{2,1,0:T(8,128)(2,1)}, bf16[3,784,128]{2,1,0:T(8,128)(2,1)S(1)}, u32[]{:S(2)}, u32[]{:S(2)}) collective-permute-start(bf16[3,784,128]{2,1,0:T(8,128)(2,1)} %get-tuple-element.41), channel_id=1, source_target_pairs={{0,16},{8,24},{16,0},{24,8},{1,17},{9,25},{17,1},{25,9},{2,18},{10... | collective-permute-start | bytes 1806344 | tf_op jit(solution)/shard_map/ppermute | solution.py:595
  127.3 66.6 %collective-permute-start.7 = (bf16[4,784,128]{2,1,0:T(8,128)(2,1)}, bf16[4,784,128]{2,1,0:T(8,128)(2,1)S(1)}, u32[]{:S(2)}, u32[]{:S(2)}) collective-permute-start(bf16[4,784,128]{2,1,0:T(8,128)(2,1)} %get-tuple-element.42), channel_id=1, source_target_pairs={{0,24},{8,16},{16,8},{24,0},{1,25},{9,17},{17,9},{25,1},{2,26},{10... | collective-permute-start | bytes 2408456 | tf_op jit(solution)/shard_map/ppermute | solution.py:595
  189.8 22.2 %collective-permute-start.8 = (bf16[4,1,2,2,64,128]{5,4,3,2,1,0:T(8,128)(2,1)}, bf16[4,1,2,2,64,128]{5,4,3,2,1,0:T(8,128)(2,1)S(1)}, u32[]{:S(2)}, u32[]{:S(2)}) collective-permute-start(bf16[4,1,2,2,64,128]{5,4,3,2,1,0:T(8,128)(2,1)} %get-tuple-element.43), channel_id=1, source_target_pairs={{0,8},{8,0},{16,24},{24,16},{1,9},{9,1},{17,25},{25,17},{2,10},{10... | collective-permute-start | bytes 786440 | tf_op jit(solution)/shard_map/ppermute | solution.py:595
  189.9 22.1 %collective-permute-start.9 = (bf16[1,784,128]{2,1,0:T(8,128)(2,1)}, bf16[1,784,128]{2,1,0:T(8,128)(2,1)S(1)}, u32[]{:S(2)}, u32[]{:S(2)}) collective-permute-start(bf16[1,784,128]{2,1,0:T(8,128)(2,1)} %get-tuple-element.44), channel_id=1, source_target_pairs={{0,16},{8,24},{16,0},{24,8},{1,17},{9,25},{17,1},{25,9},{2,18},{10... | collective-permute-start | bytes 602120 | tf_op jit(solution)/shard_map/ppermute | solution.py:595
  193.0 19.0 %collective-permute-start.10 = (bf16[1,784,128]{2,1,0:T(8,128)(2,1)}, bf16[1,784,128]{2,1,0:T(8,128)(2,1)S(1)}, u32[]{:S(2)}, u32[]{:S(2)}) collective-permute-start(bf16[1,784,128]{2,1,0:T(8,128)(2,1)} %get-tuple-element.45), channel_id=1, source_target_pairs={{0,24},{8,16},{16,8},{24,0},{1,25},{9,17},{17,9},{25,1},{2,26},{10... | collective-permute-start | bytes 602120 | tf_op jit(solution)/shard_map/ppermute | solution.py:595
  212.0 11.2 %copy-start.12 = (bf16[1,784,128]{2,1,0:T(8,128)(2,1)}, bf16[1,784,128]{2,1,0:T(8,128)(2,1)S(1)}, u32[]{:S(2)}) copy-start(bf16[1,784,128]{2,1,0:T(8,128)(2,1)S(1)} %collective-permute-done.9.refs_2_) | copy-start | bytes 602116
  212.0 11.1 %copy-start.13 = (bf16[1,784,128]{2,1,0:T(8,128)(2,1)}, bf16[1,784,128]{2,1,0:T(8,128)(2,1)S(1)}, u32[]{:S(2)}) copy-start(bf16[1,784,128]{2,1,0:T(8,128)(2,1)S(1)} %collective-permute-done.10.refs_3_) | copy-start | bytes 602116
  212.8 61.3 %all-to-all-start.2 = ((bf16[8,4,4,2,64,128]{5,4,3,2,1,0:T(8,128)(2,1)}), bf16[8,4,4,2,64,128]{5,4,3,2,1,0:T(8,128)(2,1)}, u32[]{:S(2)}, u32[]{:S(2)}) async-start(bf16[8,4,4,2,64,128]{5,4,3,2,1,0:T(8,128)(2,1)} %shard_map.78), calls=%async_computation.2 | async-start | bytes 8388608 | tf_op jit(solution)/shard_map/all_to_all | solution.py:599
  218.8 41.9 %collective-permute-start.12 = (bf16[3,784,128]{2,1,0:T(8,128)(2,1)}, bf16[3,784,128]{2,1,0:T(8,128)(2,1)S(1)}, u32[]{:S(2)}, u32[]{:S(2)}) collective-permute-start(bf16[3,784,128]{2,1,0:T(8,128)(2,1)} %get-tuple-element.49), channel_id=1, source_target_pairs={{0,16},{8,24},{16,0},{24,8},{1,17},{9,25},{17,1},{25,9},{2,18},{10... | collective-permute-start | bytes 1806344 | tf_op jit(solution)/shard_map/ppermute | solution.py:595
  220.7 53.2 %collective-permute-start.13 = (bf16[3,784,128]{2,1,0:T(8,128)(2,1)}, bf16[3,784,128]{2,1,0:T(8,128)(2,1)S(1)}, u32[]{:S(2)}, u32[]{:S(2)}) collective-permute-start(bf16[3,784,128]{2,1,0:T(8,128)(2,1)} %get-tuple-element.50), channel_id=1, source_target_pairs={{0,24},{8,16},{16,8},{24,0},{1,25},{9,17},{17,9},{25,1},{2,26},{10... | collective-permute-start | bytes 1806344 | tf_op jit(solution)/shard_map/ppermute | solution.py:595
  221.3 63.0 %collective-permute-start.11 = (bf16[4,3,2,2,64,128]{5,4,3,2,1,0:T(8,128)(2,1)}, bf16[4,3,2,2,64,128]{5,4,3,2,1,0:T(8,128)(2,1)S(1)}, u32[]{:S(2)}, u32[]{:S(2)}) collective-permute-start(bf16[4,3,2,2,64,128]{5,4,3,2,1,0:T(8,128)(2,1)} %get-tuple-element.48), channel_id=1, source_target_pairs={{0,8},{8,0},{16,24},{24,16},{1,9},{9,1},{17,25},{25,17},{2,10},{10... | collective-permute-start | bytes 2359304 | tf_op jit(solution)/shard_map/ppermute | solution.py:595
  260.6 23.7 %copy-start.4 = (bf16[3,784,128]{2,1,0:T(8,128)(2,1)}, bf16[3,784,128]{2,1,0:T(8,128)(2,1)S(1)}, u32[]{:S(2)}) copy-start(bf16[3,784,128]{2,1,0:T(8,128)(2,1)S(1)} %collective-permute-done.12.refs_6_) | copy-start | bytes 1806340
  274.0 10.4 %collective-permute-start.14 = (bf16[2,4,128,128]{3,2,1,0:T(8,128)(2,1)S(1)}, bf16[2,4,128,128]{3,2,1,0:T(8,128)(2,1)S(1)}, u32[]{:S(2)}, u32[]{:S(2)}) collective-permute-start(bf16[2,4,128,128]{3,2,1,0:T(8,128)(2,1)S(1)} %pad_maximum_fusion.1), channel_id=1, source_target_pairs={{0,8},{8,0},{16,24},{24,16},{1,9},{9,1},{17,25},{25,17},{2,10},{10... | collective-permute-start | bytes 786440 | tf_op jit(solution)/shard_map/ppermute | solution.py:595
  276.1 20.5 %collective-permute-start.17 = (bf16[8,1,2,64,128]{4,3,2,0,1:T(8,128)(2,1)S(1)}, bf16[8,1,2,64,128]{4,3,2,0,1:T(8,128)(2,1)S(1)}, u32[]{:S(2)}, u32[]{:S(2)}) collective-permute-start(bf16[8,1,2,64,128]{4,3,2,0,1:T(8,128)(2,1)S(1)} %get-tuple-element.56), channel_id=1, source_target_pairs={{0,24},{8,16},{16,8},{24,0},{1,25},{9,17},{17,9},{25,1},{2,26},{10... | collective-permute-start | bytes 786440 | tf_op jit(solution)/shard_map/ppermute | solution.py:595
  277.5 22.1 %collective-permute-start.16 = (bf16[8,1,2,64,128]{4,3,2,0,1:T(8,128)(2,1)S(1)}, bf16[8,1,2,64,128]{4,3,2,0,1:T(8,128)(2,1)S(1)}, u32[]{:S(2)}, u32[]{:S(2)}) collective-permute-start(bf16[8,1,2,64,128]{4,3,2,0,1:T(8,128)(2,1)S(1)} %get-tuple-element.57), channel_id=1, source_target_pairs={{0,16},{8,24},{16,0},{24,8},{1,17},{9,25},{17,1},{25,9},{2,18},{10... | collective-permute-start | bytes 786440 | tf_op jit(solution)/shard_map/ppermute | solution.py:595
  280.4 19.2 %collective-permute-start.15 = (bf16[8,1,2,64,128]{4,3,2,0,1:T(8,128)(2,1)S(1)}, bf16[8,1,2,64,128]{4,3,2,0,1:T(8,128)(2,1)S(1)}, u32[]{:S(2)}, u32[]{:S(2)}) collective-permute-start(bf16[8,1,2,64,128]{4,3,2,0,1:T(8,128)(2,1)S(1)} %get-tuple-element.58), channel_id=1, source_target_pairs={{0,8},{8,0},{16,24},{24,16},{1,9},{9,1},{17,25},{25,17},{2,10},{10... | collective-permute-start | bytes 786440 | tf_op jit(solution)/shard_map/ppermute | solution.py:595
  300.4 77.4 %all-to-all-start.3 = ((bf16[8,4,4,2,64,128]{5,4,3,2,1,0:T(8,128)(2,1)}), bf16[8,4,4,2,64,128]{5,4,3,2,1,0:T(8,128)(2,1)}, u32[]{:S(2)}, u32[]{:S(2)}) async-start(bf16[8,4,4,2,64,128]{5,4,3,2,1,0:T(8,128)(2,1)} %shard_map.80), calls=%async_computation.3 | async-start | bytes 8388608 | tf_op jit(solution)/shard_map/all_to_all | solution.py:599
  305.2 36.4 %collective-permute-start.18 = (bf16[8,3,2,64,128]{4,3,2,1,0:T(8,128)(2,1)}, bf16[8,3,2,64,128]{4,3,2,1,0:T(8,128)(2,1)S(1)}, u32[]{:S(2)}, u32[]{:S(2)}) collective-permute-start(bf16[8,3,2,64,128]{4,3,2,1,0:T(8,128)(2,1)} %get-tuple-element.52), channel_id=1, source_target_pairs={{0,8},{8,0},{16,24},{24,16},{1,9},{9,1},{17,25},{25,17},{2,10},{10... | collective-permute-start | bytes 2359304 | tf_op jit(solution)/shard_map/ppermute | solution.py:595
  308.0 52.6 %collective-permute-start.19 = (bf16[8,3,2,64,128]{4,3,2,1,0:T(8,128)(2,1)}, bf16[8,3,2,64,128]{4,3,2,1,0:T(8,128)(2,1)S(1)}, u32[]{:S(2)}, u32[]{:S(2)}) collective-permute-start(bf16[8,3,2,64,128]{4,3,2,1,0:T(8,128)(2,1)} %get-tuple-element.53), channel_id=1, source_target_pairs={{0,16},{8,24},{16,0},{24,8},{1,17},{9,25},{17,1},{25,9},{2,18},{10... | collective-permute-start | bytes 2359304 | tf_op jit(solution)/shard_map/ppermute | solution.py:595
  308.6 69.2 %collective-permute-start.20 = (bf16[8,3,2,64,128]{4,3,2,1,0:T(8,128)(2,1)}, bf16[8,3,2,64,128]{4,3,2,1,0:T(8,128)(2,1)S(1)}, u32[]{:S(2)}, u32[]{:S(2)}) collective-permute-start(bf16[8,3,2,64,128]{4,3,2,1,0:T(8,128)(2,1)} %get-tuple-element.54), channel_id=1, source_target_pairs={{0,24},{8,16},{16,8},{24,0},{1,25},{9,17},{17,9},{25,1},{2,26},{10... | collective-permute-start | bytes 2359304 | tf_op jit(solution)/shard_map/ppermute | solution.py:595
  341.6 36.2 %copy-start.7 = (bf16[8,3,2,64,128]{4,3,2,1,0:T(8,128)(2,1)}, bf16[8,3,2,64,128]{4,3,2,1,0:T(8,128)(2,1)S(1)}, u32[]{:S(2)}) copy-start(bf16[8,3,2,64,128]{4,3,2,1,0:T(8,128)(2,1)S(1)} %collective-permute-done.18) | copy-start | bytes 2359300
  360.6 17.2 %copy-start.8 = (bf16[8,3,2,64,128]{4,3,2,1,0:T(8,128)(2,1)}, bf16[8,3,2,64,128]{4,3,2,1,0:T(8,128)(2,1)S(1)}, u32[]{:S(2)}) copy-start(bf16[8,3,2,64,128]{4,3,2,1,0:T(8,128)(2,1)S(1)} %collective-permute-done.19) | copy-start | bytes 2359300
  (14 other events, 32.0 us)

commit v5 on v4

--- a/solution.py
+++ b/solution.py
@@ -546,24 +546,6 @@
     )(place, after, *arrays, pairs)
 
 
-def side_by_side(parts, after):
-    shape = parts[0].shape
-    n = len(parts)
-
-    def kernel(after_ref, *refs):
-        for part, ref in enumerate(refs[:n]):
-            refs[n][:, part] = ref[...]
-
-    return pl.pallas_call(
-        kernel,
-        in_specs=[UNREAD] + [IN_VMEM] * n,
-        out_specs=IN_VMEM,
-        out_shape=shaped(shape[0], n, *shape[1:]),
-        compiler_params=params(),
-        cost_estimate=cost(0, 4 * n * parts[0].size),
-    )(after, *parts)
-
-
 def apart(moved, start):
     shape = moved.shape
     n, freqs = shape[1], shape[2] - start
@@ -666,8 +648,9 @@
     first, others = (swapped(rows, 2) for rows in sent1[2:4])
     rows1 = [sent1[0], swapped(sent1[1], 1), first, others]
     rows1 += [swapped(sent1[d + 1], d) for d in range(3, n)]
-    parts = [part.reshape(2 * n, sizes[0], 2, half, src_tiles) for part in early]
-    moved0 = spread(gate(side_by_side(parts, sent1[0]), first))
+    parts = [part.reshape(2 * n, 1, sizes[0], 2, half, src_tiles) for part in early]
+    joined = jnp.concatenate([gate(part, sent1[0], first) for part in parts], axis=1)
+    moved0 = spread(joined)
     rest0 = predict(place, coeffs[0], [moved0], n, True, False, 1, sizes[0], sent1[0])
     sent0 = rest0[0]
     first0 = predict(place, coeffs[0], [moved0], n, True, False, 0, 1, sent0)

time: 390 us -> 393 us (level)
  Pallas kernels: 72.3 us -> 67.9 us
    pallas_call x1 -> x0, Pallas kernels: 4.45 us -> none  [side_by_side(): pl.pallas_call(kernel, in_specs=[UNREAD] + [IN_VMEM] * n, out_specs=IN_VM...]
  transfers between devices with their start and end apart: 25 -> 25, of which waited for: 11 -> 11; matrix products, arithmetic and copies ran while one was open for 1% -> 1% of each run, Pallas kernels for 14% -> 12%
where the time goes in v5:
time: 393 us; the launch traced here: 392 us
  waiting for transfers between devices  261 us (66%)
  Pallas kernels  67.9 us (17%)
  starting transfers between devices  49.5 us (13%)
  local copies, waits for them, and re-layouts  9.45 us (2%)
  other arithmetic  4.6 us (1%)
    ppermute x21, waiting for transfers between devices, swapped(): return lax.ppermute(value, 'src', [(i, i ^ gap) for i in range(size)])  173 us
    all_to_all x4, waiting for transfers between devices, spread(): return lax.all_to_all(value, 'rcv', split_axis=0, concat_axis=0, tiled=True)  87.4 us
    pallas_call x3, Pallas kernels, predict(): pl.pallas_call(kernel, grid=(freqs,), in_specs=[IN_SMEM, IN_SMEM, UNREAD]...  34.7 us
    ppermute x21, starting transfers between devices, swapped(): return lax.ppermute(value, 'src', [(i, i ^ gap) for i in range(size)])  28.9 us
    all_to_all x4, starting transfers between devices, spread(): return lax.all_to_all(value, 'rcv', split_axis=0, concat_axis=0, tiled=True)  20.7 us
    pallas_call x1, Pallas kernels, inverse_dft(): pl.pallas_call(kernel, grid=(half // ROWS,), in_specs=[IN_SMEM] + [pl.Blo...  10.2 us
    pallas_call x1, Pallas kernels, forward_dft(): pl.pallas_call(kernel, grid=(half // ROWS,), in_specs=[IN_SMEM, UNREAD] +...  9.49 us
  transfers between devices with their start and end apart: 25, of which 11 were waited for; matrix products, arithmetic and copies ran while one was open for 1% of the time, Pallas kernels for 12%

profile of v5, /device:TPU:10, one launch (start us, length us, event | category | flops | bytes accessed | tf_op | source)
XLA Modules:
  0.0 392.4 jit_solution(10080615468547916595)
XLA Ops:
  0.0 9.5 %shard_map.73 = (bf16[64,64,128]{2,1,0:T(8,128)(2,1)}, bf16[64,64,128]{2,1,0:T(8,128)(2,1)}, bf16[64,64,128]{2,1,0:T(8,128)(2,1)}, bf16[64,64,128]{2,1,0:T(8,128)(2,1)}, bf16[256,64,128]{2,1,0:T(8,128)(2,1)}) custom-call(s32[1]{0:T(128)} %bitcast.place_ref.after_ref, s32[1]{0:T(128)} %bitcast.place_ref.after_ref, ...), custom_call_target="tpu_custom_call" | custom-call | tf_op jit(solution)/shard_map/pallas_call | solution.py:170
  9.5 5.0 %all-to-all-start = ((bf16[8,4,4,2,64,128]{5,4,3,2,1,0:T(8,128)(2,1)}), bf16[8,4,4,2,64,128]{5,4,3,2,1,0:T(8,128)(2,1)}, u32[]{:S(2)}, u32[]{:S(2)}) async-start(bf16[8,4,4,2,64,128]{5,4,3,2,1,0:T(8,128)(2,1)} %bitcast.32), calls=%async_computation | async-start | bytes 8388608 | tf_op jit(solution)/shard_map/all_to_all | solution.py:581
  14.5 3.0 collective-permute-start.3
  18.0 44.2 %all-to-all-done.moved_ref = bf16[8,4,4,2,64,128]{5,4,3,2,1,0:T(8,128)(2,1)} async-done(((bf16[8,4,4,2,64,128]{5,4,3,2,1,0:T(8,128)(2,1)}), bf16[8,4,4,2,64,128]{5,4,3,2,1,0:T(8,128)(2,1)}, u32[]{:S(2)}, u32[]{:S(2)}) %all-to-all-start) | async-done | bytes 4194336 | tf_op jit(solution)/shard_map/all_to_all | solution.py:581
  63.3 27.9 %collective-permute-done.pairs_ref = bf16[2,2,4,64,128]{4,3,2,1,0:T(8,128)(2,1)S(1)} collective-permute-done((bf16[2,2,4,64,128]{4,3,2,1,0:T(8,128)(2,1)S(1)}, bf16[2,2,4,64,128]{4,3,2,1,0:T(8,128)(2,1)S(1)}, u32[]{:S(2)}, u32[]{:S(2)}) %collective-permute-start) | collective-permute-done | bytes 262176 | tf_op jit(solution)/shard_map/ppermute | solution.py:577
  91.9 4.6 %shard_map.74 = (bf16[4,4,2,2,64,128]{5,4,3,2,1,0:T(8,128)(2,1)}, bf16[4,4,2,2,64,128]{5,4,3,2,1,0:T(8,128)(2,1)}, bf16[1,784,128]{2,1,0:T(8,128)(2,1)}, bf16[3,...) custom-call(s32[1]{0:T(128)} %bitcast.place_ref.after_ref, s32[1]{0:T(128)} %bitcast.place_ref.after_ref, ...), custom_call_target="tpu_custom_call" | custom-call | tf_op jit(solution)/shard_map/pallas_call | solution.py:486
  96.5 3.0 collective-permute-start.1
  99.5 16.9 %collective-permute-done.1.refs_2_ = bf16[1,784,128]{2,1,0:T(8,128)(2,1)S(1)} collective-permute-done((bf16[1,784,128]{2,1,0:T(8,128)(2,1)}, bf16[1,784,128]{2,1,0:T(8,128)(2,1)S(1)}, u32[]{:S(2)}, u32[]{:S(2)}) %collective-permute-start.1) | collective-permute-done | bytes 200736 | tf_op jit(solution)/shard_map/ppermute | solution.py:577
  117.1 3.3 pad_maximum_fusion
  120.4 4.9 %all-to-all-start.1 = ((bf16[8,4,4,2,64,128]{5,4,3,2,1,0:T(8,128)(2,1)}), bf16[8,4,4,2,64,128]{5,4,3,2,1,0:T(8,128)(2,1)}, u32[]{:S(2)}, u32[]{:S(2)}) async-start(bf16[8,4,4,2,64,128]{5,4,3,2,1,0:T(8,128)(2,1)} %pad_maximum_fusion), calls=%async_computation.1 | async-start | bytes 8388608 | tf_op jit(solution)/shard_map/all_to_all | solution.py:581
  125.3 2.3 collective-permute-start.5
  129.9 43.1 %all-to-all-done.1.refs_0_ = bf16[8,4,4,2,64,128]{5,4,3,2,1,0:T(8,128)(2,1)} async-done(((bf16[8,4,4,2,64,128]{5,4,3,2,1,0:T(8,128)(2,1)}), bf16[8,4,4,2,64,128]{5,4,3,2,1,0:T(8,128)(2,1)}, u32[]{:S(2)}, u32[]{:S(2)}) %all-to-all-start.1) | async-done | bytes 4194336 | tf_op jit(solution)/shard_map/all_to_all | solution.py:581
  173.0 12.5 %shard_map.75 = (bf16[4,3,2,2,64,128]{5,4,3,2,1,0:T(8,128)(2,1)}, bf16[4,3,2,2,64,128]{5,4,3,2,1,0:T(8,128)(2,1)}, bf16[3,784,128]{2,1,0:T(8,128)(2,1)}, bf16[3,784,128]{2,1,0:T(8,128)(2,1)}) custom-call(s32[1]{0:T(128)} %bitcast.place_ref.after_ref, f32[4,2]{1,0:T(4,128)} %broadcast_multiply_fusion.coeff_ref, ...), custom_call_target="tpu_custom_call" | custom-call | tf_op jit(solution)/shard_map/pallas_call | solution.py:435
  185.6 5.4 %shard_map.76 = (bf16[4,1,2,2,64,128]{5,4,3,2,1,0:T(8,128)(2,1)}, bf16[4,1,2,2,64,128]{5,4,3,2,1,0:T(8,128)(2,1)}, bf16[1,784,128]{2,1,0:T(8,128)(2,1)}, bf16[1,784,128]{2,1,0:T(8,128)(2,1)}) custom-call(s32[1]{0:T(128)} %bitcast.place_ref.after_ref, f32[4,2]{1,0:T(4,128)} %broadcast_multiply_fusion.coeff_ref, ...), custom_call_target="tpu_custom_call" | custom-call | tf_op jit(solution)/shard_map/pallas_call | solution.py:435
  191.0 2.3 collective-permute-start.8
  196.8 16.8 %shard_map.77 = bf16[8,4,4,2,64,128]{5,4,3,2,1,0:T(8,128)(2,1)} custom-call(s32[1]{0:T(128)} %bitcast.place_ref.after_ref, f32[4,2]{1,0:T(4,128)} %broadcast_multiply_fusion.1.coeff_ref, bf16[4,1,2,2,64,128]{5,4,3,2,1,0:T(8,128)(2,1)} %get-tuple-element.45.after_ref.refs_0_, bf16[4,4,2,2,64,128]{5,4,3,2,1,0:T(8,128)(2,1)} %get-tuple-element.34.after_ref.refs_0_, ...), custom_call_target="tpu_custom_call" | custom-call | tf_op jit(solution)/shard_map/pallas_call | solution.py:435
  214.4 6.0 %all-to-all-start.2 = ((bf16[8,4,4,2,64,128]{5,4,3,2,1,0:T(8,128)(2,1)}), bf16[8,4,4,2,64,128]{5,4,3,2,1,0:T(8,128)(2,1)}, u32[]{:S(2)}, u32[]{:S(2)}) async-start(bf16[8,4,4,2,64,128]{5,4,3,2,1,0:T(8,128)(2,1)} %shard_map.77), calls=%async_computation.2 | async-start | bytes 8388608 | tf_op jit(solution)/shard_map/all_to_all | solution.py:581
  220.4 3.8 collective-permute-start.12
  225.6 36.6 %collective-permute-done.12.refs_6_ = bf16[3,784,128]{2,1,0:T(8,128)(2,1)S(1)} collective-permute-done((bf16[3,784,128]{2,1,0:T(8,128)(2,1)}, bf16[3,784,128]{2,1,0:T(8,128)(2,1)S(1)}, u32[]{:S(2)}, u32[]{:S(2)}) %collective-permute-start.12) | collective-permute-done | bytes 602144 | tf_op jit(solution)/shard_map/ppermute | solution.py:577
  262.3 14.7 %collective-permute-done.13.refs_7_ = bf16[3,784,128]{2,1,0:T(8,128)(2,1)S(1)} collective-permute-done((bf16[3,784,128]{2,1,0:T(8,128)(2,1)}, bf16[3,784,128]{2,1,0:T(8,128)(2,1)S(1)}, u32[]{:S(2)}, u32[]{:S(2)}) %collective-permute-start.13) | collective-permute-done | bytes 602144 | tf_op jit(solution)/shard_map/ppermute | solution.py:577
  277.2 2.1 fusion
  279.7 3.9 collective-permute-start.16
  283.5 4.0 %shard_map.78 = (bf16[8,3,2,64,128]{4,3,2,1,0:T(8,128)(2,1)}, bf16[8,3,2,64,128]{4,3,2,1,0:T(8,128)(2,1)}, bf16[8,3,2,64,128]{4,3,2,1,0:T(8,128)(2,1)}, bf16[8,3,2,64,128]{4,3,2,1,0:T(8,128)(2,1)}) custom-call(bf16[8,4,4,2,64,128]{5,4,3,2,1,0:T(8,128)(2,1)} %all-to-all-done.2.moved_ref), custom_call_target="tpu_custom_call" | custom-call | tf_op jit(solution)/shard_map/pallas_call | solution.py:557
  288.5 5.0 %shard_map.79 = bf16[8,4,4,2,64,128]{5,4,3,2,1,0:T(8,128)(2,1)} custom-call(s32[1]{0:T(128)} %bitcast.place_ref.after_ref, bf16[8,3,2,64,128]{4,3,2,1,0:T(8,128)(2,1)} %get-tuple-element.53.after_ref, bf16[4,1,2,2,64,128]{5,4,3,2,1,0:T(8,128)(2,1)} %get-tuple-element.45.after_ref.refs_0_, bf16[4,1,2,2,64,128]{5,4,3,2,1,0:T(8,128)(2,1)} %copy-done.15, ...), custom_call_target="tpu_custom_call" | custom-call | tf_op jit(solution)/shard_map/pallas_call | solution.py:539
  293.5 6.1 %collective-permute-done.17 = bf16[8,1,2,64,128]{4,3,2,0,1:T(8,128)(2,1)S(1)} collective-permute-done((bf16[8,1,2,64,128]{4,3,2,0,1:T(8,128)(2,1)S(1)}, bf16[8,1,2,64,128]{4,3,2,0,1:T(8,128)(2,1)S(1)}, u32[]{:S(2)}, u32[]{:S(2)}) %collective-permute-start.17) | collective-permute-done | bytes 262176 | tf_op jit(solution)/shard_map/ppermute | solution.py:577
  299.6 2.7 collective-permute-done.16
  303.2 4.8 %all-to-all-start.3 = ((bf16[8,4,4,2,64,128]{5,4,3,2,1,0:T(8,128)(2,1)}), bf16[8,4,4,2,64,128]{5,4,3,2,1,0:T(8,128)(2,1)}, u32[]{:S(2)}, u32[]{:S(2)}) async-start(bf16[8,4,4,2,64,128]{5,4,3,2,1,0:T(8,128)(2,1)} %shard_map.79), calls=%async_computation.3 | async-start | bytes 8388608 | tf_op jit(solution)/shard_map/all_to_all | solution.py:581
  308.0 3.5 collective-permute-start.18
  312.9 31.6 %collective-permute-done.18 = bf16[8,3,2,64,128]{4,3,2,1,0:T(8,128)(2,1)S(1)} collective-permute-done((bf16[8,3,2,64,128]{4,3,2,1,0:T(8,128)(2,1)}, bf16[8,3,2,64,128]{4,3,2,1,0:T(8,128)(2,1)S(1)}, u32[]{:S(2)}, u32[]{:S(2)}) %collective-permute-start.18) | collective-permute-done | bytes 786464 | tf_op jit(solution)/shard_map/ppermute | solution.py:577
  344.5 18.9 %collective-permute-done.19 = bf16[8,3,2,64,128]{4,3,2,1,0:T(8,128)(2,1)S(1)} collective-permute-done((bf16[8,3,2,64,128]{4,3,2,1,0:T(8,128)(2,1)}, bf16[8,3,2,64,128]{4,3,2,1,0:T(8,128)(2,1)S(1)}, u32[]{:S(2)}, u32[]{:S(2)}) %collective-permute-start.19) | collective-permute-done | bytes 786464 | tf_op jit(solution)/shard_map/ppermute | solution.py:577
  363.4 17.9 %collective-permute-done.20 = bf16[8,3,2,64,128]{4,3,2,1,0:T(8,128)(2,1)S(1)} collective-permute-done((bf16[8,3,2,64,128]{4,3,2,1,0:T(8,128)(2,1)}, bf16[8,3,2,64,128]{4,3,2,1,0:T(8,128)(2,1)S(1)}, u32[]{:S(2)}, u32[]{:S(2)}) %collective-permute-start.20) | collective-permute-done | bytes 786464 | tf_op jit(solution)/shard_map/ppermute | solution.py:577
  382.2 10.2 %shard_map.80 = bf16[2,64,64,512]{3,2,1,0:T(8,128)(2,1)} custom-call(s32[1]{0:T(128)} %bitcast.place_ref.after_ref, bf16[1,256,512]{2,1,0:T(8,128)(2,1)} %constant.52.clone.refs_0_, bf16[4,16,512]{2,1,0:T(8,128)(2,1)} %constant.53.clone.refs_1_, bf16[4,48,512]{2,1,0:T(8,128)(2,1)} %constant.54.clone.refs_2_, bf16[256,64,128]{2,1,0:T(8,128)(2,1)} %bitcast.14.refs_3_, ...), custom_call_target="tpu_custom_call" | custom-call | tf_op jit(solution)/shard_map/pallas_call | solution.py:223
  (82 shorter events, 16.0 us)
Async XLA Ops:
  9.5 52.7 %all-to-all-start = ((bf16[8,4,4,2,64,128]{5,4,3,2,1,0:T(8,128)(2,1)}), bf16[8,4,4,2,64,128]{5,4,3,2,1,0:T(8,128)(2,1)}, u32[]{:S(2)}, u32[]{:S(2)}) async-start(bf16[8,4,4,2,64,128]{5,4,3,2,1,0:T(8,128)(2,1)} %bitcast.32), calls=%async_computation | async-start | bytes 8388608 | tf_op jit(solution)/shard_map/all_to_all | solution.py:581
  14.5 102.6 %copy-start.1 = (bf16[64,64,128]{2,1,0:T(8,128)(2,1)S(1)}, bf16[64,64,128]{2,1,0:T(8,128)(2,1)}, u32[]{:S(2)}) copy-start(bf16[64,64,128]{2,1,0:T(8,128)(2,1)} %get-tuple-element.35) | copy-start | bytes 3145732
  14.5 101.9 %collective-permute-start.2 = (bf16[64,64,128]{2,1,0:T(8,128)(2,1)}, bf16[64,64,128]{2,1,0:T(8,128)(2,1)S(1)}, u32[]{:S(2)}, u32[]{:S(2)}) collective-permute-start(bf16[64,64,128]{2,1,0:T(8,128)(2,1)} %get-tuple-element.38), channel_id=1, source_target_pairs={{0,8},{8,0},{16,24},{24,16},{1,9},{9,1},{17,25},{25,17},{2,10},{10... | collective-permute-start | bytes 3145736 | tf_op jit(solution)/shard_map/ppermute | solution.py:577
  14.5 101.9 %collective-permute-start.3 = (bf16[64,64,128]{2,1,0:T(8,128)(2,1)}, bf16[64,64,128]{2,1,0:T(8,128)(2,1)S(1)}, u32[]{:S(2)}, u32[]{:S(2)}) collective-permute-start(bf16[64,64,128]{2,1,0:T(8,128)(2,1)} %get-tuple-element.40), channel_id=1, source_target_pairs={{0,16},{8,24},{16,0},{24,8},{1,17},{9,25},{17,1},{25,9},{2,18},{10... | collective-permute-start | bytes 3145736 | tf_op jit(solution)/shard_map/ppermute | solution.py:577
  17.5 99.5 %collective-permute-start.4 = (bf16[64,64,128]{2,1,0:T(8,128)(2,1)}, bf16[64,64,128]{2,1,0:T(8,128)(2,1)}, u32[]{:S(2)}, u32[]{:S(2)}) collective-permute-start(bf16[64,64,128]{2,1,0:T(8,128)(2,1)} %get-tuple-element.42), channel_id=1, source_target_pairs={{0,24},{8,16},{16,8},{24,0},{1,25},{9,17},{17,9},{25,1},{2,26},{10... | collective-permute-start | bytes 3145736 | tf_op jit(solution)/shard_map/ppermute | solution.py:577
  63.2 27.9 %collective-permute-start = (bf16[2,2,4,64,128]{4,3,2,1,0:T(8,128)(2,1)S(1)}, bf16[2,2,4,64,128]{4,3,2,1,0:T(8,128)(2,1)S(1)}, u32[]{:S(2)}, u32[]{:S(2)}) collective-permute-start(bf16[2,2,4,64,128]{4,3,2,1,0:T(8,128)(2,1)S(1)} %pad_maximum_fusion.1), channel_id=1, source_target_pairs={{0,8},{8,0},{16,24},{24,16},{1,9},{9,1},{17,25},{25,17},{2,10},{10... | collective-permute-start | bytes 786440 | tf_op jit(solution)/shard_map/ppermute | solution.py:577
  96.5 19.9 %collective-permute-start.1 = (bf16[1,784,128]{2,1,0:T(8,128)(2,1)}, bf16[1,784,128]{2,1,0:T(8,128)(2,1)S(1)}, u32[]{:S(2)}, u32[]{:S(2)}) collective-permute-start(bf16[1,784,128]{2,1,0:T(8,128)(2,1)} %get-tuple-element.36), channel_id=1, source_target_pairs={{0,16},{8,24},{16,0},{24,8},{1,17},{9,25},{17,1},{25,9},{2,18},{10... | collective-permute-start | bytes 602120 | tf_op jit(solution)/shard_map/ppermute | solution.py:577
  120.4 52.7 %all-to-all-start.1 = ((bf16[8,4,4,2,64,128]{5,4,3,2,1,0:T(8,128)(2,1)}), bf16[8,4,4,2,64,128]{5,4,3,2,1,0:T(8,128)(2,1)}, u32[]{:S(2)}, u32[]{:S(2)}) async-start(bf16[8,4,4,2,64,128]{5,4,3,2,1,0:T(8,128)(2,1)} %pad_maximum_fusion), calls=%async_computation.1 | async-start | bytes 8388608 | tf_op jit(solution)/shard_map/all_to_all | solution.py:581
  125.3 70.3 %collective-permute-start.5 = (bf16[4,4,2,2,64,128]{5,4,3,2,1,0:T(8,128)(2,1)}, bf16[4,4,2,2,64,128]{5,4,3,2,1,0:T(8,128)(2,1)S(1)}, u32[]{:S(2)}, u32[]{:S(2)}) collective-permute-start(bf16[4,4,2,2,64,128]{5,4,3,2,1,0:T(8,128)(2,1)} %get-tuple-element.46), channel_id=1, source_target_pairs={{0,8},{8,0},{16,24},{24,16},{1,9},{9,1},{17,25},{25,17},{2,10},{10... | collective-permute-start | bytes 3145736 | tf_op jit(solution)/shard_map/ppermute | solution.py:577
  127.6 66.8 %collective-permute-start.6 = (bf16[3,784,128]{2,1,0:T(8,128)(2,1)}, bf16[3,784,128]{2,1,0:T(8,128)(2,1)S(1)}, u32[]{:S(2)}, u32[]{:S(2)}) collective-permute-start(bf16[3,784,128]{2,1,0:T(8,128)(2,1)} %get-tuple-element.47), channel_id=1, source_target_pairs={{0,16},{8,24},{16,0},{24,8},{1,17},{9,25},{17,1},{25,9},{2,18},{10... | collective-permute-start | bytes 1806344 | tf_op jit(solution)/shard_map/ppermute | solution.py:577
  128.6 66.9 %collective-permute-start.7 = (bf16[4,784,128]{2,1,0:T(8,128)(2,1)}, bf16[4,784,128]{2,1,0:T(8,128)(2,1)S(1)}, u32[]{:S(2)}, u32[]{:S(2)}) collective-permute-start(bf16[4,784,128]{2,1,0:T(8,128)(2,1)} %get-tuple-element.48), channel_id=1, source_target_pairs={{0,24},{8,16},{16,8},{24,0},{1,25},{9,17},{17,9},{25,1},{2,26},{10... | collective-permute-start | bytes 2408456 | tf_op jit(solution)/shard_map/ppermute | solution.py:577
  191.0 22.7 %collective-permute-start.8 = (bf16[4,1,2,2,64,128]{5,4,3,2,1,0:T(8,128)(2,1)}, bf16[4,1,2,2,64,128]{5,4,3,2,1,0:T(8,128)(2,1)S(1)}, u32[]{:S(2)}, u32[]{:S(2)}) collective-permute-start(bf16[4,1,2,2,64,128]{5,4,3,2,1,0:T(8,128)(2,1)} %get-tuple-element.49), channel_id=1, source_target_pairs={{0,8},{8,0},{16,24},{24,16},{1,9},{9,1},{17,25},{25,17},{2,10},{10... | collective-permute-start | bytes 786440 | tf_op jit(solution)/shard_map/ppermute | solution.py:577
  193.3 20.3 %collective-permute-start.9 = (bf16[1,784,128]{2,1,0:T(8,128)(2,1)}, bf16[1,784,128]{2,1,0:T(8,128)(2,1)S(1)}, u32[]{:S(2)}, u32[]{:S(2)}) collective-permute-start(bf16[1,784,128]{2,1,0:T(8,128)(2,1)} %get-tuple-element.50), channel_id=1, source_target_pairs={{0,16},{8,24},{16,0},{24,8},{1,17},{9,25},{17,1},{25,9},{2,18},{10... | collective-permute-start | bytes 602120 | tf_op jit(solution)/shard_map/ppermute | solution.py:577
  194.3 19.3 %collective-permute-start.10 = (bf16[1,784,128]{2,1,0:T(8,128)(2,1)}, bf16[1,784,128]{2,1,0:T(8,128)(2,1)S(1)}, u32[]{:S(2)}, u32[]{:S(2)}) collective-permute-start(bf16[1,784,128]{2,1,0:T(8,128)(2,1)} %get-tuple-element.51), channel_id=1, source_target_pairs={{0,24},{8,16},{16,8},{24,0},{1,25},{9,17},{17,9},{25,1},{2,26},{10... | collective-permute-start | bytes 602120 | tf_op jit(solution)/shard_map/ppermute | solution.py:577
  213.6 12.0 %copy-start.10 = (bf16[1,784,128]{2,1,0:T(8,128)(2,1)}, bf16[1,784,128]{2,1,0:T(8,128)(2,1)S(1)}, u32[]{:S(2)}) copy-start(bf16[1,784,128]{2,1,0:T(8,128)(2,1)S(1)} %collective-permute-done.9.refs_2_) | copy-start | bytes 602116
  213.6 12.0 %copy-start.11 = (bf16[1,784,128]{2,1,0:T(8,128)(2,1)}, bf16[1,784,128]{2,1,0:T(8,128)(2,1)S(1)}, u32[]{:S(2)}) copy-start(bf16[1,784,128]{2,1,0:T(8,128)(2,1)S(1)} %collective-permute-done.10.refs_3_) | copy-start | bytes 602116
  214.4 62.8 %all-to-all-start.2 = ((bf16[8,4,4,2,64,128]{5,4,3,2,1,0:T(8,128)(2,1)}), bf16[8,4,4,2,64,128]{5,4,3,2,1,0:T(8,128)(2,1)}, u32[]{:S(2)}, u32[]{:S(2)}) async-start(bf16[8,4,4,2,64,128]{5,4,3,2,1,0:T(8,128)(2,1)} %shard_map.77), calls=%async_computation.2 | async-start | bytes 8388608 | tf_op jit(solution)/shard_map/all_to_all | solution.py:581
  220.4 41.9 %collective-permute-start.12 = (bf16[3,784,128]{2,1,0:T(8,128)(2,1)}, bf16[3,784,128]{2,1,0:T(8,128)(2,1)S(1)}, u32[]{:S(2)}, u32[]{:S(2)}) collective-permute-start(bf16[3,784,128]{2,1,0:T(8,128)(2,1)} %get-tuple-element.55), channel_id=1, source_target_pairs={{0,16},{8,24},{16,0},{24,8},{1,17},{9,25},{17,1},{25,9},{2,18},{10... | collective-permute-start | bytes 1806344 | tf_op jit(solution)/shard_map/ppermute | solution.py:577
  224.1 52.9 %collective-permute-start.13 = (bf16[3,784,128]{2,1,0:T(8,128)(2,1)}, bf16[3,784,128]{2,1,0:T(8,128)(2,1)S(1)}, u32[]{:S(2)}, u32[]{:S(2)}) collective-permute-start(bf16[3,784,128]{2,1,0:T(8,128)(2,1)} %get-tuple-element.56), channel_id=1, source_target_pairs={{0,24},{8,16},{16,8},{24,0},{1,25},{9,17},{17,9},{25,1},{2,26},{10... | collective-permute-start | bytes 1806344 | tf_op jit(solution)/shard_map/ppermute | solution.py:577
  224.6 62.9 %collective-permute-start.11 = (bf16[4,3,2,2,64,128]{5,4,3,2,1,0:T(8,128)(2,1)}, bf16[4,3,2,2,64,128]{5,4,3,2,1,0:T(8,128)(2,1)S(1)}, u32[]{:S(2)}, u32[]{:S(2)}) collective-permute-start(bf16[4,3,2,2,64,128]{5,4,3,2,1,0:T(8,128)(2,1)} %get-tuple-element.54), channel_id=1, source_target_pairs={{0,8},{8,0},{16,24},{24,16},{1,9},{9,1},{17,25},{25,17},{2,10},{10... | collective-permute-start | bytes 2359304 | tf_op jit(solution)/shard_map/ppermute | solution.py:577
  262.2 25.3 %copy-start.2 = (bf16[3,784,128]{2,1,0:T(8,128)(2,1)}, bf16[3,784,128]{2,1,0:T(8,128)(2,1)S(1)}, u32[]{:S(2)}) copy-start(bf16[3,784,128]{2,1,0:T(8,128)(2,1)S(1)} %collective-permute-done.12.refs_6_) | copy-start | bytes 1806340
  277.0 10.6 %copy-start.3 = (bf16[3,784,128]{2,1,0:T(8,128)(2,1)}, bf16[3,784,128]{2,1,0:T(8,128)(2,1)S(1)}, u32[]{:S(2)}) copy-start(bf16[3,784,128]{2,1,0:T(8,128)(2,1)S(1)} %collective-permute-done.13.refs_7_) | copy-start | bytes 1806340
  277.1 10.5 %collective-permute-start.14 = (bf16[2,4,128,128]{3,2,1,0:T(8,128)(2,1)S(1)}, bf16[2,4,128,128]{3,2,1,0:T(8,128)(2,1)S(1)}, u32[]{:S(2)}, u32[]{:S(2)}) collective-permute-start(bf16[2,4,128,128]{3,2,1,0:T(8,128)(2,1)S(1)} %pad_maximum_fusion.2), channel_id=1, source_target_pairs={{0,8},{8,0},{16,24},{24,16},{1,9},{9,1},{17,25},{25,17},{2,10},{10... | collective-permute-start | bytes 786440 | tf_op jit(solution)/shard_map/ppermute | solution.py:577
  279.2 20.4 %collective-permute-start.17 = (bf16[8,1,2,64,128]{4,3,2,0,1:T(8,128)(2,1)S(1)}, bf16[8,1,2,64,128]{4,3,2,0,1:T(8,128)(2,1)S(1)}, u32[]{:S(2)}, u32[]{:S(2)}) collective-permute-start(bf16[8,1,2,64,128]{4,3,2,0,1:T(8,128)(2,1)S(1)} %get-tuple-element.62), channel_id=1, source_target_pairs={{0,24},{8,16},{16,8},{24,0},{1,25},{9,17},{17,9},{25,1},{2,26},{10... | collective-permute-start | bytes 786440 | tf_op jit(solution)/shard_map/ppermute | solution.py:577
  279.7 22.6 %collective-permute-start.16 = (bf16[8,1,2,64,128]{4,3,2,0,1:T(8,128)(2,1)S(1)}, bf16[8,1,2,64,128]{4,3,2,0,1:T(8,128)(2,1)S(1)}, u32[]{:S(2)}, u32[]{:S(2)}) collective-permute-start(bf16[8,1,2,64,128]{4,3,2,0,1:T(8,128)(2,1)S(1)} %get-tuple-element.63), channel_id=1, source_target_pairs={{0,16},{8,24},{16,0},{24,8},{1,17},{9,25},{17,1},{25,9},{2,18},{10... | collective-permute-start | bytes 786440 | tf_op jit(solution)/shard_map/ppermute | solution.py:577
  283.5 18.8 %collective-permute-start.15 = (bf16[8,1,2,64,128]{4,3,2,0,1:T(8,128)(2,1)S(1)}, bf16[8,1,2,64,128]{4,3,2,0,1:T(8,128)(2,1)S(1)}, u32[]{:S(2)}, u32[]{:S(2)}) collective-permute-start(bf16[8,1,2,64,128]{4,3,2,0,1:T(8,128)(2,1)S(1)} %get-tuple-element.64), channel_id=1, source_target_pairs={{0,8},{8,0},{16,24},{24,16},{1,9},{9,1},{17,25},{25,17},{2,10},{10... | collective-permute-start | bytes 786440 | tf_op jit(solution)/shard_map/ppermute | solution.py:577
  303.2 78.2 %all-to-all-start.3 = ((bf16[8,4,4,2,64,128]{5,4,3,2,1,0:T(8,128)(2,1)}), bf16[8,4,4,2,64,128]{5,4,3,2,1,0:T(8,128)(2,1)}, u32[]{:S(2)}, u32[]{:S(2)}) async-start(bf16[8,4,4,2,64,128]{5,4,3,2,1,0:T(8,128)(2,1)} %shard_map.79), calls=%async_computation.3 | async-start | bytes 8388608 | tf_op jit(solution)/shard_map/all_to_all | solution.py:581
  308.0 36.5 %collective-permute-start.18 = (bf16[8,3,2,64,128]{4,3,2,1,0:T(8,128)(2,1)}, bf16[8,3,2,64,128]{4,3,2,1,0:T(8,128)(2,1)S(1)}, u32[]{:S(2)}, u32[]{:S(2)}) collective-permute-start(bf16[8,3,2,64,128]{4,3,2,1,0:T(8,128)(2,1)} %get-tuple-element.58), channel_id=1, source_target_pairs={{0,8},{8,0},{16,24},{24,16},{1,9},{9,1},{17,25},{25,17},{2,10},{10... | collective-permute-start | bytes 2359304 | tf_op jit(solution)/shard_map/ppermute | solution.py:577
  311.5 52.0 %collective-permute-start.19 = (bf16[8,3,2,64,128]{4,3,2,1,0:T(8,128)(2,1)}, bf16[8,3,2,64,128]{4,3,2,1,0:T(8,128)(2,1)S(1)}, u32[]{:S(2)}, u32[]{:S(2)}) collective-permute-start(bf16[8,3,2,64,128]{4,3,2,1,0:T(8,128)(2,1)} %get-tuple-element.59), channel_id=1, source_target_pairs={{0,16},{8,24},{16,0},{24,8},{1,17},{9,25},{17,1},{25,9},{2,18},{10... | collective-permute-start | bytes 2359304 | tf_op jit(solution)/shard_map/ppermute | solution.py:577
  311.5 69.8 %collective-permute-start.20 = (bf16[8,3,2,64,128]{4,3,2,1,0:T(8,128)(2,1)}, bf16[8,3,2,64,128]{4,3,2,1,0:T(8,128)(2,1)S(1)}, u32[]{:S(2)}, u32[]{:S(2)}) collective-permute-start(bf16[8,3,2,64,128]{4,3,2,1,0:T(8,128)(2,1)} %get-tuple-element.60), channel_id=1, source_target_pairs={{0,24},{8,16},{16,8},{24,0},{1,25},{9,17},{17,9},{25,1},{2,26},{10... | collective-permute-start | bytes 2359304 | tf_op jit(solution)/shard_map/ppermute | solution.py:577
  344.5 36.8 %copy-start.5 = (bf16[8,3,2,64,128]{4,3,2,1,0:T(8,128)(2,1)}, bf16[8,3,2,64,128]{4,3,2,1,0:T(8,128)(2,1)S(1)}, u32[]{:S(2)}) copy-start(bf16[8,3,2,64,128]{4,3,2,1,0:T(8,128)(2,1)S(1)} %collective-permute-done.18) | copy-start | bytes 2359300
  363.4 17.9 %copy-start.6 = (bf16[8,3,2,64,128]{4,3,2,1,0:T(8,128)(2,1)}, bf16[8,3,2,64,128]{4,3,2,1,0:T(8,128)(2,1)S(1)}, u32[]{:S(2)}) copy-start(bf16[8,3,2,64,128]{4,3,2,1,0:T(8,128)(2,1)S(1)} %collective-permute-done.19) | copy-start | bytes 2359300
  (13 other events, 21.4 us)

commit v6 on v5

--- a/solution.py
+++ b/solution.py
@@ -649,8 +649,8 @@
     rows1 = [sent1[0], swapped(sent1[1], 1), first, others]
     rows1 += [swapped(sent1[d + 1], d) for d in range(3, n)]
     parts = [part.reshape(2 * n, 1, sizes[0], 2, half, src_tiles) for part in early]
-    joined = jnp.concatenate([gate(part, sent1[0], first) for part in parts], axis=1)
-    moved0 = spread(joined)
+    joined = jnp.concatenate([gate(part, sent1[0]) for part in parts], axis=1)
+    moved0 = spread(gate(joined, first))
     rest0 = predict(place, coeffs[0], [moved0], n, True, False, 1, sizes[0], sent1[0])
     sent0 = rest0[0]
     first0 = predict(place, coeffs[0], [moved0], n, True, False, 0, 1, sent0)

time: 393 us -> 389 us (0.990)
  transfers between devices with their start and end apart: 25 -> 25, of which waited for: 11 -> 11; matrix products, arithmetic and copies ran while one was open for 1% -> 2% of each run, Pallas kernels for 12% -> 12%
where the time goes in v6:
time: 389 us; the launch traced here: 388 us
  waiting for transfers between devices  259 us (67%)
  Pallas kernels  67.9 us (17%)
  starting transfers between devices  47.7 us (12%)
  local copies, waits for them, and re-layouts  8.74 us (2%)
  other arithmetic  4.49 us (1%)
    ppermute x21, waiting for transfers between devices, swapped(): return lax.ppermute(value, 'src', [(i, i ^ gap) for i in range(size)])  172 us
    all_to_all x4, waiting for transfers between devices, spread(): return lax.all_to_all(value, 'rcv', split_axis=0, concat_axis=0, tiled=True)  87.6 us
    pallas_call x3, Pallas kernels, predict(): pl.pallas_call(kernel, grid=(freqs,), in_specs=[IN_SMEM, IN_SMEM, UNREAD]...  34.7 us
    ppermute x21, starting transfers between devices, swapped(): return lax.ppermute(value, 'src', [(i, i ^ gap) for i in range(size)])  27.2 us
    all_to_all x4, starting transfers between devices, spread(): return lax.all_to_all(value, 'rcv', split_axis=0, concat_axis=0, tiled=True)  20.5 us
    pallas_call x1, Pallas kernels, inverse_dft(): pl.pallas_call(kernel, grid=(half // ROWS,), in_specs=[IN_SMEM] + [pl.Blo...  10.2 us
    pallas_call x1, Pallas kernels, forward_dft(): pl.pallas_call(kernel, grid=(half // ROWS,), in_specs=[IN_SMEM, UNREAD] +...  9.49 us
  transfers between devices with their start and end apart: 25, of which 11 were waited for; matrix products, arithmetic and copies ran while one was open for 2% of the time, Pallas kernels for 12%

profile of v6, /device:TPU:10, one launch (start us, length us, event | category | flops | bytes accessed | tf_op | source)
XLA Modules:
  0.0 388.2 jit_solution(16784510781354401945)
XLA Ops:
  0.0 9.5 %shard_map.73 = (bf16[64,64,128]{2,1,0:T(8,128)(2,1)}, bf16[64,64,128]{2,1,0:T(8,128)(2,1)}, bf16[64,64,128]{2,1,0:T(8,128)(2,1)}, bf16[64,64,128]{2,1,0:T(8,128)(2,1)}, bf16[256,64,128]{2,1,0:T(8,128)(2,1)}) custom-call(s32[1]{0:T(128)} %bitcast.place_ref.after_ref, s32[1]{0:T(128)} %bitcast.place_ref.after_ref, ...), custom_call_target="tpu_custom_call" | custom-call | tf_op jit(solution)/shard_map/pallas_call | solution.py:170
  9.5 5.0 %all-to-all-start = ((bf16[8,4,4,2,64,128]{5,4,3,2,1,0:T(8,128)(2,1)}), bf16[8,4,4,2,64,128]{5,4,3,2,1,0:T(8,128)(2,1)}, u32[]{:S(2)}, u32[]{:S(2)}) async-start(bf16[8,4,4,2,64,128]{5,4,3,2,1,0:T(8,128)(2,1)} %bitcast.32), calls=%async_computation | async-start | bytes 8388608 | tf_op jit(solution)/shard_map/all_to_all | solution.py:581
  14.5 3.0 collective-permute-start.2
  17.9 44.2 %all-to-all-done.moved_ref = bf16[8,4,4,2,64,128]{5,4,3,2,1,0:T(8,128)(2,1)} async-done(((bf16[8,4,4,2,64,128]{5,4,3,2,1,0:T(8,128)(2,1)}), bf16[8,4,4,2,64,128]{5,4,3,2,1,0:T(8,128)(2,1)}, u32[]{:S(2)}, u32[]{:S(2)}) %all-to-all-start) | async-done | bytes 4194336 | tf_op jit(solution)/shard_map/all_to_all | solution.py:581
  63.3 27.9 %collective-permute-done.pairs_ref = bf16[2,2,4,64,128]{4,3,2,1,0:T(8,128)(2,1)S(1)} collective-permute-done((bf16[2,2,4,64,128]{4,3,2,1,0:T(8,128)(2,1)S(1)}, bf16[2,2,4,64,128]{4,3,2,1,0:T(8,128)(2,1)S(1)}, u32[]{:S(2)}, u32[]{:S(2)}) %collective-permute-start) | collective-permute-done | bytes 262176 | tf_op jit(solution)/shard_map/ppermute | solution.py:577
  91.8 4.6 %shard_map.74 = (bf16[4,4,2,2,64,128]{5,4,3,2,1,0:T(8,128)(2,1)}, bf16[4,4,2,2,64,128]{5,4,3,2,1,0:T(8,128)(2,1)}, bf16[1,784,128]{2,1,0:T(8,128)(2,1)}, bf16[3,...) custom-call(s32[1]{0:T(128)} %bitcast.place_ref.after_ref, s32[1]{0:T(128)} %bitcast.place_ref.after_ref, ...), custom_call_target="tpu_custom_call" | custom-call | tf_op jit(solution)/shard_map/pallas_call | solution.py:486
  96.5 3.0 collective-permute-start.4
  99.5 14.6 %collective-permute-done.3 = bf16[64,64,128]{2,1,0:T(8,128)(2,1)} collective-permute-done((bf16[64,64,128]{2,1,0:T(8,128)(2,1)}, bf16[64,64,128]{2,1,0:T(8,128)(2,1)}, u32[]{:S(2)}, u32[]{:S(2)}) %collective-permute-start.3) | collective-permute-done | bytes 1048608 | tf_op jit(solution)/shard_map/ppermute | solution.py:577
  114.0 3.3 pad_maximum_fusion
  117.3 4.8 %all-to-all-start.1 = ((bf16[8,4,4,2,64,128]{5,4,3,2,1,0:T(8,128)(2,1)}), bf16[8,4,4,2,64,128]{5,4,3,2,1,0:T(8,128)(2,1)}, u32[]{:S(2)}, u32[]{:S(2)}) async-start(bf16[8,4,4,2,64,128]{5,4,3,2,1,0:T(8,128)(2,1)} %pad_maximum_fusion), calls=%async_computation.1 | async-start | bytes 8388608 | tf_op jit(solution)/shard_map/all_to_all | solution.py:581
  123.5 1.8 collective-permute-start.6
  126.5 43.4 %all-to-all-done.1.refs_0_ = bf16[8,4,4,2,64,128]{5,4,3,2,1,0:T(8,128)(2,1)} async-done(((bf16[8,4,4,2,64,128]{5,4,3,2,1,0:T(8,128)(2,1)}), bf16[8,4,4,2,64,128]{5,4,3,2,1,0:T(8,128)(2,1)}, u32[]{:S(2)}, u32[]{:S(2)}) %all-to-all-start.1) | async-done | bytes 4194336 | tf_op jit(solution)/shard_map/all_to_all | solution.py:581
  169.9 12.5 %shard_map.75 = (bf16[4,3,2,2,64,128]{5,4,3,2,1,0:T(8,128)(2,1)}, bf16[4,3,2,2,64,128]{5,4,3,2,1,0:T(8,128)(2,1)}, bf16[3,784,128]{2,1,0:T(8,128)(2,1)}, bf16[3,784,128]{2,1,0:T(8,128)(2,1)}) custom-call(s32[1]{0:T(128)} %bitcast.place_ref.after_ref, f32[4,2]{1,0:T(4,128)} %broadcast_multiply_fusion.coeff_ref, ...), custom_call_target="tpu_custom_call" | custom-call | tf_op jit(solution)/shard_map/pallas_call | solution.py:435
  182.4 5.4 %shard_map.76 = (bf16[4,1,2,2,64,128]{5,4,3,2,1,0:T(8,128)(2,1)}, bf16[4,1,2,2,64,128]{5,4,3,2,1,0:T(8,128)(2,1)}, bf16[1,784,128]{2,1,0:T(8,128)(2,1)}, bf16[1,784,128]{2,1,0:T(8,128)(2,1)}) custom-call(s32[1]{0:T(128)} %bitcast.place_ref.after_ref, f32[4,2]{1,0:T(4,128)} %broadcast_multiply_fusion.coeff_ref, ...), custom_call_target="tpu_custom_call" | custom-call | tf_op jit(solution)/shard_map/pallas_call | solution.py:435
  189.3 1.7 collective-permute-start.9
  193.2 16.8 %shard_map.77 = bf16[8,4,4,2,64,128]{5,4,3,2,1,0:T(8,128)(2,1)} custom-call(s32[1]{0:T(128)} %bitcast.place_ref.after_ref, f32[4,2]{1,0:T(4,128)} %broadcast_multiply_fusion.1.coeff_ref, bf16[4,1,2,2,64,128]{5,4,3,2,1,0:T(8,128)(2,1)} %get-tuple-element.47.after_ref.refs_0_, bf16[4,4,2,2,64,128]{5,4,3,2,1,0:T(8,128)(2,1)} %get-tuple-element.35.after_ref.refs_0_, ...), custom_call_target="tpu_custom_call" | custom-call | tf_op jit(solution)/shard_map/pallas_call | solution.py:435
  210.8 6.0 %all-to-all-start.2 = ((bf16[8,4,4,2,64,128]{5,4,3,2,1,0:T(8,128)(2,1)}), bf16[8,4,4,2,64,128]{5,4,3,2,1,0:T(8,128)(2,1)}, u32[]{:S(2)}, u32[]{:S(2)}) async-start(bf16[8,4,4,2,64,128]{5,4,3,2,1,0:T(8,128)(2,1)} %shard_map.77), calls=%async_computation.2 | async-start | bytes 8388608 | tf_op jit(solution)/shard_map/all_to_all | solution.py:581
  216.7 3.3 collective-permute-start.12
  221.5 37.1 %collective-permute-done.12.refs_6_ = bf16[3,784,128]{2,1,0:T(8,128)(2,1)S(1)} collective-permute-done((bf16[3,784,128]{2,1,0:T(8,128)(2,1)}, bf16[3,784,128]{2,1,0:T(8,128)(2,1)S(1)}, u32[]{:S(2)}, u32[]{:S(2)}) %collective-permute-start.12) | collective-permute-done | bytes 602144 | tf_op jit(solution)/shard_map/ppermute | solution.py:577
  258.6 14.2 %collective-permute-done.13.refs_7_ = bf16[3,784,128]{2,1,0:T(8,128)(2,1)S(1)} collective-permute-done((bf16[3,784,128]{2,1,0:T(8,128)(2,1)}, bf16[3,784,128]{2,1,0:T(8,128)(2,1)S(1)}, u32[]{:S(2)}, u32[]{:S(2)}) %collective-permute-start.13) | collective-permute-done | bytes 602144 | tf_op jit(solution)/shard_map/ppermute | solution.py:577
  273.0 2.1 fusion
  276.0 3.4 collective-permute-start.16
  279.4 3.9 %shard_map.78 = (bf16[8,3,2,64,128]{4,3,2,1,0:T(8,128)(2,1)}, bf16[8,3,2,64,128]{4,3,2,1,0:T(8,128)(2,1)}, bf16[8,3,2,64,128]{4,3,2,1,0:T(8,128)(2,1)}, bf16[8,3,2,64,128]{4,3,2,1,0:T(8,128)(2,1)}) custom-call(bf16[8,4,4,2,64,128]{5,4,3,2,1,0:T(8,128)(2,1)} %all-to-all-done.2.moved_ref), custom_call_target="tpu_custom_call" | custom-call | tf_op jit(solution)/shard_map/pallas_call | solution.py:557
  284.4 5.0 %shard_map.79 = bf16[8,4,4,2,64,128]{5,4,3,2,1,0:T(8,128)(2,1)} custom-call(s32[1]{0:T(128)} %bitcast.place_ref.after_ref, bf16[8,3,2,64,128]{4,3,2,1,0:T(8,128)(2,1)} %get-tuple-element.55.after_ref, bf16[4,1,2,2,64,128]{5,4,3,2,1,0:T(8,128)(2,1)} %get-tuple-element.47.after_ref.refs_0_, bf16[4,1,2,2,64,128]{5,4,3,2,1,0:T(8,128)(2,1)} %copy-done.15, ...), custom_call_target="tpu_custom_call" | custom-call | tf_op jit(solution)/shard_map/pallas_call | solution.py:539
  289.3 6.2 %collective-permute-done.17 = bf16[8,1,2,64,128]{4,3,2,0,1:T(8,128)(2,1)S(1)} collective-permute-done((bf16[8,1,2,64,128]{4,3,2,0,1:T(8,128)(2,1)S(1)}, bf16[8,1,2,64,128]{4,3,2,0,1:T(8,128)(2,1)S(1)}, u32[]{:S(2)}, u32[]{:S(2)}) %collective-permute-start.17) | collective-permute-done | bytes 262176 | tf_op jit(solution)/shard_map/ppermute | solution.py:577
  295.5 3.1 collective-permute-done.16
  299.5 4.8 %all-to-all-start.3 = ((bf16[8,4,4,2,64,128]{5,4,3,2,1,0:T(8,128)(2,1)}), bf16[8,4,4,2,64,128]{5,4,3,2,1,0:T(8,128)(2,1)}, u32[]{:S(2)}, u32[]{:S(2)}) async-start(bf16[8,4,4,2,64,128]{5,4,3,2,1,0:T(8,128)(2,1)} %shard_map.79), calls=%async_computation.3 | async-start | bytes 8388608 | tf_op jit(solution)/shard_map/all_to_all | solution.py:581
  304.3 3.0 collective-permute-start.18
  308.8 32.0 %collective-permute-done.18 = bf16[8,3,2,64,128]{4,3,2,1,0:T(8,128)(2,1)S(1)} collective-permute-done((bf16[8,3,2,64,128]{4,3,2,1,0:T(8,128)(2,1)}, bf16[8,3,2,64,128]{4,3,2,1,0:T(8,128)(2,1)S(1)}, u32[]{:S(2)}, u32[]{:S(2)}) %collective-permute-start.18) | collective-permute-done | bytes 786464 | tf_op jit(solution)/shard_map/ppermute | solution.py:577
  340.8 18.8 %collective-permute-done.19 = bf16[8,3,2,64,128]{4,3,2,1,0:T(8,128)(2,1)S(1)} collective-permute-done((bf16[8,3,2,64,128]{4,3,2,1,0:T(8,128)(2,1)}, bf16[8,3,2,64,128]{4,3,2,1,0:T(8,128)(2,1)S(1)}, u32[]{:S(2)}, u32[]{:S(2)}) %collective-permute-start.19) | collective-permute-done | bytes 786464 | tf_op jit(solution)/shard_map/ppermute | solution.py:577
  359.6 17.5 %collective-permute-done.20 = bf16[8,3,2,64,128]{4,3,2,1,0:T(8,128)(2,1)S(1)} collective-permute-done((bf16[8,3,2,64,128]{4,3,2,1,0:T(8,128)(2,1)}, bf16[8,3,2,64,128]{4,3,2,1,0:T(8,128)(2,1)S(1)}, u32[]{:S(2)}, u32[]{:S(2)}) %collective-permute-start.20) | collective-permute-done | bytes 786464 | tf_op jit(solution)/shard_map/ppermute | solution.py:577
  378.0 10.2 %shard_map.80 = bf16[2,64,64,512]{3,2,1,0:T(8,128)(2,1)} custom-call(s32[1]{0:T(128)} %bitcast.place_ref.after_ref, bf16[1,256,512]{2,1,0:T(8,128)(2,1)} %constant.52.clone.refs_0_, bf16[4,16,512]{2,1,0:T(8,128)(2,1)} %constant.53.clone.refs_1_, bf16[4,48,512]{2,1,0:T(8,128)(2,1)} %constant.54.clone.refs_2_, bf16[256,64,128]{2,1,0:T(8,128)(2,1)} %bitcast.14.refs_3_, ...), custom_call_target="tpu_custom_call" | custom-call | tf_op jit(solution)/shard_map/pallas_call | solution.py:223
  (80 shorter events, 16.0 us)
Async XLA Ops:
  9.5 52.7 %all-to-all-start = ((bf16[8,4,4,2,64,128]{5,4,3,2,1,0:T(8,128)(2,1)}), bf16[8,4,4,2,64,128]{5,4,3,2,1,0:T(8,128)(2,1)}, u32[]{:S(2)}, u32[]{:S(2)}) async-start(bf16[8,4,4,2,64,128]{5,4,3,2,1,0:T(8,128)(2,1)} %bitcast.32), calls=%async_computation | async-start | bytes 8388608 | tf_op jit(solution)/shard_map/all_to_all | solution.py:581
  14.5 99.6 %copy-start.1 = (bf16[64,64,128]{2,1,0:T(8,128)(2,1)S(1)}, bf16[64,64,128]{2,1,0:T(8,128)(2,1)}, u32[]{:S(2)}) copy-start(bf16[64,64,128]{2,1,0:T(8,128)(2,1)} %get-tuple-element.36) | copy-start | bytes 3145732
  14.5 85.0 %collective-permute-start.1 = (bf16[64,64,128]{2,1,0:T(8,128)(2,1)}, bf16[64,64,128]{2,1,0:T(8,128)(2,1)S(1)}, u32[]{:S(2)}, u32[]{:S(2)}) collective-permute-start(bf16[64,64,128]{2,1,0:T(8,128)(2,1)} %get-tuple-element.38), channel_id=1, source_target_pairs={{0,8},{8,0},{16,24},{24,16},{1,9},{9,1},{17,25},{25,17},{2,10},{10... | collective-permute-start | bytes 3145736 | tf_op jit(solution)/shard_map/ppermute | solution.py:577
  14.5 84.9 %collective-permute-start.2 = (bf16[64,64,128]{2,1,0:T(8,128)(2,1)}, bf16[64,64,128]{2,1,0:T(8,128)(2,1)S(1)}, u32[]{:S(2)}, u32[]{:S(2)}) collective-permute-start(bf16[64,64,128]{2,1,0:T(8,128)(2,1)} %get-tuple-element.40), channel_id=1, source_target_pairs={{0,16},{8,24},{16,0},{24,8},{1,17},{9,25},{17,1},{25,9},{2,18},{10... | collective-permute-start | bytes 3145736 | tf_op jit(solution)/shard_map/ppermute | solution.py:577
  17.5 96.5 %collective-permute-start.3 = (bf16[64,64,128]{2,1,0:T(8,128)(2,1)}, bf16[64,64,128]{2,1,0:T(8,128)(2,1)}, u32[]{:S(2)}, u32[]{:S(2)}) collective-permute-start(bf16[64,64,128]{2,1,0:T(8,128)(2,1)} %get-tuple-element.42), channel_id=1, source_target_pairs={{0,24},{8,16},{16,8},{24,0},{1,25},{9,17},{17,9},{25,1},{2,26},{10... | collective-permute-start | bytes 3145736 | tf_op jit(solution)/shard_map/ppermute | solution.py:577
  63.2 27.9 %collective-permute-start = (bf16[2,2,4,64,128]{4,3,2,1,0:T(8,128)(2,1)S(1)}, bf16[2,2,4,64,128]{4,3,2,1,0:T(8,128)(2,1)S(1)}, u32[]{:S(2)}, u32[]{:S(2)}) collective-permute-start(bf16[2,2,4,64,128]{4,3,2,1,0:T(8,128)(2,1)S(1)} %pad_maximum_fusion.1), channel_id=1, source_target_pairs={{0,8},{8,0},{16,24},{24,16},{1,9},{9,1},{17,25},{25,17},{2,10},{10... | collective-permute-start | bytes 786440 | tf_op jit(solution)/shard_map/ppermute | solution.py:577
  96.5 20.9 %collective-permute-start.4 = (bf16[1,784,128]{2,1,0:T(8,128)(2,1)}, bf16[1,784,128]{2,1,0:T(8,128)(2,1)}, u32[]{:S(2)}, u32[]{:S(2)}) collective-permute-start(bf16[1,784,128]{2,1,0:T(8,128)(2,1)} %get-tuple-element.44), channel_id=1, source_target_pairs={{0,16},{8,24},{16,0},{24,8},{1,17},{9,25},{17,1},{25,9},{2,18},{10... | collective-permute-start | bytes 602120 | tf_op jit(solution)/shard_map/ppermute | solution.py:577
  117.3 52.5 %all-to-all-start.1 = ((bf16[8,4,4,2,64,128]{5,4,3,2,1,0:T(8,128)(2,1)}), bf16[8,4,4,2,64,128]{5,4,3,2,1,0:T(8,128)(2,1)}, u32[]{:S(2)}, u32[]{:S(2)}) async-start(bf16[8,4,4,2,64,128]{5,4,3,2,1,0:T(8,128)(2,1)} %pad_maximum_fusion), calls=%async_computation.1 | async-start | bytes 8388608 | tf_op jit(solution)/shard_map/all_to_all | solution.py:581
  122.2 69.8 %collective-permute-start.5 = (bf16[4,4,2,2,64,128]{5,4,3,2,1,0:T(8,128)(2,1)}, bf16[4,4,2,2,64,128]{5,4,3,2,1,0:T(8,128)(2,1)S(1)}, u32[]{:S(2)}, u32[]{:S(2)}) collective-permute-start(bf16[4,4,2,2,64,128]{5,4,3,2,1,0:T(8,128)(2,1)} %get-tuple-element.48), channel_id=1, source_target_pairs={{0,8},{8,0},{16,24},{24,16},{1,9},{9,1},{17,25},{25,17},{2,10},{10... | collective-permute-start | bytes 3145736 | tf_op jit(solution)/shard_map/ppermute | solution.py:577
  123.5 67.4 %collective-permute-start.6 = (bf16[3,784,128]{2,1,0:T(8,128)(2,1)}, bf16[3,784,128]{2,1,0:T(8,128)(2,1)S(1)}, u32[]{:S(2)}, u32[]{:S(2)}) collective-permute-start(bf16[3,784,128]{2,1,0:T(8,128)(2,1)} %get-tuple-element.49), channel_id=1, source_target_pairs={{0,16},{8,24},{16,0},{24,8},{1,17},{9,25},{17,1},{25,9},{2,18},{10... | collective-permute-start | bytes 1806344 | tf_op jit(solution)/shard_map/ppermute | solution.py:577
  125.3 66.6 %collective-permute-start.7 = (bf16[4,784,128]{2,1,0:T(8,128)(2,1)}, bf16[4,784,128]{2,1,0:T(8,128)(2,1)S(1)}, u32[]{:S(2)}, u32[]{:S(2)}) collective-permute-start(bf16[4,784,128]{2,1,0:T(8,128)(2,1)} %get-tuple-element.50), channel_id=1, source_target_pairs={{0,24},{8,16},{16,8},{24,0},{1,25},{9,17},{17,9},{25,1},{2,26},{10... | collective-permute-start | bytes 2408456 | tf_op jit(solution)/shard_map/ppermute | solution.py:577
  187.8 22.2 %collective-permute-start.8 = (bf16[4,1,2,2,64,128]{5,4,3,2,1,0:T(8,128)(2,1)}, bf16[4,1,2,2,64,128]{5,4,3,2,1,0:T(8,128)(2,1)S(1)}, u32[]{:S(2)}, u32[]{:S(2)}) collective-permute-start(bf16[4,1,2,2,64,128]{5,4,3,2,1,0:T(8,128)(2,1)} %get-tuple-element.51), channel_id=1, source_target_pairs={{0,8},{8,0},{16,24},{24,16},{1,9},{9,1},{17,25},{25,17},{2,10},{10... | collective-permute-start | bytes 786440 | tf_op jit(solution)/shard_map/ppermute | solution.py:577
  189.3 20.7 %collective-permute-start.9 = (bf16[1,784,128]{2,1,0:T(8,128)(2,1)}, bf16[1,784,128]{2,1,0:T(8,128)(2,1)S(1)}, u32[]{:S(2)}, u32[]{:S(2)}) collective-permute-start(bf16[1,784,128]{2,1,0:T(8,128)(2,1)} %get-tuple-element.52), channel_id=1, source_target_pairs={{0,16},{8,24},{16,0},{24,8},{1,17},{9,25},{17,1},{25,9},{2,18},{10... | collective-permute-start | bytes 602120 | tf_op jit(solution)/shard_map/ppermute | solution.py:577
  190.9 19.0 %collective-permute-start.10 = (bf16[1,784,128]{2,1,0:T(8,128)(2,1)}, bf16[1,784,128]{2,1,0:T(8,128)(2,1)S(1)}, u32[]{:S(2)}, u32[]{:S(2)}) collective-permute-start(bf16[1,784,128]{2,1,0:T(8,128)(2,1)} %get-tuple-element.53), channel_id=1, source_target_pairs={{0,24},{8,16},{16,8},{24,0},{1,25},{9,17},{17,9},{25,1},{2,26},{10... | collective-permute-start | bytes 602120 | tf_op jit(solution)/shard_map/ppermute | solution.py:577
  210.0 11.5 %copy-start.10 = (bf16[1,784,128]{2,1,0:T(8,128)(2,1)}, bf16[1,784,128]{2,1,0:T(8,128)(2,1)S(1)}, u32[]{:S(2)}) copy-start(bf16[1,784,128]{2,1,0:T(8,128)(2,1)S(1)} %collective-permute-done.9.refs_2_) | copy-start | bytes 602116
  210.0 11.5 %copy-start.11 = (bf16[1,784,128]{2,1,0:T(8,128)(2,1)}, bf16[1,784,128]{2,1,0:T(8,128)(2,1)S(1)}, u32[]{:S(2)}) copy-start(bf16[1,784,128]{2,1,0:T(8,128)(2,1)S(1)} %collective-permute-done.10.refs_3_) | copy-start | bytes 602116
  210.8 62.3 %all-to-all-start.2 = ((bf16[8,4,4,2,64,128]{5,4,3,2,1,0:T(8,128)(2,1)}), bf16[8,4,4,2,64,128]{5,4,3,2,1,0:T(8,128)(2,1)}, u32[]{:S(2)}, u32[]{:S(2)}) async-start(bf16[8,4,4,2,64,128]{5,4,3,2,1,0:T(8,128)(2,1)} %shard_map.77), calls=%async_computation.2 | async-start | bytes 8388608 | tf_op jit(solution)/shard_map/all_to_all | solution.py:581
  216.7 41.9 %collective-permute-start.12 = (bf16[3,784,128]{2,1,0:T(8,128)(2,1)}, bf16[3,784,128]{2,1,0:T(8,128)(2,1)S(1)}, u32[]{:S(2)}, u32[]{:S(2)}) collective-permute-start(bf16[3,784,128]{2,1,0:T(8,128)(2,1)} %get-tuple-element.57), channel_id=1, source_target_pairs={{0,16},{8,24},{16,0},{24,8},{1,17},{9,25},{17,1},{25,9},{2,18},{10... | collective-permute-start | bytes 1806344 | tf_op jit(solution)/shard_map/ppermute | solution.py:577
  220.0 52.9 %collective-permute-start.13 = (bf16[3,784,128]{2,1,0:T(8,128)(2,1)}, bf16[3,784,128]{2,1,0:T(8,128)(2,1)S(1)}, u32[]{:S(2)}, u32[]{:S(2)}) collective-permute-start(bf16[3,784,128]{2,1,0:T(8,128)(2,1)} %get-tuple-element.58), channel_id=1, source_target_pairs={{0,24},{8,16},{16,8},{24,0},{1,25},{9,17},{17,9},{25,1},{2,26},{10... | collective-permute-start | bytes 1806344 | tf_op jit(solution)/shard_map/ppermute | solution.py:577
  220.5 62.9 %collective-permute-start.11 = (bf16[4,3,2,2,64,128]{5,4,3,2,1,0:T(8,128)(2,1)}, bf16[4,3,2,2,64,128]{5,4,3,2,1,0:T(8,128)(2,1)S(1)}, u32[]{:S(2)}, u32[]{:S(2)}) collective-permute-start(bf16[4,3,2,2,64,128]{5,4,3,2,1,0:T(8,128)(2,1)} %get-tuple-element.56), channel_id=1, source_target_pairs={{0,8},{8,0},{16,24},{24,16},{1,9},{9,1},{17,25},{25,17},{2,10},{10... | collective-permute-start | bytes 2359304 | tf_op jit(solution)/shard_map/ppermute | solution.py:577
  258.6 24.8 %copy-start.2 = (bf16[3,784,128]{2,1,0:T(8,128)(2,1)}, bf16[3,784,128]{2,1,0:T(8,128)(2,1)S(1)}, u32[]{:S(2)}) copy-start(bf16[3,784,128]{2,1,0:T(8,128)(2,1)S(1)} %collective-permute-done.12.refs_6_) | copy-start | bytes 1806340
  272.9 10.5 %copy-start.3 = (bf16[3,784,128]{2,1,0:T(8,128)(2,1)}, bf16[3,784,128]{2,1,0:T(8,128)(2,1)S(1)}, u32[]{:S(2)}) copy-start(bf16[3,784,128]{2,1,0:T(8,128)(2,1)S(1)} %collective-permute-done.13.refs_7_) | copy-start | bytes 1806340
  273.0 10.4 %collective-permute-start.14 = (bf16[2,4,128,128]{3,2,1,0:T(8,128)(2,1)S(1)}, bf16[2,4,128,128]{3,2,1,0:T(8,128)(2,1)S(1)}, u32[]{:S(2)}, u32[]{:S(2)}) collective-permute-start(bf16[2,4,128,128]{3,2,1,0:T(8,128)(2,1)S(1)} %pad_maximum_fusion.2), channel_id=1, source_target_pairs={{0,8},{8,0},{16,24},{24,16},{1,9},{9,1},{17,25},{25,17},{2,10},{10... | collective-permute-start | bytes 786440 | tf_op jit(solution)/shard_map/ppermute | solution.py:577
  275.1 20.4 %collective-permute-start.17 = (bf16[8,1,2,64,128]{4,3,2,0,1:T(8,128)(2,1)S(1)}, bf16[8,1,2,64,128]{4,3,2,0,1:T(8,128)(2,1)S(1)}, u32[]{:S(2)}, u32[]{:S(2)}) collective-permute-start(bf16[8,1,2,64,128]{4,3,2,0,1:T(8,128)(2,1)S(1)} %get-tuple-element.64), channel_id=1, source_target_pairs={{0,24},{8,16},{16,8},{24,0},{1,25},{9,17},{17,9},{25,1},{2,26},{10... | collective-permute-start | bytes 786440 | tf_op jit(solution)/shard_map/ppermute | solution.py:577
  276.0 22.6 %collective-permute-start.16 = (bf16[8,1,2,64,128]{4,3,2,0,1:T(8,128)(2,1)S(1)}, bf16[8,1,2,64,128]{4,3,2,0,1:T(8,128)(2,1)S(1)}, u32[]{:S(2)}, u32[]{:S(2)}) collective-permute-start(bf16[8,1,2,64,128]{4,3,2,0,1:T(8,128)(2,1)S(1)} %get-tuple-element.65), channel_id=1, source_target_pairs={{0,16},{8,24},{16,0},{24,8},{1,17},{9,25},{17,1},{25,9},{2,18},{10... | collective-permute-start | bytes 786440 | tf_op jit(solution)/shard_map/ppermute | solution.py:577
  279.4 19.3 %collective-permute-start.15 = (bf16[8,1,2,64,128]{4,3,2,0,1:T(8,128)(2,1)S(1)}, bf16[8,1,2,64,128]{4,3,2,0,1:T(8,128)(2,1)S(1)}, u32[]{:S(2)}, u32[]{:S(2)}) collective-permute-start(bf16[8,1,2,64,128]{4,3,2,0,1:T(8,128)(2,1)S(1)} %get-tuple-element.66), channel_id=1, source_target_pairs={{0,8},{8,0},{16,24},{24,16},{1,9},{9,1},{17,25},{25,17},{2,10},{10... | collective-permute-start | bytes 786440 | tf_op jit(solution)/shard_map/ppermute | solution.py:577
  299.5 77.7 %all-to-all-start.3 = ((bf16[8,4,4,2,64,128]{5,4,3,2,1,0:T(8,128)(2,1)}), bf16[8,4,4,2,64,128]{5,4,3,2,1,0:T(8,128)(2,1)}, u32[]{:S(2)}, u32[]{:S(2)}) async-start(bf16[8,4,4,2,64,128]{5,4,3,2,1,0:T(8,128)(2,1)} %shard_map.79), calls=%async_computation.3 | async-start | bytes 8388608 | tf_op jit(solution)/shard_map/all_to_all | solution.py:581
  304.3 36.5 %collective-permute-start.18 = (bf16[8,3,2,64,128]{4,3,2,1,0:T(8,128)(2,1)}, bf16[8,3,2,64,128]{4,3,2,1,0:T(8,128)(2,1)S(1)}, u32[]{:S(2)}, u32[]{:S(2)}) collective-permute-start(bf16[8,3,2,64,128]{4,3,2,1,0:T(8,128)(2,1)} %get-tuple-element.60), channel_id=1, source_target_pairs={{0,8},{8,0},{16,24},{24,16},{1,9},{9,1},{17,25},{25,17},{2,10},{10... | collective-permute-start | bytes 2359304 | tf_op jit(solution)/shard_map/ppermute | solution.py:577
  307.3 52.3 %collective-permute-start.19 = (bf16[8,3,2,64,128]{4,3,2,1,0:T(8,128)(2,1)}, bf16[8,3,2,64,128]{4,3,2,1,0:T(8,128)(2,1)S(1)}, u32[]{:S(2)}, u32[]{:S(2)}) collective-permute-start(bf16[8,3,2,64,128]{4,3,2,1,0:T(8,128)(2,1)} %get-tuple-element.61), channel_id=1, source_target_pairs={{0,16},{8,24},{16,0},{24,8},{1,17},{9,25},{17,1},{25,9},{2,18},{10... | collective-permute-start | bytes 2359304 | tf_op jit(solution)/shard_map/ppermute | solution.py:577
  307.7 69.5 %collective-permute-start.20 = (bf16[8,3,2,64,128]{4,3,2,1,0:T(8,128)(2,1)}, bf16[8,3,2,64,128]{4,3,2,1,0:T(8,128)(2,1)S(1)}, u32[]{:S(2)}, u32[]{:S(2)}) collective-permute-start(bf16[8,3,2,64,128]{4,3,2,1,0:T(8,128)(2,1)} %get-tuple-element.62), channel_id=1, source_target_pairs={{0,24},{8,16},{16,8},{24,0},{1,25},{9,17},{17,9},{25,1},{2,26},{10... | collective-permute-start | bytes 2359304 | tf_op jit(solution)/shard_map/ppermute | solution.py:577
  340.8 36.4 %copy-start.5 = (bf16[8,3,2,64,128]{4,3,2,1,0:T(8,128)(2,1)}, bf16[8,3,2,64,128]{4,3,2,1,0:T(8,128)(2,1)S(1)}, u32[]{:S(2)}) copy-start(bf16[8,3,2,64,128]{4,3,2,1,0:T(8,128)(2,1)S(1)} %collective-permute-done.18) | copy-start | bytes 2359300
  359.6 17.5 %copy-start.6 = (bf16[8,3,2,64,128]{4,3,2,1,0:T(8,128)(2,1)}, bf16[8,3,2,64,128]{4,3,2,1,0:T(8,128)(2,1)S(1)}, u32[]{:S(2)}) copy-start(bf16[8,3,2,64,128]{4,3,2,1,0:T(8,128)(2,1)S(1)} %collective-permute-done.19) | copy-start | bytes 2359300
  (12 other events, 20.6 us)

commit v7 on v6

--- a/solution.py
+++ b/solution.py
@@ -100,7 +100,7 @@
 TN = (((0,), (0,)), ((), ()))
 VMEM_LIMIT = 56 * 2**20
 ROWS = 16
-BATCH = 4
+BATCH = 8
 WIDE = jnp.float32
 NARROW = jnp.bfloat16
 IN_VMEM = pl.BlockSpec(memory_space=pltpu.VMEM)

time: 389 us -> 389 us (level)
  no operation moved by 1% of the time
where the time goes in v7:
time: 389 us; the launch traced here: 388 us
  waiting for transfers between devices  259 us (67%)
  Pallas kernels  68 us (17%)
  starting transfers between devices  47.7 us (12%)
  local copies, waits for them, and re-layouts  8.74 us (2%)
  other arithmetic  4.49 us (1%)
    ppermute x21, waiting for transfers between devices, swapped(): return lax.ppermute(value, 'src', [(i, i ^ gap) for i in range(size)])  172 us
    all_to_all x4, waiting for transfers between devices, spread(): return lax.all_to_all(value, 'rcv', split_axis=0, concat_axis=0, tiled=True)  87.6 us
    pallas_call x3, Pallas kernels, predict(): pl.pallas_call(kernel, grid=(freqs,), in_specs=[IN_SMEM, IN_SMEM, UNREAD]...  34.7 us
    ppermute x21, starting transfers between devices, swapped(): return lax.ppermute(value, 'src', [(i, i ^ gap) for i in range(size)])  27.2 us
    all_to_all x4, starting transfers between devices, spread(): return lax.all_to_all(value, 'rcv', split_axis=0, concat_axis=0, tiled=True)  20.5 us
    pallas_call x1, Pallas kernels, inverse_dft(): pl.pallas_call(kernel, grid=(half // ROWS,), in_specs=[IN_SMEM] + [pl.Blo...  10.3 us
    pallas_call x1, Pallas kernels, forward_dft(): pl.pallas_call(kernel, grid=(half // ROWS,), in_specs=[IN_SMEM, UNREAD] +...  9.49 us
  transfers between devices with their start and end apart: 25, of which 11 were waited for; matrix products, arithmetic and copies ran while one was open for 2% of the time, Pallas kernels for 12%

profile of v7, /device:TPU:10, one launch (start us, length us, event | category | flops | bytes accessed | tf_op | source)
XLA Modules:
  0.0 388.3 jit_solution(3671509085233224403)
XLA Ops:
  0.0 9.5 %shard_map.73 = (bf16[64,64,128]{2,1,0:T(8,128)(2,1)}, bf16[64,64,128]{2,1,0:T(8,128)(2,1)}, bf16[64,64,128]{2,1,0:T(8,128)(2,1)}, bf16[64,64,128]{2,1,0:T(8,128)(2,1)}, bf16[256,64,128]{2,1,0:T(8,128)(2,1)}) custom-call(s32[1]{0:T(128)} %bitcast.place_ref.after_ref, s32[1]{0:T(128)} %bitcast.place_ref.after_ref, ...), custom_call_target="tpu_custom_call" | custom-call | tf_op jit(solution)/shard_map/pallas_call | solution.py:170
  9.5 5.0 %all-to-all-start = ((bf16[8,4,4,2,64,128]{5,4,3,2,1,0:T(8,128)(2,1)}), bf16[8,4,4,2,64,128]{5,4,3,2,1,0:T(8,128)(2,1)}, u32[]{:S(2)}, u32[]{:S(2)}) async-start(bf16[8,4,4,2,64,128]{5,4,3,2,1,0:T(8,128)(2,1)} %bitcast.32), calls=%async_computation | async-start | bytes 8388608 | tf_op jit(solution)/shard_map/all_to_all | solution.py:581
  14.5 3.0 collective-permute-start.2
  17.9 44.2 %all-to-all-done.moved_ref = bf16[8,4,4,2,64,128]{5,4,3,2,1,0:T(8,128)(2,1)} async-done(((bf16[8,4,4,2,64,128]{5,4,3,2,1,0:T(8,128)(2,1)}), bf16[8,4,4,2,64,128]{5,4,3,2,1,0:T(8,128)(2,1)}, u32[]{:S(2)}, u32[]{:S(2)}) %all-to-all-start) | async-done | bytes 4194336 | tf_op jit(solution)/shard_map/all_to_all | solution.py:581
  63.3 27.9 %collective-permute-done.pairs_ref = bf16[2,2,4,64,128]{4,3,2,1,0:T(8,128)(2,1)S(1)} collective-permute-done((bf16[2,2,4,64,128]{4,3,2,1,0:T(8,128)(2,1)S(1)}, bf16[2,2,4,64,128]{4,3,2,1,0:T(8,128)(2,1)S(1)}, u32[]{:S(2)}, u32[]{:S(2)}) %collective-permute-start) | collective-permute-done | bytes 262176 | tf_op jit(solution)/shard_map/ppermute | solution.py:577
  91.8 4.6 %shard_map.74 = (bf16[4,4,2,2,64,128]{5,4,3,2,1,0:T(8,128)(2,1)}, bf16[4,4,2,2,64,128]{5,4,3,2,1,0:T(8,128)(2,1)}, bf16[1,784,128]{2,1,0:T(8,128)(2,1)}, bf16[3,...) custom-call(s32[1]{0:T(128)} %bitcast.place_ref.after_ref, s32[1]{0:T(128)} %bitcast.place_ref.after_ref, ...), custom_call_target="tpu_custom_call" | custom-call | tf_op jit(solution)/shard_map/pallas_call | solution.py:486
  96.5 3.0 collective-permute-start.4
  99.5 14.6 %collective-permute-done.3 = bf16[64,64,128]{2,1,0:T(8,128)(2,1)} collective-permute-done((bf16[64,64,128]{2,1,0:T(8,128)(2,1)}, bf16[64,64,128]{2,1,0:T(8,128)(2,1)}, u32[]{:S(2)}, u32[]{:S(2)}) %collective-permute-start.3) | collective-permute-done | bytes 1048608 | tf_op jit(solution)/shard_map/ppermute | solution.py:577
  114.0 3.3 pad_maximum_fusion
  117.3 4.8 %all-to-all-start.1 = ((bf16[8,4,4,2,64,128]{5,4,3,2,1,0:T(8,128)(2,1)}), bf16[8,4,4,2,64,128]{5,4,3,2,1,0:T(8,128)(2,1)}, u32[]{:S(2)}, u32[]{:S(2)}) async-start(bf16[8,4,4,2,64,128]{5,4,3,2,1,0:T(8,128)(2,1)} %pad_maximum_fusion), calls=%async_computation.1 | async-start | bytes 8388608 | tf_op jit(solution)/shard_map/all_to_all | solution.py:581
  123.5 1.8 collective-permute-start.6
  126.5 43.4 %all-to-all-done.1.refs_0_ = bf16[8,4,4,2,64,128]{5,4,3,2,1,0:T(8,128)(2,1)} async-done(((bf16[8,4,4,2,64,128]{5,4,3,2,1,0:T(8,128)(2,1)}), bf16[8,4,4,2,64,128]{5,4,3,2,1,0:T(8,128)(2,1)}, u32[]{:S(2)}, u32[]{:S(2)}) %all-to-all-start.1) | async-done | bytes 4194336 | tf_op jit(solution)/shard_map/all_to_all | solution.py:581
  169.9 12.5 %shard_map.75 = (bf16[4,3,2,2,64,128]{5,4,3,2,1,0:T(8,128)(2,1)}, bf16[4,3,2,2,64,128]{5,4,3,2,1,0:T(8,128)(2,1)}, bf16[3,784,128]{2,1,0:T(8,128)(2,1)}, bf16[3,784,128]{2,1,0:T(8,128)(2,1)}) custom-call(s32[1]{0:T(128)} %bitcast.place_ref.after_ref, f32[4,2]{1,0:T(4,128)} %broadcast_multiply_fusion.coeff_ref, ...), custom_call_target="tpu_custom_call" | custom-call | tf_op jit(solution)/shard_map/pallas_call | solution.py:435
  182.4 5.4 %shard_map.76 = (bf16[4,1,2,2,64,128]{5,4,3,2,1,0:T(8,128)(2,1)}, bf16[4,1,2,2,64,128]{5,4,3,2,1,0:T(8,128)(2,1)}, bf16[1,784,128]{2,1,0:T(8,128)(2,1)}, bf16[1,784,128]{2,1,0:T(8,128)(2,1)}) custom-call(s32[1]{0:T(128)} %bitcast.place_ref.after_ref, f32[4,2]{1,0:T(4,128)} %broadcast_multiply_fusion.coeff_ref, ...), custom_call_target="tpu_custom_call" | custom-call | tf_op jit(solution)/shard_map/pallas_call | solution.py:435
  189.3 1.7 collective-permute-start.9
  193.2 16.8 %shard_map.77 = bf16[8,4,4,2,64,128]{5,4,3,2,1,0:T(8,128)(2,1)} custom-call(s32[1]{0:T(128)} %bitcast.place_ref.after_ref, f32[4,2]{1,0:T(4,128)} %broadcast_multiply_fusion.1.coeff_ref, bf16[4,1,2,2,64,128]{5,4,3,2,1,0:T(8,128)(2,1)} %get-tuple-element.47.after_ref.refs_0_, bf16[4,4,2,2,64,128]{5,4,3,2,1,0:T(8,128)(2,1)} %get-tuple-element.35.after_ref.refs_0_, ...), custom_call_target="tpu_custom_call" | custom-call | tf_op jit(solution)/shard_map/pallas_call | solution.py:435
  210.8 6.0 %all-to-all-start.2 = ((bf16[8,4,4,2,64,128]{5,4,3,2,1,0:T(8,128)(2,1)}), bf16[8,4,4,2,64,128]{5,4,3,2,1,0:T(8,128)(2,1)}, u32[]{:S(2)}, u32[]{:S(2)}) async-start(bf16[8,4,4,2,64,128]{5,4,3,2,1,0:T(8,128)(2,1)} %shard_map.77), calls=%async_computation.2 | async-start | bytes 8388608 | tf_op jit(solution)/shard_map/all_to_all | solution.py:581
  216.7 3.3 collective-permute-start.12
  221.5 37.1 %collective-permute-done.12.refs_6_ = bf16[3,784,128]{2,1,0:T(8,128)(2,1)S(1)} collective-permute-done((bf16[3,784,128]{2,1,0:T(8,128)(2,1)}, bf16[3,784,128]{2,1,0:T(8,128)(2,1)S(1)}, u32[]{:S(2)}, u32[]{:S(2)}) %collective-permute-start.12) | collective-permute-done | bytes 602144 | tf_op jit(solution)/shard_map/ppermute | solution.py:577
  258.6 14.2 %collective-permute-done.13.refs_7_ = bf16[3,784,128]{2,1,0:T(8,128)(2,1)S(1)} collective-permute-done((bf16[3,784,128]{2,1,0:T(8,128)(2,1)}, bf16[3,784,128]{2,1,0:T(8,128)(2,1)S(1)}, u32[]{:S(2)}, u32[]{:S(2)}) %collective-permute-start.13) | collective-permute-done | bytes 602144 | tf_op jit(solution)/shard_map/ppermute | solution.py:577
  273.0 2.1 fusion
  276.0 3.4 collective-permute-start.16
  279.4 3.9 %shard_map.78 = (bf16[8,3,2,64,128]{4,3,2,1,0:T(8,128)(2,1)}, bf16[8,3,2,64,128]{4,3,2,1,0:T(8,128)(2,1)}, bf16[8,3,2,64,128]{4,3,2,1,0:T(8,128)(2,1)}, bf16[8,3,2,64,128]{4,3,2,1,0:T(8,128)(2,1)}) custom-call(bf16[8,4,4,2,64,128]{5,4,3,2,1,0:T(8,128)(2,1)} %all-to-all-done.2.moved_ref), custom_call_target="tpu_custom_call" | custom-call | tf_op jit(solution)/shard_map/pallas_call | solution.py:557
  284.4 5.0 %shard_map.79 = bf16[8,4,4,2,64,128]{5,4,3,2,1,0:T(8,128)(2,1)} custom-call(s32[1]{0:T(128)} %bitcast.place_ref.after_ref, bf16[8,3,2,64,128]{4,3,2,1,0:T(8,128)(2,1)} %get-tuple-element.55.after_ref, bf16[4,1,2,2,64,128]{5,4,3,2,1,0:T(8,128)(2,1)} %get-tuple-element.47.after_ref.refs_0_, bf16[4,1,2,2,64,128]{5,4,3,2,1,0:T(8,128)(2,1)} %copy-done.15, ...), custom_call_target="tpu_custom_call" | custom-call | tf_op jit(solution)/shard_map/pallas_call | solution.py:539
  289.3 6.2 %collective-permute-done.17 = bf16[8,1,2,64,128]{4,3,2,0,1:T(8,128)(2,1)S(1)} collective-permute-done((bf16[8,1,2,64,128]{4,3,2,0,1:T(8,128)(2,1)S(1)}, bf16[8,1,2,64,128]{4,3,2,0,1:T(8,128)(2,1)S(1)}, u32[]{:S(2)}, u32[]{:S(2)}) %collective-permute-start.17) | collective-permute-done | bytes 262176 | tf_op jit(solution)/shard_map/ppermute | solution.py:577
  295.5 3.1 collective-permute-done.16
  299.5 4.8 %all-to-all-start.3 = ((bf16[8,4,4,2,64,128]{5,4,3,2,1,0:T(8,128)(2,1)}), bf16[8,4,4,2,64,128]{5,4,3,2,1,0:T(8,128)(2,1)}, u32[]{:S(2)}, u32[]{:S(2)}) async-start(bf16[8,4,4,2,64,128]{5,4,3,2,1,0:T(8,128)(2,1)} %shard_map.79), calls=%async_computation.3 | async-start | bytes 8388608 | tf_op jit(solution)/shard_map/all_to_all | solution.py:581
  304.3 3.0 collective-permute-start.18
  308.8 32.0 %collective-permute-done.18 = bf16[8,3,2,64,128]{4,3,2,1,0:T(8,128)(2,1)S(1)} collective-permute-done((bf16[8,3,2,64,128]{4,3,2,1,0:T(8,128)(2,1)}, bf16[8,3,2,64,128]{4,3,2,1,0:T(8,128)(2,1)S(1)}, u32[]{:S(2)}, u32[]{:S(2)}) %collective-permute-start.18) | collective-permute-done | bytes 786464 | tf_op jit(solution)/shard_map/ppermute | solution.py:577
  340.8 18.8 %collective-permute-done.19 = bf16[8,3,2,64,128]{4,3,2,1,0:T(8,128)(2,1)S(1)} collective-permute-done((bf16[8,3,2,64,128]{4,3,2,1,0:T(8,128)(2,1)}, bf16[8,3,2,64,128]{4,3,2,1,0:T(8,128)(2,1)S(1)}, u32[]{:S(2)}, u32[]{:S(2)}) %collective-permute-start.19) | collective-permute-done | bytes 786464 | tf_op jit(solution)/shard_map/ppermute | solution.py:577
  359.6 17.5 %collective-permute-done.20 = bf16[8,3,2,64,128]{4,3,2,1,0:T(8,128)(2,1)S(1)} collective-permute-done((bf16[8,3,2,64,128]{4,3,2,1,0:T(8,128)(2,1)}, bf16[8,3,2,64,128]{4,3,2,1,0:T(8,128)(2,1)S(1)}, u32[]{:S(2)}, u32[]{:S(2)}) %collective-permute-start.20) | collective-permute-done | bytes 786464 | tf_op jit(solution)/shard_map/ppermute | solution.py:577
  378.0 10.3 %shard_map.80 = bf16[2,64,64,512]{3,2,1,0:T(8,128)(2,1)} custom-call(s32[1]{0:T(128)} %bitcast.place_ref.after_ref, bf16[1,256,512]{2,1,0:T(8,128)(2,1)} %constant.52.clone.refs_0_, bf16[4,16,512]{2,1,0:T(8,128)(2,1)} %constant.53.clone.refs_1_, bf16[4,48,512]{2,1,0:T(8,128)(2,1)} %constant.54.clone.refs_2_, bf16[256,64,128]{2,1,0:T(8,128)(2,1)} %bitcast.14.refs_3_, ...), custom_call_target="tpu_custom_call" | custom-call | tf_op jit(solution)/shard_map/pallas_call | solution.py:223
  (80 shorter events, 16.0 us)
Async XLA Ops:
  9.5 52.7 %all-to-all-start = ((bf16[8,4,4,2,64,128]{5,4,3,2,1,0:T(8,128)(2,1)}), bf16[8,4,4,2,64,128]{5,4,3,2,1,0:T(8,128)(2,1)}, u32[]{:S(2)}, u32[]{:S(2)}) async-start(bf16[8,4,4,2,64,128]{5,4,3,2,1,0:T(8,128)(2,1)} %bitcast.32), calls=%async_computation | async-start | bytes 8388608 | tf_op jit(solution)/shard_map/all_to_all | solution.py:581
  14.5 99.6 %copy-start.1 = (bf16[64,64,128]{2,1,0:T(8,128)(2,1)S(1)}, bf16[64,64,128]{2,1,0:T(8,128)(2,1)}, u32[]{:S(2)}) copy-start(bf16[64,64,128]{2,1,0:T(8,128)(2,1)} %get-tuple-element.36) | copy-start | bytes 3145732
  14.5 85.0 %collective-permute-start.1 = (bf16[64,64,128]{2,1,0:T(8,128)(2,1)}, bf16[64,64,128]{2,1,0:T(8,128)(2,1)S(1)}, u32[]{:S(2)}, u32[]{:S(2)}) collective-permute-start(bf16[64,64,128]{2,1,0:T(8,128)(2,1)} %get-tuple-element.38), channel_id=1, source_target_pairs={{0,8},{8,0},{16,24},{24,16},{1,9},{9,1},{17,25},{25,17},{2,10},{10... | collective-permute-start | bytes 3145736 | tf_op jit(solution)/shard_map/ppermute | solution.py:577
  14.5 84.9 %collective-permute-start.2 = (bf16[64,64,128]{2,1,0:T(8,128)(2,1)}, bf16[64,64,128]{2,1,0:T(8,128)(2,1)S(1)}, u32[]{:S(2)}, u32[]{:S(2)}) collective-permute-start(bf16[64,64,128]{2,1,0:T(8,128)(2,1)} %get-tuple-element.40), channel_id=1, source_target_pairs={{0,16},{8,24},{16,0},{24,8},{1,17},{9,25},{17,1},{25,9},{2,18},{10... | collective-permute-start | bytes 3145736 | tf_op jit(solution)/shard_map/ppermute | solution.py:577
  17.5 96.5 %collective-permute-start.3 = (bf16[64,64,128]{2,1,0:T(8,128)(2,1)}, bf16[64,64,128]{2,1,0:T(8,128)(2,1)}, u32[]{:S(2)}, u32[]{:S(2)}) collective-permute-start(bf16[64,64,128]{2,1,0:T(8,128)(2,1)} %get-tuple-element.42), channel_id=1, source_target_pairs={{0,24},{8,16},{16,8},{24,0},{1,25},{9,17},{17,9},{25,1},{2,26},{10... | collective-permute-start | bytes 3145736 | tf_op jit(solution)/shard_map/ppermute | solution.py:577
  63.2 27.9 %collective-permute-start = (bf16[2,2,4,64,128]{4,3,2,1,0:T(8,128)(2,1)S(1)}, bf16[2,2,4,64,128]{4,3,2,1,0:T(8,128)(2,1)S(1)}, u32[]{:S(2)}, u32[]{:S(2)}) collective-permute-start(bf16[2,2,4,64,128]{4,3,2,1,0:T(8,128)(2,1)S(1)} %pad_maximum_fusion.1), channel_id=1, source_target_pairs={{0,8},{8,0},{16,24},{24,16},{1,9},{9,1},{17,25},{25,17},{2,10},{10... | collective-permute-start | bytes 786440 | tf_op jit(solution)/shard_map/ppermute | solution.py:577
  96.5 20.9 %collective-permute-start.4 = (bf16[1,784,128]{2,1,0:T(8,128)(2,1)}, bf16[1,784,128]{2,1,0:T(8,128)(2,1)}, u32[]{:S(2)}, u32[]{:S(2)}) collective-permute-start(bf16[1,784,128]{2,1,0:T(8,128)(2,1)} %get-tuple-element.44), channel_id=1, source_target_pairs={{0,16},{8,24},{16,0},{24,8},{1,17},{9,25},{17,1},{25,9},{2,18},{10... | collective-permute-start | bytes 602120 | tf_op jit(solution)/shard_map/ppermute | solution.py:577
  117.3 52.5 %all-to-all-start.1 = ((bf16[8,4,4,2,64,128]{5,4,3,2,1,0:T(8,128)(2,1)}), bf16[8,4,4,2,64,128]{5,4,3,2,1,0:T(8,128)(2,1)}, u32[]{:S(2)}, u32[]{:S(2)}) async-start(bf16[8,4,4,2,64,128]{5,4,3,2,1,0:T(8,128)(2,1)} %pad_maximum_fusion), calls=%async_computation.1 | async-start | bytes 8388608 | tf_op jit(solution)/shard_map/all_to_all | solution.py:581
  122.2 69.8 %collective-permute-start.5 = (bf16[4,4,2,2,64,128]{5,4,3,2,1,0:T(8,128)(2,1)}, bf16[4,4,2,2,64,128]{5,4,3,2,1,0:T(8,128)(2,1)S(1)}, u32[]{:S(2)}, u32[]{:S(2)}) collective-permute-start(bf16[4,4,2,2,64,128]{5,4,3,2,1,0:T(8,128)(2,1)} %get-tuple-element.48), channel_id=1, source_target_pairs={{0,8},{8,0},{16,24},{24,16},{1,9},{9,1},{17,25},{25,17},{2,10},{10... | collective-permute-start | bytes 3145736 | tf_op jit(solution)/shard_map/ppermute | solution.py:577
  123.5 67.4 %collective-permute-start.6 = (bf16[3,784,128]{2,1,0:T(8,128)(2,1)}, bf16[3,784,128]{2,1,0:T(8,128)(2,1)S(1)}, u32[]{:S(2)}, u32[]{:S(2)}) collective-permute-start(bf16[3,784,128]{2,1,0:T(8,128)(2,1)} %get-tuple-element.49), channel_id=1, source_target_pairs={{0,16},{8,24},{16,0},{24,8},{1,17},{9,25},{17,1},{25,9},{2,18},{10... | collective-permute-start | bytes 1806344 | tf_op jit(solution)/shard_map/ppermute | solution.py:577
  125.3 66.6 %collective-permute-start.7 = (bf16[4,784,128]{2,1,0:T(8,128)(2,1)}, bf16[4,784,128]{2,1,0:T(8,128)(2,1)S(1)}, u32[]{:S(2)}, u32[]{:S(2)}) collective-permute-start(bf16[4,784,128]{2,1,0:T(8,128)(2,1)} %get-tuple-element.50), channel_id=1, source_target_pairs={{0,24},{8,16},{16,8},{24,0},{1,25},{9,17},{17,9},{25,1},{2,26},{10... | collective-permute-start | bytes 2408456 | tf_op jit(solution)/shard_map/ppermute | solution.py:577
  187.8 22.2 %collective-permute-start.8 = (bf16[4,1,2,2,64,128]{5,4,3,2,1,0:T(8,128)(2,1)}, bf16[4,1,2,2,64,128]{5,4,3,2,1,0:T(8,128)(2,1)S(1)}, u32[]{:S(2)}, u32[]{:S(2)}) collective-permute-start(bf16[4,1,2,2,64,128]{5,4,3,2,1,0:T(8,128)(2,1)} %get-tuple-element.51), channel_id=1, source_target_pairs={{0,8},{8,0},{16,24},{24,16},{1,9},{9,1},{17,25},{25,17},{2,10},{10... | collective-permute-start | bytes 786440 | tf_op jit(solution)/shard_map/ppermute | solution.py:577
  189.3 20.7 %collective-permute-start.9 = (bf16[1,784,128]{2,1,0:T(8,128)(2,1)}, bf16[1,784,128]{2,1,0:T(8,128)(2,1)S(1)}, u32[]{:S(2)}, u32[]{:S(2)}) collective-permute-start(bf16[1,784,128]{2,1,0:T(8,128)(2,1)} %get-tuple-element.52), channel_id=1, source_target_pairs={{0,16},{8,24},{16,0},{24,8},{1,17},{9,25},{17,1},{25,9},{2,18},{10... | collective-permute-start | bytes 602120 | tf_op jit(solution)/shard_map/ppermute | solution.py:577
  190.9 19.0 %collective-permute-start.10 = (bf16[1,784,128]{2,1,0:T(8,128)(2,1)}, bf16[1,784,128]{2,1,0:T(8,128)(2,1)S(1)}, u32[]{:S(2)}, u32[]{:S(2)}) collective-permute-start(bf16[1,784,128]{2,1,0:T(8,128)(2,1)} %get-tuple-element.53), channel_id=1, source_target_pairs={{0,24},{8,16},{16,8},{24,0},{1,25},{9,17},{17,9},{25,1},{2,26},{10... | collective-permute-start | bytes 602120 | tf_op jit(solution)/shard_map/ppermute | solution.py:577
  210.0 11.5 %copy-start.10 = (bf16[1,784,128]{2,1,0:T(8,128)(2,1)}, bf16[1,784,128]{2,1,0:T(8,128)(2,1)S(1)}, u32[]{:S(2)}) copy-start(bf16[1,784,128]{2,1,0:T(8,128)(2,1)S(1)} %collective-permute-done.9.refs_2_) | copy-start | bytes 602116
  210.0 11.5 %copy-start.11 = (bf16[1,784,128]{2,1,0:T(8,128)(2,1)}, bf16[1,784,128]{2,1,0:T(8,128)(2,1)S(1)}, u32[]{:S(2)}) copy-start(bf16[1,784,128]{2,1,0:T(8,128)(2,1)S(1)} %collective-permute-done.10.refs_3_) | copy-start | bytes 602116
  210.8 62.3 %all-to-all-start.2 = ((bf16[8,4,4,2,64,128]{5,4,3,2,1,0:T(8,128)(2,1)}), bf16[8,4,4,2,64,128]{5,4,3,2,1,0:T(8,128)(2,1)}, u32[]{:S(2)}, u32[]{:S(2)}) async-start(bf16[8,4,4,2,64,128]{5,4,3,2,1,0:T(8,128)(2,1)} %shard_map.77), calls=%async_computation.2 | async-start | bytes 8388608 | tf_op jit(solution)/shard_map/all_to_all | solution.py:581
  216.7 41.9 %collective-permute-start.12 = (bf16[3,784,128]{2,1,0:T(8,128)(2,1)}, bf16[3,784,128]{2,1,0:T(8,128)(2,1)S(1)}, u32[]{:S(2)}, u32[]{:S(2)}) collective-permute-start(bf16[3,784,128]{2,1,0:T(8,128)(2,1)} %get-tuple-element.57), channel_id=1, source_target_pairs={{0,16},{8,24},{16,0},{24,8},{1,17},{9,25},{17,1},{25,9},{2,18},{10... | collective-permute-start | bytes 1806344 | tf_op jit(solution)/shard_map/ppermute | solution.py:577
  220.0 52.9 %collective-permute-start.13 = (bf16[3,784,128]{2,1,0:T(8,128)(2,1)}, bf16[3,784,128]{2,1,0:T(8,128)(2,1)S(1)}, u32[]{:S(2)}, u32[]{:S(2)}) collective-permute-start(bf16[3,784,128]{2,1,0:T(8,128)(2,1)} %get-tuple-element.58), channel_id=1, source_target_pairs={{0,24},{8,16},{16,8},{24,0},{1,25},{9,17},{17,9},{25,1},{2,26},{10... | collective-permute-start | bytes 1806344 | tf_op jit(solution)/shard_map/ppermute | solution.py:577
  220.5 62.9 %collective-permute-start.11 = (bf16[4,3,2,2,64,128]{5,4,3,2,1,0:T(8,128)(2,1)}, bf16[4,3,2,2,64,128]{5,4,3,2,1,0:T(8,128)(2,1)S(1)}, u32[]{:S(2)}, u32[]{:S(2)}) collective-permute-start(bf16[4,3,2,2,64,128]{5,4,3,2,1,0:T(8,128)(2,1)} %get-tuple-element.56), channel_id=1, source_target_pairs={{0,8},{8,0},{16,24},{24,16},{1,9},{9,1},{17,25},{25,17},{2,10},{10... | collective-permute-start | bytes 2359304 | tf_op jit(solution)/shard_map/ppermute | solution.py:577
  258.6 24.8 %copy-start.2 = (bf16[3,784,128]{2,1,0:T(8,128)(2,1)}, bf16[3,784,128]{2,1,0:T(8,128)(2,1)S(1)}, u32[]{:S(2)}) copy-start(bf16[3,784,128]{2,1,0:T(8,128)(2,1)S(1)} %collective-permute-done.12.refs_6_) | copy-start | bytes 1806340
  272.9 10.5 %copy-start.3 = (bf16[3,784,128]{2,1,0:T(8,128)(2,1)}, bf16[3,784,128]{2,1,0:T(8,128)(2,1)S(1)}, u32[]{:S(2)}) copy-start(bf16[3,784,128]{2,1,0:T(8,128)(2,1)S(1)} %collective-permute-done.13.refs_7_) | copy-start | bytes 1806340
  273.0 10.4 %collective-permute-start.14 = (bf16[2,4,128,128]{3,2,1,0:T(8,128)(2,1)S(1)}, bf16[2,4,128,128]{3,2,1,0:T(8,128)(2,1)S(1)}, u32[]{:S(2)}, u32[]{:S(2)}) collective-permute-start(bf16[2,4,128,128]{3,2,1,0:T(8,128)(2,1)S(1)} %pad_maximum_fusion.2), channel_id=1, source_target_pairs={{0,8},{8,0},{16,24},{24,16},{1,9},{9,1},{17,25},{25,17},{2,10},{10... | collective-permute-start | bytes 786440 | tf_op jit(solution)/shard_map/ppermute | solution.py:577
  275.1 20.4 %collective-permute-start.17 = (bf16[8,1,2,64,128]{4,3,2,0,1:T(8,128)(2,1)S(1)}, bf16[8,1,2,64,128]{4,3,2,0,1:T(8,128)(2,1)S(1)}, u32[]{:S(2)}, u32[]{:S(2)}) collective-permute-start(bf16[8,1,2,64,128]{4,3,2,0,1:T(8,128)(2,1)S(1)} %get-tuple-element.64), channel_id=1, source_target_pairs={{0,24},{8,16},{16,8},{24,0},{1,25},{9,17},{17,9},{25,1},{2,26},{10... | collective-permute-start | bytes 786440 | tf_op jit(solution)/shard_map/ppermute | solution.py:577
  276.0 22.6 %collective-permute-start.16 = (bf16[8,1,2,64,128]{4,3,2,0,1:T(8,128)(2,1)S(1)}, bf16[8,1,2,64,128]{4,3,2,0,1:T(8,128)(2,1)S(1)}, u32[]{:S(2)}, u32[]{:S(2)}) collective-permute-start(bf16[8,1,2,64,128]{4,3,2,0,1:T(8,128)(2,1)S(1)} %get-tuple-element.65), channel_id=1, source_target_pairs={{0,16},{8,24},{16,0},{24,8},{1,17},{9,25},{17,1},{25,9},{2,18},{10... | collective-permute-start | bytes 786440 | tf_op jit(solution)/shard_map/ppermute | solution.py:577
  279.4 19.3 %collective-permute-start.15 = (bf16[8,1,2,64,128]{4,3,2,0,1:T(8,128)(2,1)S(1)}, bf16[8,1,2,64,128]{4,3,2,0,1:T(8,128)(2,1)S(1)}, u32[]{:S(2)}, u32[]{:S(2)}) collective-permute-start(bf16[8,1,2,64,128]{4,3,2,0,1:T(8,128)(2,1)S(1)} %get-tuple-element.66), channel_id=1, source_target_pairs={{0,8},{8,0},{16,24},{24,16},{1,9},{9,1},{17,25},{25,17},{2,10},{10... | collective-permute-start | bytes 786440 | tf_op jit(solution)/shard_map/ppermute | solution.py:577
  299.5 77.7 %all-to-all-start.3 = ((bf16[8,4,4,2,64,128]{5,4,3,2,1,0:T(8,128)(2,1)}), bf16[8,4,4,2,64,128]{5,4,3,2,1,0:T(8,128)(2,1)}, u32[]{:S(2)}, u32[]{:S(2)}) async-start(bf16[8,4,4,2,64,128]{5,4,3,2,1,0:T(8,128)(2,1)} %shard_map.79), calls=%async_computation.3 | async-start | bytes 8388608 | tf_op jit(solution)/shard_map/all_to_all | solution.py:581
  304.3 36.5 %collective-permute-start.18 = (bf16[8,3,2,64,128]{4,3,2,1,0:T(8,128)(2,1)}, bf16[8,3,2,64,128]{4,3,2,1,0:T(8,128)(2,1)S(1)}, u32[]{:S(2)}, u32[]{:S(2)}) collective-permute-start(bf16[8,3,2,64,128]{4,3,2,1,0:T(8,128)(2,1)} %get-tuple-element.60), channel_id=1, source_target_pairs={{0,8},{8,0},{16,24},{24,16},{1,9},{9,1},{17,25},{25,17},{2,10},{10... | collective-permute-start | bytes 2359304 | tf_op jit(solution)/shard_map/ppermute | solution.py:577
  307.3 52.3 %collective-permute-start.19 = (bf16[8,3,2,64,128]{4,3,2,1,0:T(8,128)(2,1)}, bf16[8,3,2,64,128]{4,3,2,1,0:T(8,128)(2,1)S(1)}, u32[]{:S(2)}, u32[]{:S(2)}) collective-permute-start(bf16[8,3,2,64,128]{4,3,2,1,0:T(8,128)(2,1)} %get-tuple-element.61), channel_id=1, source_target_pairs={{0,16},{8,24},{16,0},{24,8},{1,17},{9,25},{17,1},{25,9},{2,18},{10... | collective-permute-start | bytes 2359304 | tf_op jit(solution)/shard_map/ppermute | solution.py:577
  307.7 69.5 %collective-permute-start.20 = (bf16[8,3,2,64,128]{4,3,2,1,0:T(8,128)(2,1)}, bf16[8,3,2,64,128]{4,3,2,1,0:T(8,128)(2,1)S(1)}, u32[]{:S(2)}, u32[]{:S(2)}) collective-permute-start(bf16[8,3,2,64,128]{4,3,2,1,0:T(8,128)(2,1)} %get-tuple-element.62), channel_id=1, source_target_pairs={{0,24},{8,16},{16,8},{24,0},{1,25},{9,17},{17,9},{25,1},{2,26},{10... | collective-permute-start | bytes 2359304 | tf_op jit(solution)/shard_map/ppermute | solution.py:577
  340.8 36.4 %copy-start.5 = (bf16[8,3,2,64,128]{4,3,2,1,0:T(8,128)(2,1)}, bf16[8,3,2,64,128]{4,3,2,1,0:T(8,128)(2,1)S(1)}, u32[]{:S(2)}) copy-start(bf16[8,3,2,64,128]{4,3,2,1,0:T(8,128)(2,1)S(1)} %collective-permute-done.18) | copy-start | bytes 2359300
  359.6 17.5 %copy-start.6 = (bf16[8,3,2,64,128]{4,3,2,1,0:T(8,128)(2,1)}, bf16[8,3,2,64,128]{4,3,2,1,0:T(8,128)(2,1)S(1)}, u32[]{:S(2)}) copy-start(bf16[8,3,2,64,128]{4,3,2,1,0:T(8,128)(2,1)S(1)} %collective-permute-done.19) | copy-start | bytes 2359300
  (12 other events, 20.6 us)
